TPU v7x, 32 devices: a whole 2x2x4 slice. The times are simulated.
32 devices in a mesh: cube: 8 (over z, y), front: 4 (over x, core).
Axes of the slice: x: 2, y: 2, z: 4, core: 2. Of those that a mesh axis runs over, the one named last changes fastest.
Arguments:
- kkt_blocks: float32 [4, 2048, 128], P('front', 'cube'), may hold values from -1.5 to 1.5
- kkt_owner: int32 [4, 2048, 1], P('front', 'cube'), may hold values from 0 to 7; in each aligned block of 256 rows (0 to 255, 256 to 511, ..., all dimensions but the last counted through in order) at most 64 rows name the same one
- kkt_target: int32 [4, 2048], P('front', 'cube'), may hold values from 0 to 255
- leaf_pivot: float32 [16, 512, 128], P('cube', 'front'), may hold values from -3.5 to 3.5
- pivot_signs: int32 [16, 512], P('cube', 'front'), may hold values from -1 to 1, as said below
- perturb: float32 [16, 512], P('cube', 'front'), may hold values from 0.25 to 1
- leaf_coupling: float32 [16, 512, 128], P('cube', 'front'), may hold values from -1.5 to 1.5
- leaf_map: int32 [16, 512], P('cube', 'front'), may hold values from 256 to 2047
- mid_front: bfloat16 [8192, 2048], P('cube', 'front'), may hold values from -3.5 to 3.5
- level_map: int32 [4, 2048], replicated, may hold values from 256 to 2047, as said below
- top_front: bfloat16 [4096, 2048], P('cube', 'front'), may hold values from -3.5 to 3.5
Outputs:
- leaf_factor: float32 [16, 512, 128], P('cube', 'front')
- mid_factor: float32 [8192, 256], P(('cube', 'front'))
- upper_schur: float32 [4096, 2048], P('cube', 'front')
Inputs may be any that keep to these rules, and one draw needn't show every extreme that they name: `kkt_owner`: the rows of one device name one cube index at most 64 times, and some cube index exactly 64 times. `pivot_signs`: every entry is -1 or 1. `level_map`: position p of a level-1 front goes to a position of the same quarter floor(p / 512) of the level-2 front, never below 256.
All inputs are finite; a program needn't handle non-finite values.
Results may differ from a plain program's by a relative error of at most 0.0003.
Values sent between devices are 32-bit elements; how exact they have to be, the bound alone decides.
No kernel may reach another device: no remote copies, remote signals or barrier semaphores. Data moves between devices by JAX's collectives and lax.ppermute only.
A program may use at most 64 MiB of HBM per device.

v0:
```python
import jax
import jax.numpy as jnp
from jax import lax
from jax.sharding import PartitionSpec as P

NU = 2048
PIV = 128
PANELS = 2
NS_STEPS = 2


HIGHEST = lax.Precision.HIGHEST


def partner(array, axis, stride):
    return lax.ppermute(array, axis, [(i, i ^ 1 << stride) for i in range(lax.axis_size(axis))])


def from_root(array, axis, root):
    mine = lax.axis_index(axis) == root
    return lax.psum(jnp.where(mine, array, jnp.zeros_like(array)), axis)


def newton_inverse(pivot_block):
    diagonal = jnp.diagonal(pivot_block, axis1=-2, axis2=-1)
    current = jnp.eye(pivot_block.shape[-1], dtype=jnp.float32) * (1.0 / diagonal)[..., None, :]
    for sweep_index in range(NS_STEPS):
        product = jnp.einsum("...ij,...jk->...ik", pivot_block, current, precision=HIGHEST)
        current = 2.0 * current - jnp.einsum(
            "...ij,...jk->...ik", current, product, precision=HIGHEST
        )
    return current


def apply_panel(front_block, own_cols, pivot_rows, col_rows, row_positions, col_positions, finish):
    inverse = newton_inverse(pivot_rows)
    keep_rows = (row_positions >= finish).astype(jnp.float32)[:, None]
    keep_cols = (col_positions >= finish).astype(jnp.float32)[:, None]
    lower_rows = jnp.dot(own_cols, inverse, precision=HIGHEST) * keep_rows
    return (
        front_block - jnp.dot(lower_rows, (col_rows * keep_cols).T, precision=HIGHEST),
        lower_rows,
    )


def local(
    kkt_blocks,
    kkt_owner,
    kkt_target,
    leaf_pivot,
    pivot_signs,
    perturb,
    leaf_coupling,
    leaf_map,
    mid_front,
    level_map,
    top_front,
):
    cube_count = lax.axis_size("cube")
    front_count = lax.axis_size("front")
    cube_pos = lax.axis_index("cube")
    front_pos = lax.axis_index("front")
    low_bit = cube_pos % 2
    high_bit = cube_pos // 2 % 2
    blocks = kkt_blocks[0]
    block_count = blocks.shape[0]
    block_width = blocks.shape[1]
    capacity = max(2, 2 * block_count // cube_count)
    destination = kkt_owner[0, :, 0]
    onehot = (destination[:, None] == jnp.arange(cube_count, dtype=jnp.int32)[None, :]).astype(
        jnp.int32
    )
    slot_rank = jnp.sum((jnp.cumsum(onehot, axis=0) - 1) * onehot, axis=1)
    send_slot = destination * capacity + slot_rank
    send_values = (
        jnp.zeros((cube_count * capacity, block_width), jnp.float32).at[send_slot].set(blocks)
    )
    send_rows = (
        jnp.full((cube_count * capacity,), -1.0, jnp.float32)
        .at[send_slot]
        .set(kkt_target[0].astype(jnp.float32))
    )
    got_values, got_rows = (
        lax.all_to_all(
            send_values.reshape(cube_count, capacity, block_width),
            "cube",
            split_axis=0,
            concat_axis=0,
            tiled=True,
        ),
        lax.all_to_all(
            send_rows.reshape(cube_count, capacity), "cube", split_axis=0, concat_axis=0, tiled=True
        ),
    )
    leaf_count = leaf_pivot.shape[0]
    pivot_size = leaf_pivot.shape[2]
    row_count = leaf_coupling.shape[1]
    identity = jnp.eye(pivot_size, dtype=jnp.float32)
    pivots = leaf_pivot + identity * (pivot_signs.astype(jnp.float32) * perturb)[:, None, :]
    inverse = newton_inverse(pivots)
    leaf_rows = leaf_count * row_count
    targets = got_rows.reshape(-1).astype(jnp.int32)
    targets = jnp.where(targets < 0, leaf_rows, targets)
    arrivals = jax.ops.segment_sum(
        got_values.reshape(-1, block_width), targets, num_segments=leaf_rows + 1
    )[:leaf_rows]
    coupling = leaf_coupling + arrivals.reshape(leaf_count, row_count, block_width)
    factor = jnp.einsum("lrk,lkj->lrj", coupling, inverse, precision=HIGHEST)
    contrib = -jnp.einsum("lrk,lsk->lrs", factor, coupling, precision=HIGHEST)
    shared_terms, shared_maps = (
        lax.all_gather(contrib, "front", axis=0, tiled=True),
        lax.all_gather(leaf_map.astype(jnp.float32), "front", axis=0, tiled=True),
    )
    partner_terms, partner_maps = partner((shared_terms, shared_maps), "cube", 0)
    child_terms = jnp.concatenate([shared_terms, partner_terms], axis=0)
    child_maps = jnp.concatenate([shared_maps, partner_maps], axis=0).astype(jnp.int32)
    half_rows = NU // 2
    quarter = NU // 4
    child_count = child_terms.shape[0]
    child_rows = child_terms.shape[1]
    row_local = child_maps - low_bit * half_rows
    col_local = child_maps - front_pos * quarter
    row_valid = (row_local >= 0) & (row_local < half_rows)
    col_valid = (col_local >= 0) & (col_local < quarter)
    block_ids = jnp.arange(child_count, dtype=jnp.int32)[:, None]
    col_ids = jnp.where(col_valid, block_ids * quarter + col_local, child_count * quarter)
    by_cols = jax.ops.segment_sum(
        jnp.swapaxes(child_terms, 1, 2).reshape(-1, child_rows),
        col_ids.reshape(-1),
        num_segments=child_count * quarter + 1,
    )[:-1]
    by_cols = jnp.swapaxes(by_cols.reshape(child_count, quarter, child_rows), 1, 2).reshape(
        -1, quarter
    )
    row_ids = jnp.where(row_valid, row_local, half_rows)
    assembled = jax.ops.segment_sum(by_cols, row_ids.reshape(-1), num_segments=half_rows + 1)[:-1]
    mid_block = mid_front.astype(jnp.float32) + assembled
    mid_positions = low_bit * half_rows + jnp.arange(half_rows)
    col_positions = front_pos * quarter + jnp.arange(quarter)
    factors = []
    for panel_index in range(PANELS):
        first_col = panel_index * PIV
        finish = first_col + PIV
        own_cols = from_root(mid_block[:, first_col:finish], "front", 0)
        other_cols = partner(own_cols, "cube", 0)
        whole_cols = jnp.where(
            low_bit == 0,
            jnp.concatenate([own_cols, other_cols], axis=0),
            jnp.concatenate([other_cols, own_cols], axis=0),
        )
        pivot_rows = whole_cols[first_col:finish]
        col_rows = lax.dynamic_slice_in_dim(whole_cols, front_pos * quarter, quarter, 0)
        mid_block, lower_rows = apply_panel(
            mid_block, own_cols, pivot_rows, col_rows, mid_positions, col_positions, finish
        )
        factors.append(lower_rows)
    factor_rows = jnp.concatenate(factors, axis=1)
    slab_rows = half_rows // front_count
    mid_factor = lax.dynamic_slice_in_dim(factor_rows, front_pos * slab_rows, slab_rows, 0)
    group_one = cube_pos // 2
    other_group = group_one + 1 - 2 * high_bit
    own_map = lax.dynamic_index_in_dim(level_map, group_one, 0, keepdims=False)
    other_map = lax.dynamic_index_in_dim(level_map, other_group, 0, keepdims=False)
    own_piece = lax.dynamic_slice_in_dim(mid_block, high_bit * quarter, quarter, 0)
    received = partner(mid_block, "cube", 1)
    other_piece = lax.dynamic_slice_in_dim(received, high_bit * quarter, quarter, 0)
    row_quarter = 2 * low_bit + high_bit
    top_positions = row_quarter * quarter + jnp.arange(quarter)

    def spread_cols(piece, mapping):
        col_target = jnp.take(mapping, col_positions) - front_pos * quarter
        col_ids = jnp.where(col_positions >= PANELS * PIV, col_target, quarter)
        return jax.ops.segment_sum(piece.T, col_ids, num_segments=quarter + 1)[:-1].T

    def row_ids_of(mapping):
        row_target = jnp.take(mapping, top_positions) - row_quarter * quarter
        return jnp.where(top_positions >= PANELS * PIV, row_target, quarter)

    top_rows = jnp.concatenate(
        [spread_cols(own_piece, own_map), spread_cols(other_piece, other_map)], axis=0
    )
    top_ids = jnp.concatenate([row_ids_of(own_map), row_ids_of(other_map)])
    top_added = jax.ops.segment_sum(top_rows, top_ids, num_segments=quarter + 1)[:-1]
    top_block = top_front.astype(jnp.float32) + top_added
    for panel_index in range(PANELS):
        first_col = panel_index * PIV
        finish = first_col + PIV
        own_cols = from_root(top_block[:, first_col:finish], "front", 0)
        first_swap = partner(own_cols, "cube", 0)
        by_low = jnp.where(
            low_bit == 0, jnp.stack([own_cols, first_swap]), jnp.stack([first_swap, own_cols])
        )
        second_swap = partner(by_low, "cube", 1)
        by_both = jnp.where(
            high_bit == 0,
            jnp.stack([by_low, second_swap], axis=1),
            jnp.stack([second_swap, by_low], axis=1),
        )
        whole_cols = by_both.reshape(NU, PIV)
        pivot_rows = whole_cols[first_col:finish]
        col_rows = lax.dynamic_slice_in_dim(whole_cols, front_pos * quarter, quarter, 0)
        top_block, unused = apply_panel(
            top_block, own_cols, pivot_rows, col_rows, top_positions, col_positions, finish
        )
    return (factor, mid_factor, top_block)


def solution(mesh):
    in_specs = (
        P("front", "cube", None),
        P("front", "cube", None),
        P("front", "cube"),
        P("cube", "front", None),
        P("cube", "front"),
        P("cube", "front"),
        P("cube", "front", None),
        P("cube", "front"),
        P("cube", "front"),
        P(),
        P("cube", "front"),
    )
    out_specs = (P("cube", "front", None), P(("cube", "front"), None), P("cube", "front"))
    return jax.shard_map(local, mesh=mesh, in_specs=in_specs, out_specs=out_specs, check_vma=False)
```

profile of v0, /device:TPU:0, one launch (start us, length us, event | category | flops | bytes accessed | tf_op | source)
XLA Modules:
  0.0 424.6 jit_solution(14030384231092047827)
XLA Ops:
  7.9 6.0 %all-gather = f32[4,2,128]{2,1,0:T(2,128)S(1)} all-gather(f32[1,2,128]{2,1,0:T(2,128)S(1)} %convert_bitcast_fusion), channel_id=1, replica_groups=mesh['cube'=8,'front'=4] {'front'}, dimensions={0}, use_global_device_ids=true | all-gather | bytes 5120 | tf_op jit(solution)/shard_map/all_gather | solution.py:112
  13.9 2.1 collective-permute-start
  21.6 4.9 %all-to-all-start = ((f32[8,1,64]{2,1,0:T(1,128)}), f32[8,1,64]{2,1,0:T(1,128)S(1)}, u32[]{:S(2)}, u32[]{:S(2)}) async-start(f32[8,1,64]{2,1,0:T(1,128)} %all_to_all.9), calls=%async_computation | async-start | bytes 8192 | tf_op jit(solution)/shard_map/all_to_all | solution.py:91
  28.2 4.6 %copy.38 = f32[2,128,128]{0,2,1:T(8,128)} copy(f32[2,128,128]{2,1,0:T(8,128)S(1)} %multiply_add_fusion) | data formatting | bytes 262144 | tf_op jit(solution)/shard_map/add | solution.py:99
  32.8 1.8 gather_fusion
  35.6 1.8 scatter_custom_fusion.1
  37.4 6.0 %all-to-all-start.1 = ((f32[8,64,128]{2,1,0:T(8,128)}), f32[8,64,128]{2,1,0:T(8,128)S(1)}, u32[]{:S(2)}, u32[]{:S(2)}) async-start(f32[8,64,128]{2,1,0:T(8,128)} %bitcast.10), calls=%async_computation.1 | async-start | bytes 524288 | tf_op jit(solution)/shard_map/all_to_all | solution.py:84
  43.8 8.1 %all-to-all-done.1 = f32[8,64,128]{2,1,0:T(8,128)S(1)} async-done(((f32[8,64,128]{2,1,0:T(8,128)}), f32[8,64,128]{2,1,0:T(8,128)S(1)}, u32[]{:S(2)}, u32[]{:S(2)}) %all-to-all-start.1) | async-done | bytes 262176 | tf_op jit(solution)/shard_map/all_to_all | solution.py:84
  51.9 3.4 scatter_custom_fusion.2
  56.1 7.2 %all_gather.7 = f32[8,128,128]{2,1,0:T(8,128)S(1)} all-gather(f32[2,128,128]{2,1,0:T(8,128)S(1)} %convolution_negate_fusion), channel_id=1, replica_groups=mesh['cube'=8,'front'=4] {'front'}, dimensions={0}, use_global_device_ids=true | all-gather | bytes 655360 | tf_op jit(solution)/shard_map/all_gather | solution.py:111
  64.2 13.5 %collective-permute-done.1 = f32[8,128,128]{1,2,0:T(8,128)S(1)} collective-permute-done((f32[8,128,128]{1,2,0:T(8,128)S(1)}, f32[8,128,128]{1,2,0:T(8,128)S(1)}, u32[]{:S(2)}, u32[]{:S(2)}) %collective-permute-start.1) | collective-permute-done | bytes 524320 | tf_op jit(solution)/shard_map/ppermute | solution.py:16
  77.8 15.3 %scatter_custom_fusion.3 = f32[8193,128]{1,0:T(8,128)} fusion(s32[2048]{0:T(1024)S(1)} %get-tuple-element.15, f32[2048,128]{1,0:T(8,128)S(1)} %bitcast.126, f32[]{:T(128)} %constant.62.clone.1), kind=kCustom, calls=%fused_computation.17 | custom fusion | flops 262144 | bytes 4194820 | tf_op jit(solution)/shard_map/scatter-add | solution.py:127
  93.1 4.4 %slice.84 = f32[8192,128]{1,0:T(8,128)} slice(f32[8193,128]{1,0:T(8,128)} %scatter_custom_fusion.3), slice={[0:8192], [0:128]} | slice | bytes 8388608 | tf_op jit(solution)/shard_map/slice | solution.py:127
  97.5 5.3 %copy.42 = f32[16,128,512]{2,1,0:T(8,128)} copy(f32[16,128,512]{1,2,0:T(8,128)} %bitcast.110) | data formatting | bytes 8388608 | tf_op jit(solution)/shard_map/transpose | solution.py:132
  102.8 13.8 %scatter_custom_fusion.4 = f32[1025,512]{1,0:T(8,128)S(1)} fusion(s32[2048]{0:T(1024)S(1)} %bitcast.139, f32[2048,512]{1,0:T(8,128)} %bitcast.111, f32[]{:T(128)} %constant.62.clone.1), kind=kCustom, calls=%fused_computation.43 | custom fusion | flops 1048576 | bytes 2099712 | tf_op jit(solution)/shard_map/scatter-add | solution.py:136
  119.3 31.7 %all-reduce.5.cloned.1.call-done = f32[1024,128]{1,0:T(8,128)} async-done(((f32[1024,128]{1,0:T(8,128)}), f32[1024,128]{1,0:T(8,128)}) %all-reduce.5.cloned.1.call-update) | async-done | bytes 524304 | tf_op jit(solution)/shard_map/psum | solution.py:21
  151.0 1.5 collective-permute-start.2
  152.5 11.3 %collective-permute-done.2 = f32[1024,128]{1,0:T(8,128)S(1)} collective-permute-done((f32[1024,128]{1,0:T(8,128)}, f32[1024,128]{1,0:T(8,128)S(1)}, u32[]{:S(2)}, u32[]{:S(2)}) %collective-permute-start.2) | collective-permute-done | bytes 524320 | tf_op jit(solution)/shard_map/ppermute | solution.py:16
  167.9 3.7 convolution_subtract_fusion.1
  172.7 33.3 %all-reduce.7.cloned.1.call-done = f32[1024,128]{1,0:T(8,128)} async-done(((f32[1024,128]{1,0:T(8,128)}), f32[1024,128]{1,0:T(8,128)}) %all-reduce.7.cloned.1.call-update) | async-done | bytes 524304 | tf_op jit(solution)/shard_map/psum | solution.py:21
  206.0 1.5 collective-permute-start.3
  207.5 11.2 %collective-permute-done.3 = f32[1024,128]{1,0:T(8,128)S(1)} collective-permute-done((f32[1024,128]{1,0:T(8,128)}, f32[1024,128]{1,0:T(8,128)S(1)}, u32[]{:S(2)}, u32[]{:S(2)}) %collective-permute-start.3) | collective-permute-done | bytes 524320 | tf_op jit(solution)/shard_map/ppermute | solution.py:16
  224.7 1.7 convolution_multiply_fusion
  226.4 4.3 %convolution_subtract_fusion = f32[1024,512]{1,0:T(8,128)} fusion(f32[1024,512]{1,0:T(8,128)S(1)} %convolution_subtract_fusion.1, f32[1024,128]{0,1:T(8,128)S(1)} %convolution_multiply_fusion, f32[2048,128]{1,0:T(8,128)} %copy-done.7, s32[]{:T(128)S(6)} %select_n.210, f32[512]{0:T(512)S(1)} %fusion.90), kind=kOutput, calls=%fused_computation.24 | convolution fusion | flops 805896192 | bytes 4982788 | tf_op jit(solution)/shard_map/dot_general | solution.py:41
  230.7 1.8 collective-permute-start.4
  232.5 3.1 gather_fusion.7
  235.6 3.1 gather_fusion.8
  238.8 3.1 gather_fusion.6
  242.0 3.1 gather_fusion.5
  247.8 5.0 %scatter_custom_fusion.5 = f32[513,512]{1,0:T(8,128)S(1)} fusion(s32[512]{0:T(512)S(1)} %get-tuple-element.18, f32[512,512]{1,0:T(8,128)} %copy.43, f32[]{:T(128)} %constant.62.clone.1), kind=kCustom, calls=%fused_computation.58 | custom fusion | flops 262144 | bytes 1051136 | tf_op jit(solution)/shard_map/scatter-add | solution.py:173
  253.8 2.5 copy.52
  256.3 20.2 %collective-permute-done.4 = f32[1024,512]{1,0:T(8,128)} collective-permute-done((f32[1024,512]{1,0:T(8,128)}, f32[1024,512]{1,0:T(8,128)}, u32[]{:S(2)}, u32[]{:S(2)}) %collective-permute-start.4) | collective-permute-done | bytes 2097184 | tf_op jit(solution)/shard_map/ppermute | solution.py:16
  279.1 4.7 %scatter_custom_fusion.6 = f32[513,512]{1,0:T(8,128)S(1)} fusion(s32[512]{0:T(512)S(1)} %get-tuple-element.17, f32[512,512]{1,0:T(8,128)} %copy.45, f32[]{:T(128)} %constant.62.clone.1), kind=kCustom, calls=%fused_computation.56 | custom fusion | flops 262144 | bytes 1051136 | tf_op jit(solution)/shard_map/scatter-add | solution.py:173
  284.9 1.6 copy.53
  286.6 8.4 %scatter_custom_fusion.7 = f32[513,512]{1,0:T(8,128)} fusion(s32[1024]{0:T(1024)S(1)} %pad_add_fusion, f32[512,512]{1,0:T(8,128)S(1)} %bitcast.113, f32[]{:T(128)} %constant.198, f32[512,512]{1,0:T(8,128)S(1)} %bitcast.112, f32[]{:T(128)} %constant.62.clone.1), kind=kCustom, calls=%fused_computation.20 | custom fusion | flops 1048576 | bytes 3147784 | tf_op jit(solution)/shard_map/scatter-add | solution.py:183
  295.0 1.5 slice_add_fusion.1
  297.6 31.6 %all-reduce.9.cloned.1.call-done = f32[512,128]{1,0:T(8,128)} async-done(((f32[512,128]{1,0:T(8,128)}), f32[512,128]{1,0:T(8,128)}) %all-reduce.9.cloned.1.call-update) | async-done | bytes 262160 | tf_op jit(solution)/shard_map/psum | solution.py:21
  330.7 5.4 %collective-permute-done.5 = f32[512,128]{1,0:T(8,128)S(1)} collective-permute-done((f32[512,128]{1,0:T(8,128)}, f32[512,128]{1,0:T(8,128)S(1)}, u32[]{:S(2)}, u32[]{:S(2)}) %collective-permute-start.5) | collective-permute-done | bytes 262176 | tf_op jit(solution)/shard_map/ppermute | solution.py:16
  336.0 1.9 maximum_select_fusion.4
  337.9 1.8 collective-permute-start.6
  340.8 9.0 %collective-permute-done.6 = f32[2,512,128]{2,1,0:T(8,128)S(1)} collective-permute-done((f32[2,512,128]{2,1,0:T(8,128)}, f32[2,512,128]{2,1,0:T(8,128)S(1)}, u32[]{:S(2)}, u32[]{:S(2)}) %collective-permute-start.6) | collective-permute-done | bytes 524320 | tf_op jit(solution)/shard_map/ppermute | solution.py:16
  355.1 2.0 convolution_subtract_fusion.3
  357.9 33.1 %all-reduce.11.cloned.1.call-done = f32[512,128]{1,0:T(8,128)} async-done(((f32[512,128]{1,0:T(8,128)}), f32[512,128]{1,0:T(8,128)}) %all-reduce.11.cloned.1.call-update) | async-done | bytes 262160 | tf_op jit(solution)/shard_map/psum | solution.py:21
  392.5 5.5 %collective-permute-done.7 = f32[512,128]{1,0:T(8,128)S(1)} collective-permute-done((f32[512,128]{1,0:T(8,128)}, f32[512,128]{1,0:T(8,128)S(1)}, u32[]{:S(2)}, u32[]{:S(2)}) %collective-permute-start.7) | collective-permute-done | bytes 262176 | tf_op jit(solution)/shard_map/ppermute | solution.py:16
  398.0 1.9 maximum_select_fusion.6
  399.9 1.7 collective-permute-start.8
  402.4 9.3 %collective-permute-done.8 = f32[2,512,128]{2,1,0:T(8,128)} collective-permute-done((f32[2,512,128]{2,1,0:T(8,128)}, f32[2,512,128]{2,1,0:T(8,128)}, u32[]{:S(2)}, u32[]{:S(2)}) %collective-permute-start.8) | collective-permute-done | bytes 524320 | tf_op jit(solution)/shard_map/ppermute | solution.py:16
  415.7 2.1 convolution_subtract_fusion.2
  (140 shorter events, 48.1 us)
Async XLA Ops:
  7.2 28.4 %copy-start = (f32[1,256,128]{2,1,0:T(8,128)S(1)}, f32[1,256,128]{2,1,0:T(8,128)}, u32[]{:S(2)}) copy-start(f32[1,256,128]{2,1,0:T(8,128)} %param.13) | copy-start | bytes 393220
  13.9 50.3 %collective-permute-start = (f32[8,128]{1,0:T(8,128)S(1)}, f32[8,128]{1,0:T(8,128)S(1)}, u32[]{:S(2)}, u32[]{:S(2)}) collective-permute-start(f32[8,128]{1,0:T(8,128)S(1)} %bitcast.135), channel_id=1, source_target_pairs={{0,4},{4,0},{8,12},{12,8},{16,20},{20,16},{24,28},{28,24},{1,5},{5... | collective-permute-start | bytes 12296 | tf_op jit(solution)/shard_map/ppermute | solution.py:16
  21.6 15.7 %all-to-all-start = ((f32[8,1,64]{2,1,0:T(1,128)}), f32[8,1,64]{2,1,0:T(1,128)S(1)}, u32[]{:S(2)}, u32[]{:S(2)}) async-start(f32[8,1,64]{2,1,0:T(1,128)} %all_to_all.9), calls=%async_computation | async-start | bytes 8192 | tf_op jit(solution)/shard_map/all_to_all | solution.py:91
  32.8 22.6 %copy-start.12 = (f32[2,128,128]{2,1,0:T(8,128)S(1)}, f32[2,128,128]{2,1,0:T(8,128)}, u32[]{:S(2)}) copy-start(f32[2,128,128]{2,1,0:T(8,128)} %param.19) | copy-start | bytes 393220
  37.4 14.6 %all-to-all-start.1 = ((f32[8,64,128]{2,1,0:T(8,128)}), f32[8,64,128]{2,1,0:T(8,128)S(1)}, u32[]{:S(2)}, u32[]{:S(2)}) async-start(f32[8,64,128]{2,1,0:T(8,128)} %bitcast.10), calls=%async_computation.1 | async-start | bytes 524288 | tf_op jit(solution)/shard_map/all_to_all | solution.py:84
  43.4 107.6 %all-reduce.5.cloned.1.call-start = ((), (), s32[]{:S(2)}) async-start(), calls=%async_computation.2 | async-start | bytes 1048576 | tf_op jit(solution)/shard_map/psum | solution.py:21
  55.7 22.1 %copy-start.11 = (f32[2,128,128]{2,1,0:T(8,128)}, f32[2,128,128]{2,1,0:T(8,128)S(1)}, u32[]{:S(2)}) copy-start(f32[2,128,128]{2,1,0:T(8,128)S(1)} %fusion.114) | copy-start | bytes 393220
  63.4 14.2 %collective-permute-start.1 = (f32[8,128,128]{1,2,0:T(8,128)S(1)}, f32[8,128,128]{1,2,0:T(8,128)S(1)}, u32[]{:S(2)}, u32[]{:S(2)}) collective-permute-start(f32[8,128,128]{1,2,0:T(8,128)S(1)} %copy.41), channel_id=1, source_target_pairs={{0,4},{4,0},{8,12},{12,8},{16,20},{20,16},{24,28},{28,24},{1,5},{5... | collective-permute-start | bytes 1572872 | tf_op jit(solution)/shard_map/ppermute | solution.py:16
  102.8 13.8 %copy-start.10 = (bf16[1024,512]{1,0:T(8,128)(2,1)S(1)}, bf16[1024,512]{1,0:T(8,128)(2,1)}, u32[]{:S(2)}) copy-start(bf16[1024,512]{1,0:T(8,128)(2,1)} %param.21) | copy-start | bytes 3145732
  117.0 1.4 copy-start.2
  119.2 86.7 %all-reduce.7.cloned.1.call-start = ((), (), s32[]{:S(2)}) async-start(), calls=%async_computation.3 | async-start | bytes 1048576 | tf_op jit(solution)/shard_map/psum | solution.py:21
  151.0 16.2 %copy-start.9 = (f32[1024,128]{1,0:T(8,128)S(1)}, f32[1024,128]{1,0:T(8,128)}, u32[]{:S(2)}) copy-start(f32[1024,128]{1,0:T(8,128)} %all-reduce.5.cloned.1.call-done) | copy-start | bytes 1572868
  151.0 12.7 %collective-permute-start.2 = (f32[1024,128]{1,0:T(8,128)}, f32[1024,128]{1,0:T(8,128)S(1)}, u32[]{:S(2)}, u32[]{:S(2)}) collective-permute-start(f32[1024,128]{1,0:T(8,128)} %all-reduce.5.cloned.1.call-done), channel_id=1, source_target_pairs={{0,4},{4,0},{8,12},{12,8},{16,20},{20,16},{24,28},{28,24},{1,5},{5... | collective-permute-start | bytes 1572872 | tf_op jit(solution)/shard_map/ppermute | solution.py:16
  165.1 2.1 copy-start.6
  172.4 156.7 %all-reduce.9.cloned.1.call-start = ((), (), s32[]{:S(2)}) async-start(), calls=%async_computation.4 | async-start | bytes 524288 | tf_op jit(solution)/shard_map/psum | solution.py:21
  206.0 12.7 %collective-permute-start.3 = (f32[1024,128]{1,0:T(8,128)}, f32[1024,128]{1,0:T(8,128)S(1)}, u32[]{:S(2)}, u32[]{:S(2)}) collective-permute-start(f32[1024,128]{1,0:T(8,128)} %all-reduce.7.cloned.1.call-done), channel_id=1, source_target_pairs={{0,4},{4,0},{8,12},{12,8},{16,20},{20,16},{24,28},{28,24},{1,5},{5... | collective-permute-start | bytes 1572872 | tf_op jit(solution)/shard_map/ppermute | solution.py:16
  220.0 1.0 copy-start.7
  226.4 6.1 %copy-start.13 = (s32[4,2048]{1,0:T(4,128)S(1)}, s32[4,2048]{1,0:T(4,128)}, u32[]{:S(2)}) copy-start(s32[4,2048]{1,0:T(4,128)} %param.22) | copy-start | bytes 98308
  230.7 45.8 %collective-permute-start.4 = (f32[1024,512]{1,0:T(8,128)}, f32[1024,512]{1,0:T(8,128)}, u32[]{:S(2)}, u32[]{:S(2)}) collective-permute-start(f32[1024,512]{1,0:T(8,128)} %convolution_subtract_fusion), channel_id=1, source_target_pairs={{0,8},{4,12},{8,0},{12,4},{16,24},{20,28},{24,16},{28,20},{1,9},{5... | collective-permute-start | bytes 6291464 | tf_op jit(solution)/shard_map/ppermute | solution.py:16
  284.9 1.7 copy-start.3
  297.3 93.7 %all-reduce.11.cloned.1.call-start = ((), (), s32[]{:S(2)}) async-start(), calls=%async_computation.5 | async-start | bytes 524288 | tf_op jit(solution)/shard_map/psum | solution.py:21
  329.2 6.9 %collective-permute-start.5 = (f32[512,128]{1,0:T(8,128)}, f32[512,128]{1,0:T(8,128)S(1)}, u32[]{:S(2)}, u32[]{:S(2)}) collective-permute-start(f32[512,128]{1,0:T(8,128)} %all-reduce.9.cloned.1.call-done), channel_id=1, source_target_pairs={{0,4},{4,0},{8,12},{12,8},{16,20},{20,16},{24,28},{28,24},{1,5},{5... | collective-permute-start | bytes 786440 | tf_op jit(solution)/shard_map/ppermute | solution.py:16
  337.9 11.8 %collective-permute-start.6 = (f32[2,512,128]{2,1,0:T(8,128)}, f32[2,512,128]{2,1,0:T(8,128)S(1)}, u32[]{:S(2)}, u32[]{:S(2)}) collective-permute-start(f32[2,512,128]{2,1,0:T(8,128)} %maximum_select_fusion.4), channel_id=1, source_target_pairs={{0,8},{4,12},{8,0},{12,4},{16,24},{20,28},{24,16},{28,20},{1,9},{5... | collective-permute-start | bytes 1572872 | tf_op jit(solution)/shard_map/ppermute | solution.py:16
  349.9 4.9 %copy-start.5 = (f32[512,128]{1,0:T(8,128)S(1)}, f32[512,128]{1,0:T(8,128)}, u32[]{:S(2)}) copy-start(f32[512,128]{1,0:T(8,128)} %all-reduce.9.cloned.1.call-done) | copy-start | bytes 786436
  349.9 1.0 copy-start.8
  391.0 11.4 %copy-start.4 = (f32[512,128]{1,0:T(8,128)S(1)}, f32[512,128]{1,0:T(8,128)}, u32[]{:S(2)}) copy-start(f32[512,128]{1,0:T(8,128)} %all-reduce.11.cloned.1.call-done) | copy-start | bytes 786436
  391.0 6.9 %collective-permute-start.7 = (f32[512,128]{1,0:T(8,128)}, f32[512,128]{1,0:T(8,128)S(1)}, u32[]{:S(2)}, u32[]{:S(2)}) collective-permute-start(f32[512,128]{1,0:T(8,128)} %all-reduce.11.cloned.1.call-done), channel_id=1, source_target_pairs={{0,4},{4,0},{8,12},{12,8},{16,20},{20,16},{24,28},{28,24},{1,5},{5... | collective-permute-start | bytes 786440 | tf_op jit(solution)/shard_map/ppermute | solution.py:16
  399.9 11.9 %collective-permute-start.8 = (f32[2,512,128]{2,1,0:T(8,128)}, f32[2,512,128]{2,1,0:T(8,128)}, u32[]{:S(2)}, u32[]{:S(2)}) collective-permute-start(f32[2,512,128]{2,1,0:T(8,128)} %maximum_select_fusion.6), channel_id=1, source_target_pairs={{0,8},{4,12},{8,0},{12,4},{16,24},{20,28},{24,16},{28,20},{1,9},{5... | collective-permute-start | bytes 1572872 | tf_op jit(solution)/shard_map/ppermute | solution.py:16
  413.1 4.6 %copy-start.1 = (f32[1,256,128]{2,1,0:T(8,128)S(1)}, f32[1,256,128]{2,1,0:T(8,128)}, u32[]{:S(2)}) copy-start(f32[1,256,128]{2,1,0:T(8,128)} %param.13) | copy-start | bytes 393220
Sparse Core Ops, SparseCore 0:
  119.3 31.6 all-reduce.4
  172.6 33.3 all-reduce.6
  297.4 31.7 all-reduce.8
  358.0 32.9 all-reduce.10
where the time goes:
time: 432 us; the launch traced here: 425 us
  waiting for transfers between devices  223 us (52%)
  other arithmetic  70.8 us (16%)
  local copies, waits for them, and re-layouts  54 us (12%)
  starting transfers between devices  25.3 us (6%)
  matrix products  23.5 us (5%)
  between operations  14.8 us (3%)
  blocking collectives  13.1 us (3%)
    psum x4, waiting for transfers between devices, from_root(): return lax.psum(jnp.where(mine, array, jnp.zeros_like(array)), axis)  130 us
    ppermute x9, waiting for transfers between devices, partner(): lax.ppermute(array, axis, [(i, i ^ 1 << stride) for i in range(lax.axis_s...  85.2 us
    scatter-add x1, other arithmetic, local(): jax.ops.segment_sum(jnp.swapaxes(child_terms, 1, 2).reshape(-1, child_row...  15.3 us
    ppermute x9, starting transfers between devices, partner(): lax.ppermute(array, axis, [(i, i ^ 1 << stride) for i in range(lax.axis_s...  13.8 us
    scatter-add x1, other arithmetic, local(): jax.ops.segment_sum(by_cols, row_ids.reshape(-1), num_segments=half_rows...  13.8 us
    dot_general x4, matrix products, apply_panel(): jnp.dot(lower_rows, (col_rows * keep_cols).T, precision=HIGHEST)  12.1 us
    scatter-add x2, other arithmetic, spread_cols(): jax.ops.segment_sum(piece.T, col_ids, num_segments=quarter + 1)[:-1]  9.7 us
  transfers between devices with their start and end apart: 15, of which 13 were waited for; matrix products, arithmetic and copies ran while one was open for 11% of the time, Pallas kernels for 0%

commit v1 on v0

v1 whole, which is shorter than its diff:
```python
import functools

import jax
import jax.numpy as jnp
from jax import lax
from jax.experimental import pallas as pl
from jax.experimental.pallas import tpu as pltpu
from jax.sharding import PartitionSpec as P

NU = 2048
PIV = 128
KU = 256
QUARTER = NU // 4
HALF = NU // 2

HIGHEST = lax.Precision.HIGHEST
F32 = jnp.float32
BF16 = jnp.bfloat16
AXES = ("cube", "front")
NN = (((1,), (0,)), ((), ()))
NT = (((1,), (1,)), ((), ()))


def mm(a, b, dims=NN):
    return lax.dot_general(a, b, dims, preferred_element_type=F32)


def exact(a, b, dims=NN):
    return lax.dot_general(a, b, dims, preferred_element_type=F32, precision=HIGHEST)


def split(x):
    high = x.astype(BF16)
    return high, (x - high.astype(F32)).astype(BF16)


def split3(x):
    high = x.astype(BF16)
    rest = x - high.astype(F32)
    mid = rest.astype(BF16)
    return high, mid, (rest - mid.astype(F32)).astype(BF16)


def mm3(a, b, dims=NN):
    ah, al = split(a)
    bh, bl = split(b)
    return mm(ah, bh, dims) + (mm(ah, bl, dims) + mm(al, bh, dims))


def iota(shape, axis):
    return lax.broadcasted_iota(jnp.int32, shape, axis)


def onehot(mask):
    return jnp.where(mask, 1.0, 0.0).astype(BF16)


def newton_inverse(block):
    size = block.shape[0]
    eye = iota((size, size), 0) == iota((size, size), 1)
    diagonal = jnp.where(eye, block, 0.0)
    row = 1.0 / jnp.sum(diagonal, axis=0, keepdims=True)
    col = 1.0 / jnp.sum(diagonal, axis=1, keepdims=True)
    current = jnp.where(eye, 2.0 * row, 0.0) - col * (block * row)
    return 2.0 * current - exact(current, exact(block, current))


def pack_kernel(capacity, slots, cube_count, blocks, owner, target, out):
    count = blocks.shape[0]
    owners = owner[...]
    named = iota((max(cube_count, 16), count), 0) == owners
    earlier = onehot(iota((count, count), 0) < iota((count, count), 1))
    ranks = mm(onehot(named), earlier)
    rank = jnp.sum(jnp.where(named, ranks, 0.0), axis=0, keepdims=True).astype(jnp.int32)
    first = owners * slots
    spots = iota((cube_count * slots, count), 0)
    place = onehot(spots == first + rank)
    high, mid, low = split3(blocks[...])
    values = mm(place, high) + (mm(place, mid) + mm(place, low))
    tags = jnp.where(spots == first + capacity, target[...].astype(F32), 0.0).astype(BF16)
    lanes = onehot(iota((blocks.shape[1], count), 0) == rank)
    out[...] = values + mm(tags, lanes, NT)


def prepare_kernel(where, leaf_pivot, signs, perturb, leaf_map, level_map, inverse, links):
    size = leaf_pivot.shape[1]
    eye = iota((size, size), 0) == iota((size, size), 1)
    table = level_map[pl.ds(where[4], 1), :]
    rows = iota((16, NU), 0)
    digits = jnp.where(rows == 0, table // 256, jnp.where(rows == 1, table % 256, 0))
    digits = digits.astype(F32).astype(BF16)
    links[...] = jnp.zeros(links.shape, F32)
    for leaf in range(leaf_pivot.shape[0]):
        shift = signs[leaf : leaf + 1, :].astype(F32) * perturb[leaf : leaf + 1, :]
        inverse[leaf] = newton_inverse(leaf_pivot[leaf] + jnp.where(eye, shift, 0.0))
        found = mm(digits, onehot(iota((NU, size), 0) == leaf_map[leaf : leaf + 1, :]))
        links[leaf : leaf + 1, :] = found[0:1, :] * 256.0 + found[1:2, :]


def leaf_kernel(capacity, slots, cube_count, got, inverse, links, coupling, factor, sent):
    leaves, rows, width = coupling.shape

    def arrivals(cube):
        block = got[cube]
        tags = block[capacity : capacity + 1, :].astype(jnp.int32)
        here = (iota((leaves * rows, width), 0) == tags) & (iota((leaves * rows, width), 1) < capacity)
        values = block
        if slots < width:
            values = jnp.concatenate([block, jnp.zeros((width - slots, width), F32)], axis=0)
        return onehot(here), values

    if cube_count <= 16:
        pairs = [arrivals(cube) for cube in range(cube_count)]
        place = jnp.concatenate([here for here, _ in pairs], axis=1)
        high, mid, low = split3(jnp.concatenate([values for _, values in pairs], axis=0))
        added = mm(place, high) + (mm(place, mid) + mm(place, low))
    else:

        def step(cube, total):
            here, values = arrivals(cube)
            high, mid, low = split3(values)
            return total + (mm(here, high) + (mm(here, mid) + mm(here, low)))

        added = lax.fori_loop(0, cube_count, step, jnp.zeros((leaves * rows, width), F32))
    for leaf in range(leaves):
        rhs = coupling[leaf] + added[leaf * rows : (leaf + 1) * rows, :]
        part = exact(rhs, inverse[leaf])
        factor[leaf] = part
        sent[leaf, 0:rows, :] = -mm3(part, rhs, NT)
        sent[leaf, rows : rows + 8, :] = jnp.where(
            iota((8, width), 0) == 0, links[leaf : leaf + 1, :], 0.0
        )


def panel_parts(pivots):
    upper = newton_inverse(pivots[0:PIV, 0:PIV])
    below = pivots[PIV:KU, 0:PIV]
    lower = newton_inverse(
        pivots[PIV:KU, PIV:KU] - exact(exact(below, upper), below, NT)
    )
    return upper, below, lower


def panel_rows(rows, first, upper, below, lower):
    position = first + iota((rows.shape[0], PIV), 0)
    left = jnp.where(position >= PIV, mm3(rows[:, 0:PIV], upper), 0.0)
    right = rows[:, PIV:KU] - mm3(left, below, NT)
    last = jnp.where(position >= KU, mm3(right, lower), 0.0)
    keep = jnp.concatenate(
        [jnp.where(position >= PIV, rows[:, 0:PIV], 0.0), jnp.where(position >= KU, right, 0.0)], axis=1
    )
    return jnp.concatenate([left, last], axis=1), keep


def mid_kernel(where, front, from_x, from_y, from_core, pair, far, factor, left, cols, send, rows):
    low, high, pos = where[0], where[1], where[2]
    is_low = low == 0

    @pl.when(pos == 0)
    def _():
        rows[...] = front[:, 0:KU].astype(F32)

    @pl.when(pos == 2)
    def _():
        rows[...] = from_x[...]

    @pl.when(pos % 2 == 1)
    def _():
        rows[...] = from_core[0:HALF, :]

    own_cols = pl.multiple_of((pos % 2) * QUARTER, QUARTER)
    held = (pos // 2) == low
    other_cols = jnp.where(
        pos == 0,
        from_y[0:QUARTER, :],
        jnp.where(
            pos == 1, from_core[HALF : HALF + QUARTER, :], jnp.where(pos == 2, pair[...], far[...])
        ),
    )
    col_rows = jnp.where(held, rows[pl.ds(own_cols, QUARTER), :], other_cols)
    other_pivots = jnp.where(pos == 1, from_core[HALF + QUARTER :, :], other_cols[0:KU, :])
    pivots = jnp.where(is_low, rows[0:KU, :], other_pivots)
    upper, below, lower = panel_parts(pivots)
    row_left, _ = panel_rows(rows[...], low * HALF, upper, below, lower)
    _, col_keep = panel_rows(col_rows, pos * QUARTER, upper, below, lower)
    left[...] = row_left
    cols[...] = col_keep
    slab = HALF // 4
    factor[...] = left[pl.ds(pl.multiple_of(pos * slab, slab), slab), :]
    start = pl.multiple_of((1 - high) * QUARTER, QUARTER)
    send[...] = front[pl.ds(start, QUARTER), :].astype(F32) - mm3(
        left[pl.ds(start, QUARTER), :], col_keep, NT
    )


def spread(values, level_map, group, row_quarter, col_quarter):
    def places(quarter):
        start = pl.multiple_of(quarter * QUARTER, QUARTER)
        target = level_map[pl.ds(group, 1), pl.ds(start, QUARTER)] - start
        from_pos = start + iota((1, QUARTER), 1)
        target = jnp.where(from_pos >= KU, target, -1)
        return onehot(iota((QUARTER, QUARTER), 0) == target)

    row_place = places(row_quarter)
    col_place = places(col_quarter)
    high, low = split(values)
    high, low = split(mm(row_place, high) + mm(row_place, low))
    return mm(high, col_place, NT) + mm(low, col_place, NT)


def own_kernel(where, front, left, cols, level_map, base, out):
    start = pl.multiple_of(where[1] * QUARTER, QUARTER)
    block = front[pl.ds(start, QUARTER), :].astype(F32) - mm3(
        left[pl.ds(start, QUARTER), :], cols[...], NT
    )
    out[...] = base[...] + spread(block, level_map, where[4], where[3], where[2])


def other_kernel(where, block, level_map, base, out):
    group = where[4] + 1 - 2 * where[1]
    out[...] = base[...] + spread(block[...], level_map, group, where[3], where[2])


def top_kernel(where, front, from_x, from_core, from_y, from_z, pivots_z, out, rows):
    low, high, pos, quarter = where[0], where[1], where[2], where[3]

    @pl.when(pos == 0)
    def _():
        rows[...] = front[:, 0:KU].astype(F32)

    @pl.when(pos == 2)
    def _():
        rows[...] = from_x[...]

    @pl.when(pos % 2 == 1)
    def _():
        rows[...] = from_core[...]

    own = rows[...]
    col_rows = jnp.where(
        quarter == pos, own, jnp.where(high == pos % 2, from_y[...], from_z[...])
    )
    pivots = jnp.where(
        pos == 0,
        col_rows[0:KU, :],
        jnp.where(
            high == 1, pivots_z[...], jnp.where(low == 0, own[0:KU, :], from_y[0:KU, :])
        ),
    )
    upper, below, lower = panel_parts(pivots)
    row_left, _ = panel_rows(own, quarter * QUARTER, upper, below, lower)
    _, col_keep = panel_rows(col_rows, pos * QUARTER, upper, below, lower)
    out[...] = front[...].astype(F32) - mm3(row_left, col_keep, NT)


def gather_kernel(count, where, *refs):
    own, swapped, base, out = refs[0:count], refs[count], refs[count + 1], refs[count + 2]
    row_first = where[3] * QUARTER
    col_first = where[2] * QUARTER
    width = own[0].shape[2]
    leaves = own[0].shape[0]
    total = base[...]
    for chip in range(count):
        places, highs, lows = [], [], []
        for source in (own[chip], swapped.at[chip]):
            for leaf in range(leaves):
                link = source[leaf, width : width + 1, :].astype(jnp.int32)
                spots = iota((QUARTER, width), 0)
                places.append(onehot(spots == link - row_first))
                cols = onehot(spots == link - col_first)
                high, low = split(source[leaf, 0:width, :])
                high, low = split(mm(high, cols, NT) + mm(low, cols, NT))
                highs.append(high)
                lows.append(low)
        place = jnp.concatenate(places, axis=1)
        total = total + (
            mm(place, jnp.concatenate(highs, axis=0)) + mm(place, jnp.concatenate(lows, axis=0))
        )
    out[...] = total


def call(body, outs, args, scalars=True, scratch=(), flops=10**8):
    specs = [pl.BlockSpec(memory_space=pltpu.VMEM) for _ in args]
    if scalars:
        specs[0] = pl.BlockSpec(memory_space=pltpu.SMEM)
    shapes = [jax.ShapeDtypeStruct(shape, F32) for shape in outs]
    moved = sum(4 * functools.reduce(lambda a, b: a * b, shape) for shape in outs)
    single = len(shapes) == 1
    return pl.pallas_call(
        body,
        out_shape=shapes[0] if single else shapes,
        in_specs=specs,
        out_specs=(
            pl.BlockSpec(memory_space=pltpu.VMEM)
            if single
            else [pl.BlockSpec(memory_space=pltpu.VMEM) for _ in shapes]
        ),
        scratch_shapes=list(scratch),
        compiler_params=pltpu.CompilerParams(vmem_limit_bytes=40 * 2**20),
        cost_estimate=pl.CostEstimate(flops=flops, bytes_accessed=2 * moved, transcendentals=0),
    )(*args)


def local(
    kkt_blocks,
    kkt_owner,
    kkt_target,
    leaf_pivot,
    pivot_signs,
    perturb,
    leaf_coupling,
    leaf_map,
    mid_front,
    level_map,
    top_front,
):
    cube_count = lax.axis_size("cube")
    front_count = lax.axis_size("front")
    cube = lax.axis_index("cube")
    front = lax.axis_index("front")
    b0 = cube % 2
    b1 = cube // 2 % 2
    quarter = 2 * b0 + b1
    where = jnp.stack([b0, b1, front, quarter, cube // 2]).astype(jnp.int32)

    def move(array, rule):
        pairs = []
        for source_cube in range(cube_count):
            for source_front in range(front_count):
                target = rule(source_cube % 2, source_cube // 2 % 2, source_front)
                if target is not None:
                    new_cube = source_cube // 4 * 4 + 2 * target[1] + target[0]
                    pairs.append(
                        (source_cube * front_count + source_front, new_cube * front_count + target[2])
                    )
        return lax.ppermute(array, AXES, pairs)

    blocks = kkt_blocks[0]
    block_count, width = blocks.shape
    capacity = max(2, 2 * block_count // cube_count)
    slots = -(-(capacity + 1) // 8) * 8

    mid_cols = mid_front[:, 0:KU].astype(F32)
    top_cols = top_front[:, 0:KU].astype(F32)

    packed = call(
        functools.partial(pack_kernel, capacity, slots, cube_count),
        [(cube_count * slots, width)],
        [blocks, kkt_owner.reshape(1, block_count), kkt_target.reshape(1, block_count)],
        scalars=False,
    )
    got = lax.all_to_all(
        packed.reshape(cube_count, slots, width), "cube", split_axis=0, concat_axis=0, tiled=True
    )

    mid_x = move(mid_cols, lambda y, z, f: (y, z, 2) if f == 0 else None)
    mid_y = move(mid_cols, lambda y, z, f: (1 - y, z, 0) if f == 0 else None)
    mid_core = move(
        jnp.concatenate(
            [jnp.where(front == 0, mid_cols, mid_x), mid_y[QUARTER:HALF], mid_y[0:KU]], axis=0
        ),
        lambda y, z, f: (y, z, f + 1) if f % 2 == 0 else None,
    )
    mid_pair = move(mid_x[0:QUARTER], lambda y, z, f: (1 - y, z, 2) if f == 2 else None)
    mid_far = move(
        jnp.where(b0 == 0, mid_y[QUARTER:HALF], mid_y[0:QUARTER]),
        lambda y, z, f: (y, z, 3) if f == 0 else None,
    )

    top_x = move(top_cols, lambda y, z, f: (y, z, 2) if f == 0 else None)
    top_core = move(
        jnp.where(front == 0, top_cols, top_x), lambda y, z, f: (y, z, f + 1) if f % 2 == 0 else None
    )
    top_rows = jnp.where(front == 0, top_cols, jnp.where(front == 2, top_x, top_core))

    def down_y(y, z, f):
        if y == 0:
            return (1, z, f) if z == 0 or f == 1 else None
        return (0, z, f) if (z, f) in ((0, 2), (1, 3)) else None

    top_y = move(top_rows, down_y)
    top_z = move(
        jnp.where(quarter == front, top_rows, top_y),
        lambda y, z, f: (y, 1 - z, f) if z == f % 2 else None,
    )
    top_pivots = move(
        jnp.where(b0 == 0, top_rows[0:KU], top_y[0:KU]),
        lambda y, z, f: (y, 1, f) if z == 0 and f > 0 else None,
    )

    leaves = leaf_pivot.shape[0]
    size = leaf_pivot.shape[2]
    inverse, links = call(
        prepare_kernel,
        [(leaves, size, size), (8, size)],
        [where, leaf_pivot, pivot_signs, perturb, leaf_map, level_map],
    )
    factor, sent = call(
        functools.partial(leaf_kernel, capacity, slots, cube_count),
        [leaf_coupling.shape, (leaves, size + 8, size)],
        [got, inverse, links, leaf_coupling],
        scalars=False,
    )

    k_x = move(sent, lambda y, z, f: (y, z, f ^ 2))
    k_y = move(sent, lambda y, z, f: (1 - y, z, f))
    k_z = move(sent, lambda y, z, f: (y, 1 - z, f))
    k_xy = move(k_y, lambda y, z, f: (y, z, f ^ 2))
    k_yz = move(k_z, lambda y, z, f: (1 - y, z, f))
    k_xz = move(k_x, lambda y, z, f: (y, 1 - z, f))
    k_xyz = move(k_yz, lambda y, z, f: (y, z, f ^ 2))
    chips = [sent, k_x, k_y, k_z, k_xy, k_yz, k_xz, k_xyz]
    swapped = move(jnp.stack(chips), lambda y, z, f: (y, z, f ^ 1))

    mid_factor, mid_left, mid_keep, mid_send = call(
        mid_kernel,
        [(HALF // front_count, KU), (HALF, KU), (QUARTER, KU), (QUARTER, QUARTER)],
        [where, mid_front, mid_x, mid_y, mid_core, mid_pair, mid_far],
        scratch=[pltpu.VMEM((HALF, KU), F32)],
    )
    mid_other = move(mid_send, lambda y, z, f: (y, 1 - z, f))

    square = [(QUARTER, QUARTER)]
    upper = call(
        top_kernel,
        square,
        [where, top_front, top_x, top_core, top_y, top_z, top_pivots],
        scratch=[pltpu.VMEM((QUARTER, KU), F32)],
    )
    upper = call(own_kernel, square, [where, mid_front, mid_left, mid_keep, level_map, upper])
    upper = call(
        functools.partial(gather_kernel, len(chips)), square, [where, *chips, swapped, upper]
    )
    upper = call(other_kernel, square, [where, mid_other, level_map, upper])
    return factor, mid_factor, upper


def solution(mesh):
    in_specs = (
        P("front", "cube", None),
        P("front", "cube", None),
        P("front", "cube"),
        P("cube", "front", None),
        P("cube", "front"),
        P("cube", "front"),
        P("cube", "front", None),
        P("cube", "front"),
        P("cube", "front"),
        P(),
        P("cube", "front"),
    )
    out_specs = (P("cube", "front", None), P(("cube", "front"), None), P("cube", "front"))
    return jax.shard_map(local, mesh=mesh, in_specs=in_specs, out_specs=out_specs, check_vma=False)
```

time: 432 us -> 118 us (0.27)
  the two profiles are of different devices: /device:TPU:0 before, /device:TPU:14 now
where the time goes in v1:
time: 118 us
  waiting for transfers between devices  38.3 us (32%)
  starting transfers between devices  30.6 us (26%)
  Pallas kernels  27.4 us (23%)
  local copies, waits for them, and re-layouts  13.6 us (12%)
  other arithmetic  6.46 us (5%)
    ppermute x19, waiting for transfers between devices, move(): return lax.ppermute(array, AXES, pairs)  36.6 us
    pallas_call x8, Pallas kernels, call(): pl.pallas_call(body, out_shape=shapes[0] if single else shapes, in_specs=...  27.4 us
    ppermute x19, starting transfers between devices, move(): return lax.ppermute(array, AXES, pairs)  24.3 us
    unnamed x79, local copies, waits for them, and re-layouts  12 us
    all_to_all x1, starting transfers between devices, local(): lax.all_to_all(packed.reshape(cube_count, slots, width), 'cube', split_ax...  6.22 us
  transfers between devices with their start and end apart: 20, of which 5 were waited for; matrix products, arithmetic and copies ran while one was open for 8% of the time, Pallas kernels for 20%

profile of v1, /device:TPU:14, one launch (start us, length us, event | category | flops | bytes accessed | tf_op | source)
XLA Modules:
  0.0 117.5 jit_solution(13530868010675096207)
XLA Ops:
  0.7 2.2 %slice_convert_fusion = f32[1024,256]{1,0:T(8,128)} fusion(bf16[1024,512]{1,0:T(8,128)(2,1)} %front.5), kind=kLoop, calls=%fused_computation.3 | loop fusion | flops 262144 | bytes 1572864 | tf_op jit(solution)/shard_map/convert_element_type | solution.py:343
  2.8 0.9 collective-permute-start.1
  3.7 1.3 %collective-permute-start = (f32[1024,256]{1,0:T(8,128)}, f32[1024,256]{1,0:T(8,128)S(1)}, u32[]{:S(2)}, u32[]{:S(2)}) collective-permute-start(f32[1024,256]{1,0:T(8,128)} %slice_convert_fusion), channel_id=1, source_target_pairs={{0,2},{4,6},{8,10},{12,14},{16,18},{20,22},{24,26},{28,30}} | collective-permute-start | bytes 3145736 | tf_op jit(solution)/shard_map/ppermute | solution.py:336
  5.0 1.3 %shard_map.130 = f32[576,128]{1,0:T(8,128)} custom-call(f32[256,128]{1,0:T(8,128)S(1)} %bitcast.24, s32[1,256]{1,0:T(1,128)S(1)} %bitcast.25, s32[1,256]{1,0:T(1,128)S(1)} %copy-done.31), custom_call_target="tpu_custom_call" | custom-call | flops 100000000 | bytes 589824 | tf_op jit(solution)/shard_map/pallas_call | solution.py:289
  6.4 6.2 %all-to-all-start = ((f32[8,72,128]{2,1,0:T(8,128)}), f32[8,72,128]{2,1,0:T(8,128)S(1)}, u32[]{:S(2)}, u32[]{:S(2)}) async-start(f32[8,72,128]{2,1,0:T(8,128)} %bitcast.2), calls=%async_computation | async-start | bytes 589824 | tf_op jit(solution)/shard_map/all_to_all | solution.py:352
  12.6 0.8 slice_convert_fusion.1
  13.4 1.3 %collective-permute-start.14 = (f32[512,256]{1,0:T(8,128)}, f32[512,256]{1,0:T(8,128)S(1)}, u32[]{:S(2)}, u32[]{:S(2)}) collective-permute-start(f32[512,256]{1,0:T(8,128)} %slice_convert_fusion.1), channel_id=1, source_target_pairs={{0,2},{4,6},{8,10},{12,14},{16,18},{20,22},{24,26},{28,30}} | collective-permute-start | bytes 1572872 | tf_op jit(solution)/shard_map/ppermute | solution.py:336
  14.9 0.9 copy-done.32
  15.8 1.3 %shard_map.131 = (f32[2,128,128]{2,1,0:T(8,128)S(1)}, f32[8,128]{1,0:T(8,128)S(1)}) custom-call(s32[5]{0:T(128)S(1)} %stack.50.where, f32[2,128,128]{2,1,0:T(8,128)S(1)} %copy-done.32, s32[2,128]{1,0:T(2,128)S(1)} %copy-done.33, f32[2,128]{1,0:T(2,128)S(1)} %copy-done.34, s32[2,128]{1,0:T(2,128)S(1)} %copy-done.35, s32[4,2048]{1,0:T(4,128)S(1)} %copy-done.25), custom_call_target="tpu_custom_call" | custom-call | flops 100000000 | bytes 270336 | tf_op jit(solution)/shard_map/pallas_call | solution.py:289
  17.1 0.7 copy-done.27
  17.8 1.7 %all-to-all-done.got = f32[8,72,128]{2,1,0:T(8,128)S(1)} async-done(((f32[8,72,128]{2,1,0:T(8,128)}), f32[8,72,128]{2,1,0:T(8,128)S(1)}, u32[]{:S(2)}, u32[]{:S(2)}) %all-to-all-start) | async-done | bytes 294944 | tf_op jit(solution)/shard_map/all_to_all | solution.py:352
  19.5 0.9 copy-done.26
  20.4 0.9 copy-done.28
  21.3 1.8 %shard_map.132 = (f32[2,128,128]{2,1,0:T(8,128)}, f32[2,136,128]{2,1,0:T(8,128)S(1)}) custom-call(f32[8,72,128]{2,1,0:T(8,128)S(1)} %all-to-all-done.got, f32[2,128,128]{2,1,0:T(8,128)S(1)} %copy-done.28, f32[8,128]{1,0:T(8,128)S(1)} %get-tuple-element.12.links, f32[2,128,128]{2,1,0:T(8,128)S(1)} %copy-done.26), custom_call_target="tpu_custom_call" | custom-call | flops 100000000 | bytes 540672 | tf_op jit(solution)/shard_map/pallas_call | solution.py:289
  23.1 4.1 %collective-permute-start.6 = (f32[2,136,128]{2,1,0:T(8,128)S(1)}, f32[2,136,128]{2,1,0:T(8,128)S(1)}, u32[]{:S(2)}, u32[]{:S(2)}) collective-permute-start(f32[2,136,128]{2,1,0:T(8,128)S(1)} %get-tuple-element.16.refs_0_), channel_id=1, source_target_pairs={{0,2},{1,3},{2,0},{3,1},{4,6},{5,7},{6,4},{7,5},{8,10},{9,11},{10,... | collective-permute-start | bytes 417800 | tf_op jit(solution)/shard_map/ppermute | solution.py:336
  27.7 0.7 bitcast_dynamic-update-slice_fusion.7
  28.6 2.2 %collective-permute-done.6.refs_1_ = f32[2,136,128]{2,1,0:T(8,128)S(1)} collective-permute-done((f32[2,136,128]{2,1,0:T(8,128)S(1)}, f32[2,136,128]{2,1,0:T(8,128)S(1)}, u32[]{:S(2)}, u32[]{:S(2)}) %collective-permute-start.6) | collective-permute-done | bytes 139296 | tf_op jit(solution)/shard_map/ppermute | solution.py:336
  30.9 1.3 %collective-permute-start.15 = (f32[512,256]{1,0:T(8,128)S(1)}, f32[512,256]{1,0:T(8,128)S(1)}, u32[]{:S(2)}, u32[]{:S(2)}) collective-permute-start(f32[512,256]{1,0:T(8,128)S(1)} %convert_select_fusion), channel_id=1, source_target_pairs={{0,1},{2,3},{4,5},{6,7},{8,9},{10,11},{12,13},{14,15},{16,17},{18,... | collective-permute-start | bytes 1572872 | tf_op jit(solution)/shard_map/ppermute | solution.py:336
  32.2 1.3 %collective-permute-done.7.refs_2_ = f32[2,136,128]{2,1,0:T(8,128)S(1)} collective-permute-done((f32[2,136,128]{2,1,0:T(8,128)S(1)}, f32[2,136,128]{2,1,0:T(8,128)S(1)}, u32[]{:S(2)}, u32[]{:S(2)}) %collective-permute-start.7) | collective-permute-done | bytes 139296 | tf_op jit(solution)/shard_map/ppermute | solution.py:336
  33.5 1.2 %collective-permute-start.9 = (f32[2,136,128]{2,1,0:T(8,128)S(1)}, f32[2,136,128]{2,1,0:T(8,128)S(1)}, u32[]{:S(2)}, u32[]{:S(2)}) collective-permute-start(f32[2,136,128]{2,1,0:T(8,128)S(1)} %collective-permute-done.7.refs_2_), channel_id=1, source_target_pairs={{0,2},{1,3},{2,0},{3,1},{4,6},{5,7},{6,4},{7,5},{8,10},{9,11},{10,... | collective-permute-start | bytes 417800 | tf_op jit(solution)/shard_map/ppermute | solution.py:336
  34.8 0.8 collective-permute-start.10
  35.6 1.2 %collective-permute-start.11 = (f32[2,136,128]{2,1,0:T(8,128)S(1)}, f32[2,136,128]{2,1,0:T(8,128)S(1)}, u32[]{:S(2)}, u32[]{:S(2)}) collective-permute-start(f32[2,136,128]{2,1,0:T(8,128)S(1)} %collective-permute-done.6.refs_1_), channel_id=1, source_target_pairs={{0,8},{1,9},{2,10},{3,11},{4,12},{5,13},{6,14},{7,15},{8,0},{9,1},... | collective-permute-start | bytes 417800 | tf_op jit(solution)/shard_map/ppermute | solution.py:336
  36.9 1.1 copy-done
  38.1 0.8 slice-done
  39.1 1.4 %collective-permute-start.2 = (f32[1792,256]{1,0:T(8,128)S(1)}, f32[1792,256]{1,0:T(8,128)S(1)}, u32[]{:S(2)}, u32[]{:S(2)}) collective-permute-start(f32[1792,256]{1,0:T(8,128)S(1)} %pad_maximum_fusion), channel_id=1, source_target_pairs={{0,1},{2,3},{4,5},{6,7},{8,9},{10,11},{12,13},{14,15},{16,17},{18,... | collective-permute-start | bytes 5505032 | tf_op jit(solution)/shard_map/ppermute | solution.py:336
  40.5 0.7 bitcast_dynamic-update-slice_fusion.6
  42.5 0.7 bitcast_dynamic-update-slice_fusion.3
  43.9 0.7 bitcast_dynamic-update-slice_fusion.1
  44.7 3.2 %collective-permute-start.3 = (f32[512,256]{1,0:T(8,128)S(1)}, f32[512,256]{1,0:T(8,128)S(1)}, u32[]{:S(2)}, u32[]{:S(2)}) collective-permute-start(f32[512,256]{1,0:T(8,128)S(1)} %slice.35), channel_id=1, source_target_pairs={{2,6},{6,2},{10,14},{14,10},{18,22},{22,18},{26,30},{30,26}} | collective-permute-start | bytes 1572872 | tf_op jit(solution)/shard_map/ppermute | solution.py:336
  47.9 0.7 collective-permute-start.4
  48.7 0.9 select_select_fusion
  49.5 0.8 copy-done.7
  50.4 1.5 %collective-permute-start.16 = (f32[512,256]{1,0:T(8,128)}, f32[512,256]{1,0:T(8,128)}, u32[]{:S(2)}, u32[]{:S(2)}) collective-permute-start(f32[512,256]{1,0:T(8,128)} %select_select_fusion), channel_id=1, source_target_pairs={{0,4},{1,5},{2,6},{3,7},{6,2},{9,13},{15,11},{16,20},{17,21},{18,2... | collective-permute-start | bytes 1572872 | tf_op jit(solution)/shard_map/ppermute | solution.py:336
  51.8 0.7 bitcast_dynamic-update-slice_fusion
  52.6 4.8 %collective-permute-done.3.pair = f32[512,256]{1,0:T(8,128)S(1)} collective-permute-done((f32[512,256]{1,0:T(8,128)S(1)}, f32[512,256]{1,0:T(8,128)S(1)}, u32[]{:S(2)}, u32[]{:S(2)}) %collective-permute-start.3) | collective-permute-done | bytes 524320 | tf_op jit(solution)/shard_map/ppermute | solution.py:336
  57.4 4.7 %shard_map.133 = (f32[256,256]{1,0:T(8,128)}, f32[1024,256]{1,0:T(8,128)S(1)}, f32[512,256]{1,0:T(8,128)S(1)}, f32[512,512]{1,0:T(8,128)}) custom-call(s32[5]{0:T(128)S(1)} %stack.50.where, bf16[1024,512]{1,0:T(8,128)(2,1)S(1)} %copy-done, f32[1024,256]{1,0:T(8,128)S(1)} %collective-permute-done.from_x, f32[1024,256]{1,0:T(8,128)S(1)} %copy-done.2, ...), custom_call_target="tpu_custom_call" | custom-call | flops 100000000 | bytes 5767168 | tf_op jit(solution)/shard_map/pallas_call | solution.py:289
  62.1 1.0 copy-done.9
  63.1 0.8 copy-done.23
  63.9 2.0 %collective-permute-start.5 = (f32[512,512]{1,0:T(8,128)}, f32[512,512]{1,0:T(8,128)}, u32[]{:S(2)}, u32[]{:S(2)}) collective-permute-start(f32[512,512]{1,0:T(8,128)} %get-tuple-element.15), channel_id=1, source_target_pairs={{0,8},{1,9},{2,10},{3,11},{4,12},{5,13},{6,14},{7,15},{8,0},{9,1},... | collective-permute-start | bytes 3145736 | tf_op jit(solution)/shard_map/ppermute | solution.py:336
  65.9 1.2 broadcast_select_fusion.1
  67.1 1.3 %collective-permute-start.17 = (f32[512,256]{1,0:T(8,128)S(1)}, f32[512,256]{1,0:T(8,128)S(1)}, u32[]{:S(2)}, u32[]{:S(2)}) collective-permute-start(f32[512,256]{1,0:T(8,128)S(1)} %broadcast_select_fusion.1), channel_id=1, source_target_pairs={{0,8},{2,10},{4,12},{6,14},{9,1},{11,3},{13,5},{15,7},{16,24},{18,... | collective-permute-start | bytes 1572872 | tf_op jit(solution)/shard_map/ppermute | solution.py:336
  68.4 1.1 slice_select_fusion.1
  69.5 1.4 %collective-permute-start.18 = (f32[256,256]{1,0:T(8,128)S(1)}, f32[256,256]{1,0:T(8,128)S(1)}, u32[]{:S(2)}, u32[]{:S(2)}) collective-permute-start(f32[256,256]{1,0:T(8,128)S(1)} %slice_select_fusion.1), channel_id=1, source_target_pairs={{1,9},{2,10},{3,11},{5,13},{6,14},{7,15},{17,25},{18,26},{19,27},{... | collective-permute-start | bytes 786440 | tf_op jit(solution)/shard_map/ppermute | solution.py:336
  70.9 28.2 %collective-permute-done.18.pivots_z = f32[256,256]{1,0:T(8,128)S(1)} collective-permute-done((f32[256,256]{1,0:T(8,128)S(1)}, f32[256,256]{1,0:T(8,128)S(1)}, u32[]{:S(2)}, u32[]{:S(2)}) %collective-permute-start.18) | collective-permute-done | bytes 262176 | tf_op jit(solution)/shard_map/ppermute | solution.py:336
  99.1 4.3 %shard_map.134.base = f32[512,512]{1,0:T(8,128)S(1)} custom-call(s32[5]{0:T(128)S(1)} %stack.50.where, bf16[512,512]{1,0:T(8,128)(2,1)S(1)} %copy-done.6, f32[512,256]{1,0:T(8,128)S(1)} %copy-done.4, f32[512,256]{1,0:T(8,128)S(1)} %copy-done.8, f32[512,256]{1,0:T(8,128)} %collective-permute-done.16.from_y, f32[512,256]{1,0:T(8,128)S(1)} %collective-permute-done.17.from_z, ...), custom_call_target="tpu_custom_call" | custom-call | flops 100000000 | bytes 2097152 | tf_op jit(solution)/shard_map/pallas_call | solution.py:289
  103.5 2.4 %shard_map.135.refs_9_ = f32[512,512]{1,0:T(8,128)S(1)} custom-call(s32[5]{0:T(128)S(1)} %stack.50.where, bf16[1024,512]{1,0:T(8,128)(2,1)S(1)} %copy-done, f32[1024,256]{1,0:T(8,128)S(1)} %copy-done.10, f32[512,256]{1,0:T(8,128)S(1)} %copy-done.24, s32[4,2048]{1,0:T(4,128)S(1)} %copy-done.25, f32[512,512]{1,0:T(8,128)S(1)} %shard_map.134.base), custom_call_target="tpu_custom_call" | custom-call | flops 100000000 | bytes 2097152 | tf_op jit(solution)/shard_map/pallas_call | solution.py:289
  105.9 8.1 %shard_map.136.base = f32[512,512]{1,0:T(8,128)S(1)} custom-call(s32[5]{0:T(128)S(1)} %stack.50.where, f32[2,136,128]{2,1,0:T(8,128)S(1)} %copy-done.12, f32[2,136,128]{2,1,0:T(8,128)S(1)} %collective-permute-done.6.refs_1_, f32[2,136,128]{2,1,0:T(8,128)S(1)} %collective-permute-done.7.refs_2_, f32[2,136,128]{2,1,0:T(8,128)S(1)} %copy-done.14, ...), custom_call_target="tpu_custom_call" | custom-call | flops 100000000 | bytes 2097152 | tf_op jit(solution)/shard_map/pallas_call | solution.py:289
  114.0 3.5 %shard_map.137 = f32[512,512]{1,0:T(8,128)} custom-call(s32[5]{0:T(128)S(1)} %stack.50.where, f32[512,512]{1,0:T(8,128)} %collective-permute-done.5.block, s32[4,2048]{1,0:T(4,128)S(1)} %copy-done.25, f32[512,512]{1,0:T(8,128)S(1)} %shard_map.136.base), custom_call_target="tpu_custom_call" | custom-call | flops 100000000 | bytes 2097152 | tf_op jit(solution)/shard_map/pallas_call | solution.py:289
  (93 shorter events, 3.4 us)
Async XLA Ops:
  0.6 4.4 %copy-start.29 = (f32[1,256,128]{2,1,0:T(8,128)S(1)}, f32[1,256,128]{2,1,0:T(8,128)}, u32[]{:S(2)}) copy-start(f32[1,256,128]{2,1,0:T(8,128)} %param.11) | copy-start | bytes 393220
  0.6 4.4 %copy-start.30 = (s32[1,256,1]{1,2,0:T(1,128)S(1)}, s32[1,256,1]{1,2,0:T(1,128)}, u32[]{:S(2)}) copy-start(s32[1,256,1]{1,2,0:T(1,128)} %param.12) | copy-start | bytes 3076
  0.7 4.4 %copy-start.31 = (s32[1,256]{1,0:T(1,128)S(1)}, s32[1,256]{1,0:T(1,128)}, u32[]{:S(2)}) copy-start(s32[1,256]{1,0:T(1,128)} %target.1) | copy-start | bytes 3076
  0.7 11.9 %copy-start.5 = (bf16[512,512]{1,0:T(8,128)(2,1)S(1)}, bf16[512,512]{1,0:T(8,128)(2,1)}, u32[]{:S(2)}) copy-start(bf16[512,512]{1,0:T(8,128)(2,1)} %front.4) | copy-start | bytes 1572868
  2.8 12.0 %copy-start.25 = (s32[4,2048]{1,0:T(4,128)S(1)}, s32[4,2048]{1,0:T(4,128)}, u32[]{:S(2)}) copy-start(s32[4,2048]{1,0:T(4,128)} %level_map.5) | copy-start | bytes 98308
  2.8 12.0 %copy-start.33 = (s32[2,128]{1,0:T(2,128)S(1)}, s32[2,128]{1,0:T(2,128)}, u32[]{:S(2)}) copy-start(s32[2,128]{1,0:T(2,128)} %signs.1) | copy-start | bytes 3076
  2.8 12.0 %copy-start.34 = (f32[2,128]{1,0:T(2,128)S(1)}, f32[2,128]{1,0:T(2,128)}, u32[]{:S(2)}) copy-start(f32[2,128]{1,0:T(2,128)} %perturb.1) | copy-start | bytes 3076
  2.8 12.0 %copy-start.35 = (s32[2,128]{1,0:T(2,128)S(1)}, s32[2,128]{1,0:T(2,128)}, u32[]{:S(2)}) copy-start(s32[2,128]{1,0:T(2,128)} %leaf_map.1) | copy-start | bytes 3076
  2.8 32.8 %collective-permute-start.1 = (f32[1024,256]{1,0:T(8,128)}, f32[1024,256]{1,0:T(8,128)S(1)}, u32[]{:S(2)}, u32[]{:S(2)}) collective-permute-start(f32[1024,256]{1,0:T(8,128)} %slice_convert_fusion), channel_id=1, source_target_pairs={{0,4},{4,0},{8,12},{12,8},{16,20},{20,16},{24,28},{28,24}} | collective-permute-start | bytes 3145736 | tf_op jit(solution)/shard_map/ppermute | solution.py:336
  3.7 33.2 %collective-permute-start = (f32[1024,256]{1,0:T(8,128)}, f32[1024,256]{1,0:T(8,128)S(1)}, u32[]{:S(2)}, u32[]{:S(2)}) collective-permute-start(f32[1024,256]{1,0:T(8,128)} %slice_convert_fusion), channel_id=1, source_target_pairs={{0,2},{4,6},{8,10},{12,14},{16,18},{20,22},{24,26},{28,30}} | collective-permute-start | bytes 3145736 | tf_op jit(solution)/shard_map/ppermute | solution.py:336
  6.4 13.1 %all-to-all-start = ((f32[8,72,128]{2,1,0:T(8,128)}), f32[8,72,128]{2,1,0:T(8,128)S(1)}, u32[]{:S(2)}, u32[]{:S(2)}) async-start(f32[8,72,128]{2,1,0:T(8,128)} %bitcast.2), calls=%async_computation | async-start | bytes 589824 | tf_op jit(solution)/shard_map/all_to_all | solution.py:352
  13.4 14.9 %collective-permute-start.14 = (f32[512,256]{1,0:T(8,128)}, f32[512,256]{1,0:T(8,128)S(1)}, u32[]{:S(2)}, u32[]{:S(2)}) collective-permute-start(f32[512,256]{1,0:T(8,128)} %slice_convert_fusion.1), channel_id=1, source_target_pairs={{0,2},{4,6},{8,10},{12,14},{16,18},{20,22},{24,26},{28,30}} | collective-permute-start | bytes 1572872 | tf_op jit(solution)/shard_map/ppermute | solution.py:336
  23.1 13.8 %copy-start.11 = (f32[2,136,128]{2,1,0:T(8,128)}, f32[2,136,128]{2,1,0:T(8,128)S(1)}, u32[]{:S(2)}) copy-start(f32[2,136,128]{2,1,0:T(8,128)S(1)} %get-tuple-element.16.refs_0_) | copy-start | bytes 417796
  23.1 7.8 %collective-permute-start.6 = (f32[2,136,128]{2,1,0:T(8,128)S(1)}, f32[2,136,128]{2,1,0:T(8,128)S(1)}, u32[]{:S(2)}, u32[]{:S(2)}) collective-permute-start(f32[2,136,128]{2,1,0:T(8,128)S(1)} %get-tuple-element.16.refs_0_), channel_id=1, source_target_pairs={{0,2},{1,3},{2,0},{3,1},{4,6},{5,7},{6,4},{7,5},{8,10},{9,11},{10,... | collective-permute-start | bytes 417800 | tf_op jit(solution)/shard_map/ppermute | solution.py:336
  27.1 6.4 %collective-permute-start.7 = (f32[2,136,128]{2,1,0:T(8,128)S(1)}, f32[2,136,128]{2,1,0:T(8,128)S(1)}, u32[]{:S(2)}, u32[]{:S(2)}) collective-permute-start(f32[2,136,128]{2,1,0:T(8,128)S(1)} %get-tuple-element.16.refs_0_), channel_id=1, source_target_pairs={{0,4},{1,5},{2,6},{3,7},{4,0},{5,1},{6,2},{7,3},{8,12},{9,13},{10,... | collective-permute-start | bytes 417800 | tf_op jit(solution)/shard_map/ppermute | solution.py:336
  28.3 8.5 %copy-start.3 = (f32[512,256]{1,0:T(8,128)}, f32[512,256]{1,0:T(8,128)S(1)}, u32[]{:S(2)}) copy-start(f32[512,256]{1,0:T(8,128)S(1)} %collective-permute-done.14.from_x) | copy-start | bytes 1572868
  28.3 6.4 %collective-permute-start.8 = (f32[2,136,128]{2,1,0:T(8,128)S(1)}, f32[2,136,128]{2,1,0:T(8,128)S(1)}, u32[]{:S(2)}, u32[]{:S(2)}) collective-permute-start(f32[2,136,128]{2,1,0:T(8,128)S(1)} %get-tuple-element.16.refs_0_), channel_id=1, source_target_pairs={{0,8},{1,9},{2,10},{3,11},{4,12},{5,13},{6,14},{7,15},{8,0},{9,1},... | collective-permute-start | bytes 417800 | tf_op jit(solution)/shard_map/ppermute | solution.py:336
  30.9 17.8 %collective-permute-start.15 = (f32[512,256]{1,0:T(8,128)S(1)}, f32[512,256]{1,0:T(8,128)S(1)}, u32[]{:S(2)}, u32[]{:S(2)}) collective-permute-start(f32[512,256]{1,0:T(8,128)S(1)} %convert_select_fusion), channel_id=1, source_target_pairs={{0,1},{2,3},{4,5},{6,7},{8,9},{10,11},{12,13},{14,15},{16,17},{18,... | collective-permute-start | bytes 1572872 | tf_op jit(solution)/shard_map/ppermute | solution.py:336
  33.5 9.0 %collective-permute-start.9 = (f32[2,136,128]{2,1,0:T(8,128)S(1)}, f32[2,136,128]{2,1,0:T(8,128)S(1)}, u32[]{:S(2)}, u32[]{:S(2)}) collective-permute-start(f32[2,136,128]{2,1,0:T(8,128)S(1)} %collective-permute-done.7.refs_2_), channel_id=1, source_target_pairs={{0,2},{1,3},{2,0},{3,1},{4,6},{5,7},{6,4},{7,5},{8,10},{9,11},{10,... | collective-permute-start | bytes 417800 | tf_op jit(solution)/shard_map/ppermute | solution.py:336
  34.8 7.1 %copy-start.13 = (f32[2,136,128]{2,1,0:T(8,128)}, f32[2,136,128]{2,1,0:T(8,128)S(1)}, u32[]{:S(2)}) copy-start(f32[2,136,128]{2,1,0:T(8,128)S(1)} %collective-permute-done.8.refs_3_) | copy-start | bytes 417796
  34.8 7.7 %collective-permute-start.10 = (f32[2,136,128]{2,1,0:T(8,128)S(1)}, f32[2,136,128]{2,1,0:T(8,128)S(1)}, u32[]{:S(2)}, u32[]{:S(2)}) collective-permute-start(f32[2,136,128]{2,1,0:T(8,128)S(1)} %collective-permute-done.8.refs_3_), channel_id=1, source_target_pairs={{0,4},{1,5},{2,6},{3,7},{4,0},{5,1},{6,2},{7,3},{8,12},{9,13},{10,... | collective-permute-start | bytes 417800 | tf_op jit(solution)/shard_map/ppermute | solution.py:336
  35.6 1.3 %copy-start.1 = (f32[1024,256]{1,0:T(8,128)}, f32[1024,256]{1,0:T(8,128)S(1)}, u32[]{:S(2)}) copy-start(f32[1024,256]{1,0:T(8,128)S(1)} %collective-permute-done.1.from_y) | copy-start | bytes 3145732
  35.6 8.3 %collective-permute-start.11 = (f32[2,136,128]{2,1,0:T(8,128)S(1)}, f32[2,136,128]{2,1,0:T(8,128)S(1)}, u32[]{:S(2)}, u32[]{:S(2)}) collective-permute-start(f32[2,136,128]{2,1,0:T(8,128)S(1)} %collective-permute-done.6.refs_1_), channel_id=1, source_target_pairs={{0,8},{1,9},{2,10},{3,11},{4,12},{5,13},{6,14},{7,15},{8,0},{9,1},... | collective-permute-start | bytes 417800 | tf_op jit(solution)/shard_map/ppermute | solution.py:336
  36.8 1.2 %copy-start = (bf16[1024,512]{1,0:T(8,128)(2,1)S(1)}, bf16[1024,512]{1,0:T(8,128)(2,1)}, u32[]{:S(2)}) copy-start(bf16[1024,512]{1,0:T(8,128)(2,1)} %front.5) | copy-start | bytes 3145732
  39.1 18.3 %collective-permute-start.2 = (f32[1792,256]{1,0:T(8,128)S(1)}, f32[1792,256]{1,0:T(8,128)S(1)}, u32[]{:S(2)}, u32[]{:S(2)}) collective-permute-start(f32[1792,256]{1,0:T(8,128)S(1)} %pad_maximum_fusion), channel_id=1, source_target_pairs={{0,1},{2,3},{4,5},{6,7},{8,9},{10,11},{12,13},{14,15},{16,17},{18,... | collective-permute-start | bytes 5505032 | tf_op jit(solution)/shard_map/ppermute | solution.py:336
  41.8 6.8 %copy-start.4 = (f32[512,256]{1,0:T(8,128)S(1)}, f32[512,256]{1,0:T(8,128)}, u32[]{:S(2)}) copy-start(f32[512,256]{1,0:T(8,128)} %copy-done.3) | copy-start | bytes 1572868
  41.8 6.8 %copy-start.6 = (bf16[512,512]{1,0:T(8,128)(2,1)S(1)}, bf16[512,512]{1,0:T(8,128)(2,1)}, u32[]{:S(2)}) copy-start(bf16[512,512]{1,0:T(8,128)(2,1)} %front.4) | copy-start | bytes 1572868
  42.5 7.0 %copy-start.17 = (f32[2,136,128]{2,1,0:T(8,128)}, f32[2,136,128]{2,1,0:T(8,128)S(1)}, u32[]{:S(2)}) copy-start(f32[2,136,128]{2,1,0:T(8,128)S(1)} %collective-permute-done.10.refs_5_) | copy-start | bytes 417796
  42.5 9.3 %collective-permute-start.12 = (f32[2,136,128]{2,1,0:T(8,128)S(1)}, f32[2,136,128]{2,1,0:T(8,128)S(1)}, u32[]{:S(2)}, u32[]{:S(2)}) collective-permute-start(f32[2,136,128]{2,1,0:T(8,128)S(1)} %collective-permute-done.10.refs_5_), channel_id=1, source_target_pairs={{0,2},{1,3},{2,0},{3,1},{4,6},{5,7},{6,4},{7,5},{8,10},{9,11},{10,... | collective-permute-start | bytes 417800 | tf_op jit(solution)/shard_map/ppermute | solution.py:336
  42.5 2.2 %copy-start.15 = (f32[2,136,128]{2,1,0:T(8,128)}, f32[2,136,128]{2,1,0:T(8,128)S(1)}, u32[]{:S(2)}) copy-start(f32[2,136,128]{2,1,0:T(8,128)S(1)} %collective-permute-done.9.refs_4_) | copy-start | bytes 417796
  44.7 12.7 %copy-start.2 = (f32[1024,256]{1,0:T(8,128)S(1)}, f32[1024,256]{1,0:T(8,128)}, u32[]{:S(2)}) copy-start(f32[1024,256]{1,0:T(8,128)} %copy-done.1) | copy-start | bytes 3145732
  44.7 12.6 %collective-permute-start.3 = (f32[512,256]{1,0:T(8,128)S(1)}, f32[512,256]{1,0:T(8,128)S(1)}, u32[]{:S(2)}, u32[]{:S(2)}) collective-permute-start(f32[512,256]{1,0:T(8,128)S(1)} %slice.35), channel_id=1, source_target_pairs={{2,6},{6,2},{10,14},{14,10},{18,22},{22,18},{26,30},{30,26}} | collective-permute-start | bytes 1572872 | tf_op jit(solution)/shard_map/ppermute | solution.py:336
  47.9 9.4 %collective-permute-start.4 = (f32[512,256]{1,0:T(8,128)S(1)}, f32[512,256]{1,0:T(8,128)S(1)}, u32[]{:S(2)}, u32[]{:S(2)}) collective-permute-start(f32[512,256]{1,0:T(8,128)S(1)} %get-tuple-element.19), channel_id=1, source_target_pairs={{0,3},{4,7},{8,11},{12,15},{16,19},{20,23},{24,27},{28,31}} | collective-permute-start | bytes 1572872 | tf_op jit(solution)/shard_map/ppermute | solution.py:336
  50.4 15.6 %collective-permute-start.16 = (f32[512,256]{1,0:T(8,128)}, f32[512,256]{1,0:T(8,128)}, u32[]{:S(2)}, u32[]{:S(2)}) collective-permute-start(f32[512,256]{1,0:T(8,128)} %select_select_fusion), channel_id=1, source_target_pairs={{0,4},{1,5},{2,6},{3,7},{6,2},{9,13},{15,11},{16,20},{17,21},{18,2... | collective-permute-start | bytes 1572872 | tf_op jit(solution)/shard_map/ppermute | solution.py:336
  51.8 5.5 %copy-start.21 = (f32[2,136,128]{2,1,0:T(8,128)}, f32[2,136,128]{2,1,0:T(8,128)S(1)}, u32[]{:S(2)}) copy-start(f32[2,136,128]{2,1,0:T(8,128)S(1)} %collective-permute-done.12.refs_7_) | copy-start | bytes 417796
  52.6 53.3 %collective-permute-start.13 = (f32[8,2,136,128]{3,2,1,0:T(8,128)}, f32[8,2,136,128]{3,2,1,0:T(8,128)}, u32[]{:S(2)}, u32[]{:S(2)}) collective-permute-start(f32[8,2,136,128]{3,2,1,0:T(8,128)} %bitcast_dynamic-update-slice_fusion), channel_id=1, source_target_pairs={{0,1},{1,0},{2,3},{3,2},{4,5},{5,4},{6,7},{7,6},{8,9},{9,8},{10,11... | collective-permute-start | bytes 3342344 | tf_op jit(solution)/shard_map/ppermute | solution.py:336
  63.9 50.1 %collective-permute-start.5 = (f32[512,512]{1,0:T(8,128)}, f32[512,512]{1,0:T(8,128)}, u32[]{:S(2)}, u32[]{:S(2)}) collective-permute-start(f32[512,512]{1,0:T(8,128)} %get-tuple-element.15), channel_id=1, source_target_pairs={{0,8},{1,9},{2,10},{3,11},{4,12},{5,13},{6,14},{7,15},{8,0},{9,1},... | collective-permute-start | bytes 3145736 | tf_op jit(solution)/shard_map/ppermute | solution.py:336
  65.9 33.2 %copy-start.8 = (f32[512,256]{1,0:T(8,128)S(1)}, f32[512,256]{1,0:T(8,128)}, u32[]{:S(2)}) copy-start(f32[512,256]{1,0:T(8,128)} %copy-done.7) | copy-start | bytes 1572868
  67.1 32.0 %collective-permute-start.17 = (f32[512,256]{1,0:T(8,128)S(1)}, f32[512,256]{1,0:T(8,128)S(1)}, u32[]{:S(2)}, u32[]{:S(2)}) collective-permute-start(f32[512,256]{1,0:T(8,128)S(1)} %broadcast_select_fusion.1), channel_id=1, source_target_pairs={{0,8},{2,10},{4,12},{6,14},{9,1},{11,3},{13,5},{15,7},{16,24},{18,... | collective-permute-start | bytes 1572872 | tf_op jit(solution)/shard_map/ppermute | solution.py:336
  69.5 33.9 %copy-start.10 = (f32[1024,256]{1,0:T(8,128)S(1)}, f32[1024,256]{1,0:T(8,128)}, u32[]{:S(2)}) copy-start(f32[1024,256]{1,0:T(8,128)} %copy-done.9) | copy-start | bytes 3145732
  69.5 33.9 %copy-start.24 = (f32[512,256]{1,0:T(8,128)S(1)}, f32[512,256]{1,0:T(8,128)}, u32[]{:S(2)}) copy-start(f32[512,256]{1,0:T(8,128)} %copy-done.23) | copy-start | bytes 1572868
  69.5 29.6 %collective-permute-start.18 = (f32[256,256]{1,0:T(8,128)S(1)}, f32[256,256]{1,0:T(8,128)S(1)}, u32[]{:S(2)}, u32[]{:S(2)}) collective-permute-start(f32[256,256]{1,0:T(8,128)S(1)} %slice_select_fusion.1), channel_id=1, source_target_pairs={{1,9},{2,10},{3,11},{5,13},{6,14},{7,15},{17,25},{18,26},{19,27},{... | collective-permute-start | bytes 786440 | tf_op jit(solution)/shard_map/ppermute | solution.py:336
  103.4 2.5 %copy-start.12 = (f32[2,136,128]{2,1,0:T(8,128)S(1)}, f32[2,136,128]{2,1,0:T(8,128)}, u32[]{:S(2)}) copy-start(f32[2,136,128]{2,1,0:T(8,128)} %copy-done.11) | copy-start | bytes 417796
  103.4 2.5 %copy-start.14 = (f32[2,136,128]{2,1,0:T(8,128)S(1)}, f32[2,136,128]{2,1,0:T(8,128)}, u32[]{:S(2)}) copy-start(f32[2,136,128]{2,1,0:T(8,128)} %copy-done.13) | copy-start | bytes 417796
  103.4 2.5 %copy-start.16 = (f32[2,136,128]{2,1,0:T(8,128)S(1)}, f32[2,136,128]{2,1,0:T(8,128)}, u32[]{:S(2)}) copy-start(f32[2,136,128]{2,1,0:T(8,128)} %copy-done.15) | copy-start | bytes 417796
  103.4 2.5 %copy-start.18 = (f32[2,136,128]{2,1,0:T(8,128)S(1)}, f32[2,136,128]{2,1,0:T(8,128)}, u32[]{:S(2)}) copy-start(f32[2,136,128]{2,1,0:T(8,128)} %copy-done.17) | copy-start | bytes 417796
  103.4 2.5 %copy-start.20 = (f32[2,136,128]{2,1,0:T(8,128)S(1)}, f32[2,136,128]{2,1,0:T(8,128)}, u32[]{:S(2)}) copy-start(f32[2,136,128]{2,1,0:T(8,128)} %copy-done.19) | copy-start | bytes 417796
  103.4 2.5 %copy-start.22 = (f32[2,136,128]{2,1,0:T(8,128)S(1)}, f32[2,136,128]{2,1,0:T(8,128)}, u32[]{:S(2)}) copy-start(f32[2,136,128]{2,1,0:T(8,128)} %copy-done.21) | copy-start | bytes 417796
  (9 other events, 7.7 us)

commit v2 on v1

--- a/solution.py
+++ b/solution.py
@@ -82,19 +82,52 @@
     out[...] = values + mm(tags, lanes, NT)
 
 
-def prepare_kernel(where, leaf_pivot, signs, perturb, leaf_map, level_map, inverse, links):
-    size = leaf_pivot.shape[1]
+def prepare_kernel(
+    where,
+    leaf_pivot,
+    leaf_coupling,
+    signs,
+    perturb,
+    leaf_map,
+    level_map,
+    inverse,
+    links,
+    coupling,
+    pivots,
+    done,
+):
+    copies = [
+        pltpu.make_async_copy(leaf_pivot, pivots, done.at[0]),
+        pltpu.make_async_copy(leaf_coupling, coupling, done.at[1]),
+    ]
+    for copy in copies:
+        copy.start()
+    leaves, size, _ = pivots.shape
     eye = iota((size, size), 0) == iota((size, size), 1)
     table = level_map[pl.ds(where[4], 1), :]
     rows = iota((16, NU), 0)
     digits = jnp.where(rows == 0, table // 256, jnp.where(rows == 1, table % 256, 0))
     digits = digits.astype(F32).astype(BF16)
     links[...] = jnp.zeros(links.shape, F32)
-    for leaf in range(leaf_pivot.shape[0]):
-        shift = signs[leaf : leaf + 1, :].astype(F32) * perturb[leaf : leaf + 1, :]
-        inverse[leaf] = newton_inverse(leaf_pivot[leaf] + jnp.where(eye, shift, 0.0))
+    for leaf in range(leaves):
         found = mm(digits, onehot(iota((NU, size), 0) == leaf_map[leaf : leaf + 1, :]))
         links[leaf : leaf + 1, :] = found[0:1, :] * 256.0 + found[1:2, :]
+    copies[0].wait()
+    for leaf in range(leaves):
+        shift = signs[leaf : leaf + 1, :].astype(F32) * perturb[leaf : leaf + 1, :]
+        inverse[leaf] = newton_inverse(pivots[leaf] + jnp.where(eye, shift, 0.0))
+    copies[1].wait()
+
+
+def places_kernel(where, level_map, out):
+    for index, quarter in enumerate((where[3], where[2])):
+        start = pl.multiple_of(quarter * QUARTER, QUARTER)
+        kept = start + iota((1, QUARTER), 1) >= KU
+        for other in range(2):
+            group = where[4] + other * (1 - 2 * where[1])
+            target = level_map[pl.ds(group, 1), pl.ds(start, QUARTER)] - start
+            target = jnp.where(kept, target, -1)
+            out[2 * other + index] = onehot(iota((QUARTER, QUARTER), 0) == target)
 
 
 def leaf_kernel(capacity, slots, cube_count, got, inverse, links, coupling, factor, sent):
@@ -152,7 +185,9 @@
     return jnp.concatenate([left, last], axis=1), keep
 
 
-def mid_kernel(where, front, from_x, from_y, from_core, pair, far, factor, left, cols, send, rows):
+def mid_kernel(
+    where, front, from_x, from_y, from_core, pair, far, factor, left, cols, send, rows
+):
     low, high, pos = where[0], where[1], where[2]
     is_low = low == 0
 
@@ -162,7 +197,7 @@
 
     @pl.when(pos == 2)
     def _():
-        rows[...] = from_x[...]
+        rows[...] = from_x[0:HALF, :]
 
     @pl.when(pos % 2 == 1)
     def _():
@@ -174,11 +209,11 @@
         pos == 0,
         from_y[0:QUARTER, :],
         jnp.where(
-            pos == 1, from_core[HALF : HALF + QUARTER, :], jnp.where(pos == 2, pair[...], far[...])
+            pos == 1, from_core[HALF + QUARTER : NU, :], jnp.where(pos == 2, pair[...], far[...])
         ),
     )
     col_rows = jnp.where(held, rows[pl.ds(own_cols, QUARTER), :], other_cols)
-    other_pivots = jnp.where(pos == 1, from_core[HALF + QUARTER :, :], other_cols[0:KU, :])
+    other_pivots = jnp.where(pos == 1, from_core[NU:, :], other_cols[0:KU, :])
     pivots = jnp.where(is_low, rows[0:KU, :], other_pivots)
     upper, below, lower = panel_parts(pivots)
     row_left, _ = panel_rows(rows[...], low * HALF, upper, below, lower)
@@ -193,82 +228,51 @@
     )
 
 
-def spread(values, level_map, group, row_quarter, col_quarter):
-    def places(quarter):
-        start = pl.multiple_of(quarter * QUARTER, QUARTER)
-        target = level_map[pl.ds(group, 1), pl.ds(start, QUARTER)] - start
-        from_pos = start + iota((1, QUARTER), 1)
-        target = jnp.where(from_pos >= KU, target, -1)
-        return onehot(iota((QUARTER, QUARTER), 0) == target)
-
-    row_place = places(row_quarter)
-    col_place = places(col_quarter)
+def spread(values, places, other):
     high, low = split(values)
+    row_place, col_place = places[2 * other], places[2 * other + 1]
     high, low = split(mm(row_place, high) + mm(row_place, low))
     return mm(high, col_place, NT) + mm(low, col_place, NT)
 
 
-def own_kernel(where, front, left, cols, level_map, base, out):
+def own_kernel(where, front, left, cols, places, out):
     start = pl.multiple_of(where[1] * QUARTER, QUARTER)
     block = front[pl.ds(start, QUARTER), :].astype(F32) - mm3(
         left[pl.ds(start, QUARTER), :], cols[...], NT
     )
-    out[...] = base[...] + spread(block, level_map, where[4], where[3], where[2])
-
-
-def other_kernel(where, block, level_map, base, out):
-    group = where[4] + 1 - 2 * where[1]
-    out[...] = base[...] + spread(block[...], level_map, group, where[3], where[2])
-
-
-def top_kernel(where, front, from_x, from_core, from_y, from_z, pivots_z, out, rows):
-    low, high, pos, quarter = where[0], where[1], where[2], where[3]
-
-    @pl.when(pos == 0)
-    def _():
-        rows[...] = front[:, 0:KU].astype(F32)
-
-    @pl.when(pos == 2)
-    def _():
-        rows[...] = from_x[...]
-
-    @pl.when(pos % 2 == 1)
-    def _():
-        rows[...] = from_core[...]
-
-    own = rows[...]
-    col_rows = jnp.where(
-        quarter == pos, own, jnp.where(high == pos % 2, from_y[...], from_z[...])
-    )
-    pivots = jnp.where(
-        pos == 0,
-        col_rows[0:KU, :],
-        jnp.where(
-            high == 1, pivots_z[...], jnp.where(low == 0, own[0:KU, :], from_y[0:KU, :])
-        ),
-    )
+    out[...] = spread(block, places, 0)
+
+
+def other_kernel(block, places, base, out):
+    out[...] = base[...] + spread(block[...], places, 1)
+
+
+def top_kernel(where, front, rows, here, from_y, base, out):
+    low, pos, quarter = where[0], where[2], where[3]
+    col_rows = jnp.where(low == pos // 2, here[0:QUARTER, :], from_y[0:QUARTER, :])
+    pivots = jnp.where(low == 0, here[QUARTER:, :], from_y[QUARTER:, :])
     upper, below, lower = panel_parts(pivots)
-    row_left, _ = panel_rows(own, quarter * QUARTER, upper, below, lower)
+    row_left, _ = panel_rows(rows[...], quarter * QUARTER, upper, below, lower)
     _, col_keep = panel_rows(col_rows, pos * QUARTER, upper, below, lower)
-    out[...] = front[...].astype(F32) - mm3(row_left, col_keep, NT)
+    out[...] = base[...] + front[...].astype(F32) - mm3(row_left, col_keep, NT)
 
 
 def gather_kernel(count, where, *refs):
-    own, swapped, base, out = refs[0:count], refs[count], refs[count + 1], refs[count + 2]
+    sources, base, out = refs[0:count], refs[count], refs[count + 1]
     row_first = where[3] * QUARTER
     col_first = where[2] * QUARTER
-    width = own[0].shape[2]
-    leaves = own[0].shape[0]
+    units = [source.at[unit] for source in sources for unit in range(source.shape[0])]
+    leaves, _, width = units[0].shape
     total = base[...]
-    for chip in range(count):
+    spots = iota((QUARTER, width), 0)
+    for first in range(0, len(units), 2):
         places, highs, lows = [], [], []
-        for source in (own[chip], swapped.at[chip]):
+        for unit in units[first : first + 2]:
             for leaf in range(leaves):
-                link = source[leaf, width : width + 1, :].astype(jnp.int32)
-                spots = iota((QUARTER, width), 0)
+                link = unit[leaf, width : width + 1, :].astype(jnp.int32)
                 places.append(onehot(spots == link - row_first))
                 cols = onehot(spots == link - col_first)
-                high, low = split(source[leaf, 0:width, :])
+                high, low = split(unit[leaf, 0:width, :])
                 high, low = split(mm(high, cols, NT) + mm(low, cols, NT))
                 highs.append(high)
                 lows.append(low)
@@ -279,26 +283,95 @@
     out[...] = total
 
 
-def call(body, outs, args, scalars=True, scratch=(), flops=10**8):
+def gather_kernel_of(count):
+    return functools.partial(gather_kernel, count)
+
+
+def stack_kernel(count, *refs):
+    first = 0
+    for part in refs[0:count]:
+        refs[count][first : first + part.shape[0]] = part[...]
+        first += part.shape[0]
+
+
+def stack(parts, after):
+    shape = (sum(part.shape[0] for part in parts),) + parts[0].shape[1:]
+    return call(functools.partial(stack_kernel, len(parts)), [shape], parts, after, scalars=False)
+
+
+def cast_kernel(mid_front, top_front, both, mid_cols, mid_part, top_part, done):
+    copies = [
+        pltpu.make_async_copy(front.at[:, pl.ds(0, KU)], part, done.at[index])
+        for index, (front, part) in enumerate(((mid_front, mid_part), (top_front, top_part)))
+    ]
+    for copy in copies:
+        copy.start()
+    copies[0].wait()
+    values = mid_part[...].astype(F32)
+    mid_cols[...] = values
+    both[0:HALF, :] = values
+    copies[1].wait()
+    both[HALF:, :] = top_part[...].astype(F32)
+
+
+def relay_kernel(where, both, from_x, from_y, core, far, pair):
+    core[0 : HALF + QUARTER, :] = jnp.where(where[2] == 0, both[...], from_x[...])
+    core[HALF + QUARTER : NU, :] = from_y[QUARTER:HALF, :]
+    core[NU:, :] = from_y[0:KU, :]
+    far[...] = jnp.where(where[0] == 0, from_y[QUARTER:HALF, :], from_y[0:QUARTER, :])
+    pair[...] = from_x[0:QUARTER, :]
+
+
+def choose_kernel(where, both, from_x, from_core, out):
+    pos = where[2]
+    held = jnp.where(pos == 0, both[HALF:, :], from_x[HALF:, :])
+    out[...] = jnp.where(pos % 2 == 0, held, from_core[HALF : HALF + QUARTER, :])
+
+
+def pair_kernel(where, top_rows, top_z, out):
+    first = where[1] == 0
+    even = jnp.where(first, top_rows[...], top_z[...])
+    odd = jnp.where(first, top_z[...], top_rows[...])
+    out[0:QUARTER, :] = jnp.where(where[2] % 2 == 0, even, odd)
+    out[QUARTER:, :] = even[0:KU, :]
+
+
+def slices_kernel(from_y, from_x, out_x, out_y):
+    out_x[...] = from_y[0:1]
+    out_y[...] = from_x[1:2]
+
+
+COST = pl.CostEstimate(flops=10**9, bytes_accessed=1000, transcendentals=0)
+FENCE = pl.CostEstimate(flops=10**11, bytes_accessed=1000, transcendentals=0)
+
+
+def call(body, outs, args, after=(), scalars=True, scratch=(), fence=False, far=(), kind=F32):
     specs = [pl.BlockSpec(memory_space=pltpu.VMEM) for _ in args]
     if scalars:
         specs[0] = pl.BlockSpec(memory_space=pltpu.SMEM)
-    shapes = [jax.ShapeDtypeStruct(shape, F32) for shape in outs]
-    moved = sum(4 * functools.reduce(lambda a, b: a * b, shape) for shape in outs)
+    for index in far:
+        specs[index] = pl.BlockSpec(memory_space=pltpu.HBM)
+    given = len(args)
+    skipped = len(after)
+
+    def kernel(*refs):
+        body(*refs[:given], *refs[given + skipped :])
+
+    shapes = [jax.ShapeDtypeStruct(shape, kind) for shape in outs]
     single = len(shapes) == 1
     return pl.pallas_call(
-        body,
+        kernel,
         out_shape=shapes[0] if single else shapes,
-        in_specs=specs,
+        in_specs=specs + [pl.BlockSpec(memory_space=pl.ANY) for _ in after],
         out_specs=(
             pl.BlockSpec(memory_space=pltpu.VMEM)
             if single
             else [pl.BlockSpec(memory_space=pltpu.VMEM) for _ in shapes]
         ),
         scratch_shapes=list(scratch),
-        compiler_params=pltpu.CompilerParams(vmem_limit_bytes=40 * 2**20),
-        cost_estimate=pl.CostEstimate(flops=flops, bytes_accessed=2 * moved, transcendentals=0),
-    )(*args)
+        compiler_params=pltpu.CompilerParams(vmem_limit_bytes=24 * 2**20),
+        cost_estimate=FENCE if fence else COST,
+    )(*args, *after)
 
 
 def local(
@@ -340,98 +413,95 @@
     capacity = max(2, 2 * block_count // cube_count)
     slots = -(-(capacity + 1) // 8) * 8
 
-    mid_cols = mid_front[:, 0:KU].astype(F32)
-    top_cols = top_front[:, 0:KU].astype(F32)
+    both, mid_cols = call(
+        cast_kernel,
+        [(HALF + QUARTER, KU), (HALF, KU)],
+        [mid_front, top_front],
+        scalars=False,
+        scratch=[
+            pltpu.VMEM((HALF, KU), BF16),
+            pltpu.VMEM((QUARTER, KU), BF16),
+            pltpu.SemaphoreType.DMA((2,)),
+        ],
+        far=(0, 1),
+    )
+    both_x = move(both, lambda y, z, f: (y, z, 2) if f == 0 else None)
+    mid_y = move(mid_cols, lambda y, z, f: (1 - y, z, 0) if f == 0 else None)
 
     packed = call(
         functools.partial(pack_kernel, capacity, slots, cube_count),
         [(cube_count * slots, width)],
         [blocks, kkt_owner.reshape(1, block_count), kkt_target.reshape(1, block_count)],
+        [both],
         scalars=False,
     )
     got = lax.all_to_all(
         packed.reshape(cube_count, slots, width), "cube", split_axis=0, concat_axis=0, tiled=True
     )
 
-    mid_x = move(mid_cols, lambda y, z, f: (y, z, 2) if f == 0 else None)
-    mid_y = move(mid_cols, lambda y, z, f: (1 - y, z, 0) if f == 0 else None)
-    mid_core = move(
-        jnp.concatenate(
-            [jnp.where(front == 0, mid_cols, mid_x), mid_y[QUARTER:HALF], mid_y[0:KU]], axis=0
-        ),
-        lambda y, z, f: (y, z, f + 1) if f % 2 == 0 else None,
-    )
-    mid_pair = move(mid_x[0:QUARTER], lambda y, z, f: (1 - y, z, 2) if f == 2 else None)
-    mid_far = move(
-        jnp.where(b0 == 0, mid_y[QUARTER:HALF], mid_y[0:QUARTER]),
-        lambda y, z, f: (y, z, 3) if f == 0 else None,
-    )
-
-    top_x = move(top_cols, lambda y, z, f: (y, z, 2) if f == 0 else None)
-    top_core = move(
-        jnp.where(front == 0, top_cols, top_x), lambda y, z, f: (y, z, f + 1) if f % 2 == 0 else None
-    )
-    top_rows = jnp.where(front == 0, top_cols, jnp.where(front == 2, top_x, top_core))
-
-    def down_y(y, z, f):
-        if y == 0:
-            return (1, z, f) if z == 0 or f == 1 else None
-        return (0, z, f) if (z, f) in ((0, 2), (1, 3)) else None
-
-    top_y = move(top_rows, down_y)
-    top_z = move(
-        jnp.where(quarter == front, top_rows, top_y),
-        lambda y, z, f: (y, 1 - z, f) if z == f % 2 else None,
-    )
-    top_pivots = move(
-        jnp.where(b0 == 0, top_rows[0:KU], top_y[0:KU]),
-        lambda y, z, f: (y, 1, f) if z == 0 and f > 0 else None,
-    )
-
+    places = call(
+        places_kernel, [(4, QUARTER, QUARTER)], [where, level_map], [packed], kind=BF16
+    )
     leaves = leaf_pivot.shape[0]
     size = leaf_pivot.shape[2]
-    inverse, links = call(
+    inverse, links, coupling = call(
         prepare_kernel,
-        [(leaves, size, size), (8, size)],
-        [where, leaf_pivot, pivot_signs, perturb, leaf_map, level_map],
-    )
+        [(leaves, size, size), (8, size), leaf_coupling.shape],
+        [where, leaf_pivot, leaf_coupling, pivot_signs, perturb, leaf_map, level_map],
+        [places],
+        scratch=[pltpu.VMEM(leaf_pivot.shape, F32), pltpu.SemaphoreType.DMA((2,))],
+        far=(1, 2),
+    )
+
     factor, sent = call(
         functools.partial(leaf_kernel, capacity, slots, cube_count),
         [leaf_coupling.shape, (leaves, size + 8, size)],
-        [got, inverse, links, leaf_coupling],
+        [got, inverse, links, coupling],
         scalars=False,
     )
-
-    k_x = move(sent, lambda y, z, f: (y, z, f ^ 2))
-    k_y = move(sent, lambda y, z, f: (1 - y, z, f))
+    sent = sent[None]
     k_z = move(sent, lambda y, z, f: (y, 1 - z, f))
-    k_xy = move(k_y, lambda y, z, f: (y, z, f ^ 2))
-    k_yz = move(k_z, lambda y, z, f: (1 - y, z, f))
-    k_xz = move(k_x, lambda y, z, f: (y, 1 - z, f))
-    k_xyz = move(k_yz, lambda y, z, f: (y, z, f ^ 2))
-    chips = [sent, k_x, k_y, k_z, k_xy, k_yz, k_xz, k_xyz]
-    swapped = move(jnp.stack(chips), lambda y, z, f: (y, z, f ^ 1))
+
+    to_core, to_far, to_pair = call(
+        relay_kernel,
+        [(NU + KU, KU), (QUARTER, KU), (QUARTER, KU)],
+        [where, both, both_x, mid_y],
+        [sent],
+    )
+    mid_pair = move(to_pair, lambda y, z, f: (1 - y, z, 2) if f == 2 else None)
+    mid_far = move(to_far, lambda y, z, f: (y, z, 3) if f == 0 else None)
+    mid_core = move(to_core, lambda y, z, f: (y, z, f + 1) if f % 2 == 0 else None)
+    k_own = stack([sent, k_z], [to_core])
+    k_x = move(k_own, lambda y, z, f: (y, z, f ^ 2))
+    k_y = move(k_own, lambda y, z, f: (1 - y, z, f))
+    top_rows = call(choose_kernel, [(QUARTER, KU)], [where, both, both_x, mid_core], [k_own])
+    top_z = move(top_rows, lambda y, z, f: (y, 1 - z, f))
 
     mid_factor, mid_left, mid_keep, mid_send = call(
         mid_kernel,
         [(HALF // front_count, KU), (HALF, KU), (QUARTER, KU), (QUARTER, QUARTER)],
-        [where, mid_front, mid_x, mid_y, mid_core, mid_pair, mid_far],
+        [where, mid_front, both_x, mid_y, mid_core, mid_pair, mid_far],
+        [top_rows],
         scratch=[pltpu.VMEM((HALF, KU), F32)],
     )
     mid_other = move(mid_send, lambda y, z, f: (y, 1 - z, f))
 
     square = [(QUARTER, QUARTER)]
-    upper = call(
-        top_kernel,
-        square,
-        [where, top_front, top_x, top_core, top_y, top_z, top_pivots],
-        scratch=[pltpu.VMEM((QUARTER, KU), F32)],
-    )
-    upper = call(own_kernel, square, [where, mid_front, mid_left, mid_keep, level_map, upper])
-    upper = call(
-        functools.partial(gather_kernel, len(chips)), square, [where, *chips, swapped, upper]
-    )
-    upper = call(other_kernel, square, [where, mid_other, level_map, upper])
+    to_x, to_y = call(
+        slices_kernel, [sent.shape, sent.shape], [k_y, k_x], [mid_send], scalars=False
+    )
+    k_xy = move(to_x, lambda y, z, f: (y, z, f ^ 2))
+    k_yx = move(to_y, lambda y, z, f: (1 - y, z, f))
+    here = call(pair_kernel, [(QUARTER + KU, KU)], [where, top_rows, top_z], [to_x])
+    top_y = move(here, lambda y, z, f: (1 - y, z, f))
+    upper = call(own_kernel, square, [where, mid_front, mid_left, mid_keep, places], [here])
+    upper = call(gather_kernel_of(3), square, [where, k_own, k_x, k_y, upper])
+    units = stack([k_own, k_x, k_y, k_xy, k_yx], [upper])
+    swapped = move(units, lambda y, z, f: (y, z, f ^ 1))
+    upper = call(gather_kernel_of(2), square, [where, k_xy, k_yx, upper], [units], fence=True)
+    upper = call(gather_kernel_of(1), square, [where, swapped, upper])
+    upper = call(top_kernel, square, [where, top_front, top_rows, here, top_y, upper])
+    upper = call(other_kernel, square, [mid_other, places, upper], scalars=False)
     return factor, mid_factor, upper
 
 

time: 118 us -> 83.9 us (0.71)
  the two profiles are of different devices: /device:TPU:14 before, /device:TPU:0 now
where the time goes in v2:
time: 83.9 us; the launch traced here: 83.3 us
  Pallas kernels  30.8 us (37%)
  starting transfers between devices  26.2 us (31%)
  waiting for transfers between devices  16.8 us (20%)
  local copies, waits for them, and re-layouts  8.56 us (10%)
  between operations  0.96 us (1%)
    pallas_call x18, Pallas kernels, call(): pl.pallas_call(kernel, out_shape=shapes[0] if single else shapes, in_spec...  30.8 us
    ppermute x14, starting transfers between devices, move(): return lax.ppermute(array, AXES, pairs)  21.4 us
    ppermute x14, waiting for transfers between devices, move(): return lax.ppermute(array, AXES, pairs)  13.1 us
    unnamed x42, local copies, waits for them, and re-layouts  8.48 us
    all_to_all x1, starting transfers between devices, local(): lax.all_to_all(packed.reshape(cube_count, slots, width), 'cube', split_ax...  4.89 us
    all_to_all x1, waiting for transfers between devices, local(): lax.all_to_all(packed.reshape(cube_count, slots, width), 'cube', split_ax...  3.73 us
  transfers between devices with their start and end apart: 15, of which 6 were waited for; matrix products, arithmetic and copies ran while one was open for 0% of the time, Pallas kernels for 31%

profile of v2, /device:TPU:0, one launch (start us, length us, event | category | flops | bytes accessed | tf_op | source)
XLA Modules:
  0.0 83.3 jit_solution(367166520137957881)
XLA Ops:
  0.6 1.2 %copy-done.2 = bf16[1024,512]{1,0:T(8,128)(2,1)S(1)} copy-done((bf16[1024,512]{1,0:T(8,128)(2,1)S(1)}, bf16[1024,512]{1,0:T(8,128)(2,1)}, u32[]{:S(2)}) %copy-start.2) | copy-done | bytes 1048600
  1.9 1.0 %copy-done.4 = bf16[512,512]{1,0:T(8,128)(2,1)S(1)} copy-done((bf16[512,512]{1,0:T(8,128)(2,1)S(1)}, bf16[512,512]{1,0:T(8,128)(2,1)}, u32[]{:S(2)}) %copy-start.4) | copy-done | bytes 524312
  2.9 1.2 %shard_map.130 = (f32[1536,256]{1,0:T(8,128)S(1)}, f32[1024,256]{1,0:T(8,128)}) custom-call(bf16[1024,512]{1,0:T(8,128)(2,1)S(1)} %copy-done.2, bf16[512,512]{1,0:T(8,128)(2,1)S(1)} %copy-done.4), custom_call_target="tpu_custom_call" | custom-call | flops 1000000000 | bytes 1000 | tf_op jit(solution)/shard_map/pallas_call | solution.py:362
  4.1 4.9 %collective-permute-start = (f32[1536,256]{1,0:T(8,128)S(1)}, f32[1536,256]{1,0:T(8,128)S(1)}, u32[]{:S(2)}, u32[]{:S(2)}) collective-permute-start(f32[1536,256]{1,0:T(8,128)S(1)} %get-tuple-element.19.refs_3_.refs_1_), channel_id=1, source_target_pairs={{0,2},{4,6},{8,10},{12,14},{16,18},{20,22},{24,26},{28,30}} | collective-permute-start | bytes 4718600 | tf_op jit(solution)/shard_map/ppermute | solution.py:409
  9.0 3.4 %collective-permute-start.1 = (f32[1024,256]{1,0:T(8,128)}, f32[1024,256]{1,0:T(8,128)}, u32[]{:S(2)}, u32[]{:S(2)}) collective-permute-start(f32[1024,256]{1,0:T(8,128)} %get-tuple-element.24), channel_id=1, source_target_pairs={{0,4},{4,0},{8,12},{12,8},{16,20},{20,16},{24,28},{28,24}} | collective-permute-start | bytes 3145736 | tf_op jit(solution)/shard_map/ppermute | solution.py:409
  12.5 0.6 shard_map.131.refs_2_
  13.2 0.7 copy-done.6
  13.9 4.9 %all-to-all-start = ((f32[8,72,128]{2,1,0:T(8,128)}), f32[8,72,128]{2,1,0:T(8,128)S(1)}, u32[]{:S(2)}, u32[]{:S(2)}) async-start(f32[8,72,128]{2,1,0:T(8,128)} %bitcast.9), calls=%async_computation | async-start | bytes 589824 | tf_op jit(solution)/shard_map/all_to_all | solution.py:438
  18.8 0.1 stack.23.refs_0_
  18.9 1.0 %copy-done.7 = f32[576,128]{1,0:T(8,128)S(1)} copy-done((f32[576,128]{1,0:T(8,128)S(1)}, f32[576,128]{1,0:T(8,128)}, u32[]{:S(2)}) %copy-start.7) | copy-done | bytes 294936
  19.8 0.0 copy-start.16
  19.9 0.9 %shard_map.132.refs_7_.refs_4_.refs_1_ = bf16[4,512,512]{2,1,0:T(8,128)(2,1)S(1)} custom-call(s32[5]{0:T(128)S(1)} %stack.23.refs_0_, s32[4,2048]{1,0:T(4,128)S(1)} %copy-done.11, f32[576,128]{1,0:T(8,128)S(1)} %copy-done.7), custom_call_target="tpu_custom_call" | custom-call | flops 1000000000 | bytes 1000 | tf_op jit(solution)/shard_map/pallas_call | solution.py:362
  20.9 1.8 %shard_map.133 = (f32[2,128,128]{2,1,0:T(8,128)S(1)}, f32[8,128]{1,0:T(8,128)S(1)}, f32[2,128,128]{2,1,0:T(8,128)S(1)}) custom-call(s32[5]{0:T(128)S(1)} %stack.23.refs_0_, f32[2,128,128]{2,1,0:T(8,128)S(1)} %copy-done.9, f32[2,128,128]{2,1,0:T(8,128)S(1)} %copy-done.10, s32[2,128]{1,0:T(2,128)S(1)} %copy-done.14, f32[2,128]{1,0:T(2,128)S(1)} %copy-done.15, ...), custom_call_target="tpu_custom_call" | custom-call | flops 1000000000 | bytes 1000 | tf_op jit(solution)/shard_map/pallas_call | solution.py:362
  22.7 1.4 %copy-done = bf16[4,512,512]{2,1,0:T(8,128)(2,1)} copy-done((bf16[4,512,512]{2,1,0:T(8,128)(2,1)}, bf16[4,512,512]{2,1,0:T(8,128)(2,1)S(1)}, u32[]{:S(2)}) %copy-start) | copy-done | bytes 2097176
  24.1 0.7 copy-done.17
  24.7 0.7 copy-done.19
  25.4 3.7 %all-to-all-done.refs_0_ = f32[8,72,128]{2,1,0:T(8,128)S(1)} async-done(((f32[8,72,128]{2,1,0:T(8,128)}), f32[8,72,128]{2,1,0:T(8,128)S(1)}, u32[]{:S(2)}, u32[]{:S(2)}) %all-to-all-start) | async-done | bytes 294944 | tf_op jit(solution)/shard_map/all_to_all | solution.py:438
  29.1 0.9 %copy-done.18 = f32[2,128,128]{2,1,0:T(8,128)S(1)} copy-done((f32[2,128,128]{2,1,0:T(8,128)S(1)}, f32[2,128,128]{2,1,0:T(8,128)}, u32[]{:S(2)}) %copy-start.18) | copy-done | bytes 131096
  30.0 0.9 %copy-done.20 = f32[2,128,128]{2,1,0:T(8,128)S(1)} copy-done((f32[2,128,128]{2,1,0:T(8,128)S(1)}, f32[2,128,128]{2,1,0:T(8,128)}, u32[]{:S(2)}) %copy-start.20) | copy-done | bytes 131096
  30.9 1.8 %shard_map.134 = (f32[2,128,128]{2,1,0:T(8,128)}, f32[2,136,128]{2,1,0:T(8,128)S(1)}) custom-call(f32[8,72,128]{2,1,0:T(8,128)S(1)} %all-to-all-done.refs_0_, f32[2,128,128]{2,1,0:T(8,128)S(1)} %copy-done.18, f32[8,128]{1,0:T(8,128)S(1)} %get-tuple-element.21.refs_2_, f32[2,128,128]{2,1,0:T(8,128)S(1)} %copy-done.20), custom_call_target="tpu_custom_call" | custom-call | flops 1000000000 | bytes 1000 | tf_op jit(solution)/shard_map/pallas_call | solution.py:362
  32.7 1.5 %shard_map.135 = (f32[2304,256]{1,0:T(8,128)S(1)}, f32[512,256]{1,0:T(8,128)S(1)}, f32[512,256]{1,0:T(8,128)S(1)}) custom-call(s32[5]{0:T(128)S(1)} %stack.23.refs_0_, f32[1536,256]{1,0:T(8,128)S(1)} %get-tuple-element.19.refs_3_.refs_1_, f32[1536,256]{1,0:T(8,128)S(1)} %collective-permute-done.refs_2_, f32[1024,256]{1,0:T(8,128)} %collective-permute-done.1.refs_3_, ...), custom_call_target="tpu_custom_call" | custom-call | flops 1000000000 | bytes 1000 | tf_op jit(solution)/shard_map/pallas_call | solution.py:362
  34.2 1.4 %collective-permute-start.2 = (f32[2304,256]{1,0:T(8,128)S(1)}, f32[2304,256]{1,0:T(8,128)S(1)}, u32[]{:S(2)}, u32[]{:S(2)}) collective-permute-start(f32[2304,256]{1,0:T(8,128)S(1)} %get-tuple-element.26.refs_2_), channel_id=1, source_target_pairs={{0,1},{2,3},{4,5},{6,7},{8,9},{10,11},{12,13},{14,15},{16,17},{18,... | collective-permute-start | bytes 7077896 | tf_op jit(solution)/shard_map/ppermute | solution.py:409
  35.7 1.6 %collective-permute-start.5 = (f32[1,2,136,128]{3,2,1,0:T(8,128)S(1)}, f32[1,2,136,128]{3,2,1,0:T(8,128)S(1)}, u32[]{:S(2)}, u32[]{:S(2)}) collective-permute-start(f32[1,2,136,128]{3,2,1,0:T(8,128)S(1)} %bitcast.11), channel_id=1, source_target_pairs={{0,8},{1,9},{2,10},{3,11},{4,12},{5,13},{6,14},{7,15},{8,0},{9,1},... | collective-permute-start | bytes 417800 | tf_op jit(solution)/shard_map/ppermute | solution.py:409
  37.3 0.7 collective-permute-start.3
  38.0 1.3 %collective-permute-start.4 = (f32[512,256]{1,0:T(8,128)S(1)}, f32[512,256]{1,0:T(8,128)S(1)}, u32[]{:S(2)}, u32[]{:S(2)}) collective-permute-start(f32[512,256]{1,0:T(8,128)S(1)} %get-tuple-element.28), channel_id=1, source_target_pairs={{0,3},{4,7},{8,11},{12,15},{16,19},{20,23},{24,27},{28,31}} | collective-permute-start | bytes 1572872 | tf_op jit(solution)/shard_map/ppermute | solution.py:409
  39.3 1.5 %collective-permute-done.5.refs_1_ = f32[1,2,136,128]{3,2,1,0:T(8,128)S(1)} collective-permute-done((f32[1,2,136,128]{3,2,1,0:T(8,128)S(1)}, f32[1,2,136,128]{3,2,1,0:T(8,128)S(1)}, u32[]{:S(2)}, u32[]{:S(2)}) %collective-permute-start.5) | collective-permute-done | bytes 139296 | tf_op jit(solution)/shard_map/ppermute | solution.py:409
  40.8 0.0 copy-start.3
  40.8 0.6 shard_map.137.refs_7_.refs_1_.refs_2_
  41.5 1.6 %collective-permute-start.7 = (f32[512,256]{1,0:T(8,128)S(1)}, f32[512,256]{1,0:T(8,128)S(1)}, u32[]{:S(2)}, u32[]{:S(2)}) collective-permute-start(f32[512,256]{1,0:T(8,128)S(1)} %shard_map.137.refs_7_.refs_1_.refs_2_), channel_id=1, source_target_pairs={{0,8},{1,9},{2,10},{3,11},{4,12},{5,13},{6,14},{7,15},{8,0},{9,1},... | collective-permute-start | bytes 1572872 | tf_op jit(solution)/shard_map/ppermute | solution.py:409
  43.1 1.5 %collective-permute-start.8 = (f32[2,2,136,128]{3,2,1,0:T(8,128)S(1)}, f32[2,2,136,128]{3,2,1,0:T(8,128)S(1)}, u32[]{:S(2)}, u32[]{:S(2)}) collective-permute-start(f32[2,2,136,128]{3,2,1,0:T(8,128)S(1)} %shard_map.136.refs_4_.refs_1_.refs_0_), channel_id=1, source_target_pairs={{0,4},{1,5},{2,6},{3,7},{4,0},{5,1},{6,2},{7,3},{8,12},{9,13},{10,... | collective-permute-start | bytes 835592 | tf_op jit(solution)/shard_map/ppermute | solution.py:409
  44.6 3.6 %collective-permute-done.4.refs_6_ = f32[512,256]{1,0:T(8,128)S(1)} collective-permute-done((f32[512,256]{1,0:T(8,128)S(1)}, f32[512,256]{1,0:T(8,128)S(1)}, u32[]{:S(2)}, u32[]{:S(2)}) %collective-permute-start.4) | collective-permute-done | bytes 524320 | tf_op jit(solution)/shard_map/ppermute | solution.py:409
  48.2 4.7 %shard_map.138 = (f32[256,256]{1,0:T(8,128)}, f32[1024,256]{1,0:T(8,128)S(1)}, f32[512,256]{1,0:T(8,128)S(1)}, f32[512,512]{1,0:T(8,128)S(1)}) custom-call(s32[5]{0:T(128)S(1)} %stack.23.refs_0_, bf16[1024,512]{1,0:T(8,128)(2,1)S(1)} %copy-done.3, f32[1536,256]{1,0:T(8,128)S(1)} %collective-permute-done.refs_2_, f32[1024,256]{1,0:T(8,128)} %collective-permute-done.1.refs_3_, ...), custom_call_target="tpu_custom_call" | custom-call | flops 1000000000 | bytes 1000 | tf_op jit(solution)/shard_map/pallas_call | solution.py:362
  52.9 0.4 collective-permute-start.6
  53.4 1.1 %collective-permute-start.11 = (f32[1,2,136,128]{3,2,1,0:T(8,128)S(1)}, f32[1,2,136,128]{3,2,1,0:T(8,128)S(1)}, u32[]{:S(2)}, u32[]{:S(2)}) collective-permute-start(f32[1,2,136,128]{3,2,1,0:T(8,128)S(1)} %get-tuple-element.31.refs_3_), channel_id=1, source_target_pairs={{0,2},{1,3},{2,0},{3,1},{4,6},{5,7},{6,4},{7,5},{8,10},{9,11},{10,... | collective-permute-start | bytes 417800 | tf_op jit(solution)/shard_map/ppermute | solution.py:409
  54.5 1.5 %collective-permute-start.12 = (f32[1,2,136,128]{3,2,1,0:T(8,128)S(1)}, f32[1,2,136,128]{3,2,1,0:T(8,128)S(1)}, u32[]{:S(2)}, u32[]{:S(2)}) collective-permute-start(f32[1,2,136,128]{3,2,1,0:T(8,128)S(1)} %get-tuple-element.32), channel_id=1, source_target_pairs={{0,4},{1,5},{2,6},{3,7},{4,0},{5,1},{6,2},{7,3},{8,12},{9,13},{10,... | collective-permute-start | bytes 417800 | tf_op jit(solution)/shard_map/ppermute | solution.py:409
  56.0 0.3 collective-permute-done.7.refs_2_
  56.4 0.6 shard_map.140.refs_5_.refs_3_
  57.0 1.6 %collective-permute-start.10 = (f32[768,256]{1,0:T(8,128)S(1)}, f32[768,256]{1,0:T(8,128)S(1)}, u32[]{:S(2)}, u32[]{:S(2)}) collective-permute-start(f32[768,256]{1,0:T(8,128)S(1)} %shard_map.140.refs_5_.refs_3_), channel_id=1, source_target_pairs={{0,4},{1,5},{2,6},{3,7},{4,0},{5,1},{6,2},{7,3},{8,12},{9,13},{10,... | collective-permute-start | bytes 2359304 | tf_op jit(solution)/shard_map/ppermute | solution.py:409
  58.6 2.3 %shard_map.141.refs_4_ = f32[512,512]{1,0:T(8,128)S(1)} custom-call(s32[5]{0:T(128)S(1)} %stack.23.refs_0_, bf16[1024,512]{1,0:T(8,128)(2,1)S(1)} %copy-done.3, f32[1024,256]{1,0:T(8,128)S(1)} %get-tuple-element.33.refs_2_, f32[512,256]{1,0:T(8,128)S(1)} %get-tuple-element.34.refs_3_, bf16[4,512,512]{2,1,0:T(8,128)(2,1)S(1)} %copy-done.1, ...), custom_call_target="tpu_custom_call" | custom-call | flops 1000000000 | bytes 1000 | tf_op jit(solution)/shard_map/pallas_call | solution.py:362
  60.9 3.2 %shard_map.142.refs_5_.refs_3_ = f32[512,512]{1,0:T(8,128)S(1)} custom-call(s32[5]{0:T(128)S(1)} %stack.23.refs_0_, f32[2,2,136,128]{3,2,1,0:T(8,128)S(1)} %shard_map.136.refs_4_.refs_1_.refs_0_, f32[2,2,136,128]{3,2,1,0:T(8,128)S(1)} %collective-permute-done.9.refs_1_.refs_2_, f32[2,2,136,128]{3,2,1,0:T(8,128)S(1)} %collective-permute-done.8.refs_0_.refs_3_.refs_2_, ...), custom_call_target="tpu_custom_call" | custom-call | flops 1000000000 | bytes 1000 | tf_op jit(solution)/shard_map/pallas_call | solution.py:362
  64.2 0.1 shard_map.143.refs_4_
  64.2 0.1 collective-permute-start.13
  64.3 1.5 %shard_map.144.refs_2_ = f32[512,512]{1,0:T(8,128)S(1)} custom-call(s32[5]{0:T(128)S(1)} %stack.23.refs_0_, f32[1,2,136,128]{3,2,1,0:T(8,128)S(1)} %collective-permute-done.11.refs_3_.refs_1_, f32[1,2,136,128]{3,2,1,0:T(8,128)S(1)} %collective-permute-done.12.refs_4_.refs_2_, f32[512,512]{1,0:T(8,128)S(1)} %shard_map.142.refs_5_.refs_3_, ...), custom_call_target="tpu_custom_call" | custom-call | flops 99999997952 | bytes 1000 | tf_op jit(solution)/shard_map/pallas_call | solution.py:362
  65.9 1.2 %collective-permute-done.13.refs_1_ = f32[8,2,136,128]{3,2,1,0:T(8,128)S(1)} collective-permute-done((f32[8,2,136,128]{3,2,1,0:T(8,128)S(1)}, f32[8,2,136,128]{3,2,1,0:T(8,128)S(1)}, u32[]{:S(2)}, u32[]{:S(2)}) %collective-permute-start.13) | collective-permute-done | bytes 1114144 | tf_op jit(solution)/shard_map/ppermute | solution.py:409
  67.1 4.0 %shard_map.145.refs_5_ = f32[512,512]{1,0:T(8,128)S(1)} custom-call(s32[5]{0:T(128)S(1)} %stack.23.refs_0_, f32[8,2,136,128]{3,2,1,0:T(8,128)S(1)} %collective-permute-done.13.refs_1_, f32[512,512]{1,0:T(8,128)S(1)} %shard_map.144.refs_2_), custom_call_target="tpu_custom_call" | custom-call | flops 1000000000 | bytes 1000 | tf_op jit(solution)/shard_map/pallas_call | solution.py:362
  71.1 6.4 %collective-permute-done.10.refs_4_ = f32[768,256]{1,0:T(8,128)S(1)} collective-permute-done((f32[768,256]{1,0:T(8,128)S(1)}, f32[768,256]{1,0:T(8,128)S(1)}, u32[]{:S(2)}, u32[]{:S(2)}) %collective-permute-start.10) | collective-permute-done | bytes 786464 | tf_op jit(solution)/shard_map/ppermute | solution.py:409
  77.5 3.5 %shard_map.146.refs_2_ = f32[512,512]{1,0:T(8,128)S(1)} custom-call(s32[5]{0:T(128)S(1)} %stack.23.refs_0_, bf16[512,512]{1,0:T(8,128)(2,1)S(1)} %copy-done.5, f32[512,256]{1,0:T(8,128)S(1)} %shard_map.137.refs_7_.refs_1_.refs_2_, f32[768,256]{1,0:T(8,128)S(1)} %shard_map.140.refs_5_.refs_3_, f32[768,256]{1,0:T(8,128)S(1)} %collective-permute-done.10.refs_4_, ...), custom_call_target="tpu_custom_call" | custom-call | flops 1000000000 | bytes 1000 | tf_op jit(solution)/shard_map/pallas_call | solution.py:362
  81.1 2.2 %shard_map.147 = f32[512,512]{1,0:T(8,128)} custom-call(f32[512,512]{1,0:T(8,128)S(1)} %collective-permute-done.6.refs_0_, bf16[4,512,512]{2,1,0:T(8,128)(2,1)S(1)} %copy-done.1, f32[512,512]{1,0:T(8,128)S(1)} %shard_map.146.refs_2_), custom_call_target="tpu_custom_call" | custom-call | flops 1000000000 | bytes 1000 | tf_op jit(solution)/shard_map/pallas_call | solution.py:362
  (43 shorter events, 0.1 us)
Async XLA Ops:
  0.6 1.2 %copy-start.2 = (bf16[1024,512]{1,0:T(8,128)(2,1)S(1)}, bf16[1024,512]{1,0:T(8,128)(2,1)}, u32[]{:S(2)}) copy-start(bf16[1024,512]{1,0:T(8,128)(2,1)} %refs_1_.10) | copy-start | bytes 3145732
  1.9 1.0 %copy-start.4 = (bf16[512,512]{1,0:T(8,128)(2,1)S(1)}, bf16[512,512]{1,0:T(8,128)(2,1)}, u32[]{:S(2)}) copy-start(bf16[512,512]{1,0:T(8,128)(2,1)} %refs_1_.11) | copy-start | bytes 1572868
  2.9 9.6 %copy-start.8 = (f32[1,256,128]{2,1,0:T(8,128)S(1)}, f32[1,256,128]{2,1,0:T(8,128)}, u32[]{:S(2)}) copy-start(f32[1,256,128]{2,1,0:T(8,128)} %param.11) | copy-start | bytes 393220
  2.9 9.6 %copy-start.12 = (s32[1,256,1]{1,2,0:T(1,128)S(1)}, s32[1,256,1]{1,2,0:T(1,128)}, u32[]{:S(2)}) copy-start(s32[1,256,1]{1,2,0:T(1,128)} %param.12) | copy-start | bytes 3076
  2.9 9.6 %copy-start.13 = (s32[1,256]{1,0:T(1,128)S(1)}, s32[1,256]{1,0:T(1,128)}, u32[]{:S(2)}) copy-start(s32[1,256]{1,0:T(1,128)} %refs_2_.2) | copy-start | bytes 3076
  4.1 28.6 %collective-permute-start = (f32[1536,256]{1,0:T(8,128)S(1)}, f32[1536,256]{1,0:T(8,128)S(1)}, u32[]{:S(2)}, u32[]{:S(2)}) collective-permute-start(f32[1536,256]{1,0:T(8,128)S(1)} %get-tuple-element.19.refs_3_.refs_1_), channel_id=1, source_target_pairs={{0,2},{4,6},{8,10},{12,14},{16,18},{20,22},{24,26},{28,30}} | collective-permute-start | bytes 4718600 | tf_op jit(solution)/shard_map/ppermute | solution.py:409
  9.0 23.6 %collective-permute-start.1 = (f32[1024,256]{1,0:T(8,128)}, f32[1024,256]{1,0:T(8,128)}, u32[]{:S(2)}, u32[]{:S(2)}) collective-permute-start(f32[1024,256]{1,0:T(8,128)} %get-tuple-element.24), channel_id=1, source_target_pairs={{0,4},{4,0},{8,12},{12,8},{16,20},{20,16},{24,28},{28,24}} | collective-permute-start | bytes 3145736 | tf_op jit(solution)/shard_map/ppermute | solution.py:409
  12.5 6.4 %copy-start.11 = (s32[4,2048]{1,0:T(4,128)S(1)}, s32[4,2048]{1,0:T(4,128)}, u32[]{:S(2)}) copy-start(s32[4,2048]{1,0:T(4,128)} %refs_6_.1) | copy-start | bytes 98308
  13.2 0.7 copy-start.6
  13.9 15.2 %all-to-all-start = ((f32[8,72,128]{2,1,0:T(8,128)}), f32[8,72,128]{2,1,0:T(8,128)S(1)}, u32[]{:S(2)}, u32[]{:S(2)}) async-start(f32[8,72,128]{2,1,0:T(8,128)} %bitcast.9), calls=%async_computation | async-start | bytes 589824 | tf_op jit(solution)/shard_map/all_to_all | solution.py:438
  18.9 1.0 %copy-start.7 = (f32[576,128]{1,0:T(8,128)S(1)}, f32[576,128]{1,0:T(8,128)}, u32[]{:S(2)}) copy-start(f32[576,128]{1,0:T(8,128)} %copy-done.6) | copy-start | bytes 884740
  19.8 1.0 %copy-start.9 = (f32[2,128,128]{2,1,0:T(8,128)S(1)}, f32[2,128,128]{2,1,0:T(8,128)}, u32[]{:S(2)}) copy-start(f32[2,128,128]{2,1,0:T(8,128)} %refs_1_.8) | copy-start | bytes 393220
  19.8 1.0 %copy-start.10 = (f32[2,128,128]{2,1,0:T(8,128)S(1)}, f32[2,128,128]{2,1,0:T(8,128)}, u32[]{:S(2)}) copy-start(f32[2,128,128]{2,1,0:T(8,128)} %refs_2_.3) | copy-start | bytes 393220
  19.8 1.0 %copy-start.14 = (s32[2,128]{1,0:T(2,128)S(1)}, s32[2,128]{1,0:T(2,128)}, u32[]{:S(2)}) copy-start(s32[2,128]{1,0:T(2,128)} %refs_3_.1) | copy-start | bytes 3076
  19.8 1.0 %copy-start.15 = (f32[2,128]{1,0:T(2,128)S(1)}, f32[2,128]{1,0:T(2,128)}, u32[]{:S(2)}) copy-start(f32[2,128]{1,0:T(2,128)} %refs_4_.1) | copy-start | bytes 3076
  19.8 1.0 %copy-start.16 = (s32[2,128]{1,0:T(2,128)S(1)}, s32[2,128]{1,0:T(2,128)}, u32[]{:S(2)}) copy-start(s32[2,128]{1,0:T(2,128)} %refs_5_.1) | copy-start | bytes 3076
  22.7 1.4 %copy-start = (bf16[4,512,512]{2,1,0:T(8,128)(2,1)}, bf16[4,512,512]{2,1,0:T(8,128)(2,1)S(1)}, u32[]{:S(2)}) copy-start(bf16[4,512,512]{2,1,0:T(8,128)(2,1)S(1)} %shard_map.132.refs_7_.refs_4_.refs_1_) | copy-start | bytes 6291460
  24.1 0.7 copy-start.17
  24.7 0.7 copy-start.19
  29.1 0.9 %copy-start.18 = (f32[2,128,128]{2,1,0:T(8,128)S(1)}, f32[2,128,128]{2,1,0:T(8,128)}, u32[]{:S(2)}) copy-start(f32[2,128,128]{2,1,0:T(8,128)} %copy-done.17) | copy-start | bytes 393220
  30.0 0.9 %copy-start.20 = (f32[2,128,128]{2,1,0:T(8,128)S(1)}, f32[2,128,128]{2,1,0:T(8,128)}, u32[]{:S(2)}) copy-start(f32[2,128,128]{2,1,0:T(8,128)} %copy-done.19) | copy-start | bytes 393220
  34.2 6.6 %collective-permute-start.2 = (f32[2304,256]{1,0:T(8,128)S(1)}, f32[2304,256]{1,0:T(8,128)S(1)}, u32[]{:S(2)}, u32[]{:S(2)}) collective-permute-start(f32[2304,256]{1,0:T(8,128)S(1)} %get-tuple-element.26.refs_2_), channel_id=1, source_target_pairs={{0,1},{2,3},{4,5},{6,7},{8,9},{10,11},{12,13},{14,15},{16,17},{18,... | collective-permute-start | bytes 7077896 | tf_op jit(solution)/shard_map/ppermute | solution.py:409
  35.7 5.1 %collective-permute-start.5 = (f32[1,2,136,128]{3,2,1,0:T(8,128)S(1)}, f32[1,2,136,128]{3,2,1,0:T(8,128)S(1)}, u32[]{:S(2)}, u32[]{:S(2)}) collective-permute-start(f32[1,2,136,128]{3,2,1,0:T(8,128)S(1)} %bitcast.11), channel_id=1, source_target_pairs={{0,8},{1,9},{2,10},{3,11},{4,12},{5,13},{6,14},{7,15},{8,0},{9,1},... | collective-permute-start | bytes 417800 | tf_op jit(solution)/shard_map/ppermute | solution.py:409
  37.3 7.3 %collective-permute-start.3 = (f32[512,256]{1,0:T(8,128)S(1)}, f32[512,256]{1,0:T(8,128)S(1)}, u32[]{:S(2)}, u32[]{:S(2)}) collective-permute-start(f32[512,256]{1,0:T(8,128)S(1)} %get-tuple-element.27), channel_id=1, source_target_pairs={{2,6},{6,2},{10,14},{14,10},{18,22},{22,18},{26,30},{30,26}} | collective-permute-start | bytes 1572872 | tf_op jit(solution)/shard_map/ppermute | solution.py:409
  38.0 10.2 %collective-permute-start.4 = (f32[512,256]{1,0:T(8,128)S(1)}, f32[512,256]{1,0:T(8,128)S(1)}, u32[]{:S(2)}, u32[]{:S(2)}) collective-permute-start(f32[512,256]{1,0:T(8,128)S(1)} %get-tuple-element.28), channel_id=1, source_target_pairs={{0,3},{4,7},{8,11},{12,15},{16,19},{20,23},{24,27},{28,31}} | collective-permute-start | bytes 1572872 | tf_op jit(solution)/shard_map/ppermute | solution.py:409
  40.8 7.4 %copy-start.3 = (bf16[1024,512]{1,0:T(8,128)(2,1)S(1)}, bf16[1024,512]{1,0:T(8,128)(2,1)}, u32[]{:S(2)}) copy-start(bf16[1024,512]{1,0:T(8,128)(2,1)} %refs_1_.10) | copy-start | bytes 3145732
  41.5 14.9 %collective-permute-start.7 = (f32[512,256]{1,0:T(8,128)S(1)}, f32[512,256]{1,0:T(8,128)S(1)}, u32[]{:S(2)}, u32[]{:S(2)}) collective-permute-start(f32[512,256]{1,0:T(8,128)S(1)} %shard_map.137.refs_7_.refs_1_.refs_2_), channel_id=1, source_target_pairs={{0,8},{1,9},{2,10},{3,11},{4,12},{5,13},{6,14},{7,15},{8,0},{9,1},... | collective-permute-start | bytes 1572872 | tf_op jit(solution)/shard_map/ppermute | solution.py:409
  43.1 10.3 %collective-permute-start.8 = (f32[2,2,136,128]{3,2,1,0:T(8,128)S(1)}, f32[2,2,136,128]{3,2,1,0:T(8,128)S(1)}, u32[]{:S(2)}, u32[]{:S(2)}) collective-permute-start(f32[2,2,136,128]{3,2,1,0:T(8,128)S(1)} %shard_map.136.refs_4_.refs_1_.refs_0_), channel_id=1, source_target_pairs={{0,4},{1,5},{2,6},{3,7},{4,0},{5,1},{6,2},{7,3},{8,12},{9,13},{10,... | collective-permute-start | bytes 835592 | tf_op jit(solution)/shard_map/ppermute | solution.py:409
  44.6 8.8 %collective-permute-start.9 = (f32[2,2,136,128]{3,2,1,0:T(8,128)S(1)}, f32[2,2,136,128]{3,2,1,0:T(8,128)S(1)}, u32[]{:S(2)}, u32[]{:S(2)}) collective-permute-start(f32[2,2,136,128]{3,2,1,0:T(8,128)S(1)} %shard_map.136.refs_4_.refs_1_.refs_0_), channel_id=1, source_target_pairs={{0,2},{1,3},{2,0},{3,1},{4,6},{5,7},{6,4},{7,5},{8,10},{9,11},{10,... | collective-permute-start | bytes 835592 | tf_op jit(solution)/shard_map/ppermute | solution.py:409
  52.9 28.1 %collective-permute-start.6 = (f32[512,512]{1,0:T(8,128)S(1)}, f32[512,512]{1,0:T(8,128)S(1)}, u32[]{:S(2)}, u32[]{:S(2)}) collective-permute-start(f32[512,512]{1,0:T(8,128)S(1)} %get-tuple-element.30.refs_2_), channel_id=1, source_target_pairs={{0,8},{1,9},{2,10},{3,11},{4,12},{5,13},{6,14},{7,15},{8,0},{9,1},... | collective-permute-start | bytes 3145736 | tf_op jit(solution)/shard_map/ppermute | solution.py:409
  53.4 10.7 %collective-permute-start.11 = (f32[1,2,136,128]{3,2,1,0:T(8,128)S(1)}, f32[1,2,136,128]{3,2,1,0:T(8,128)S(1)}, u32[]{:S(2)}, u32[]{:S(2)}) collective-permute-start(f32[1,2,136,128]{3,2,1,0:T(8,128)S(1)} %get-tuple-element.31.refs_3_), channel_id=1, source_target_pairs={{0,2},{1,3},{2,0},{3,1},{4,6},{5,7},{6,4},{7,5},{8,10},{9,11},{10,... | collective-permute-start | bytes 417800 | tf_op jit(solution)/shard_map/ppermute | solution.py:409
  54.5 4.1 %copy-start.1 = (bf16[4,512,512]{2,1,0:T(8,128)(2,1)S(1)}, bf16[4,512,512]{2,1,0:T(8,128)(2,1)}, u32[]{:S(2)}) copy-start(bf16[4,512,512]{2,1,0:T(8,128)(2,1)} %copy-done) | copy-start | bytes 6291460
  54.5 9.6 %collective-permute-start.12 = (f32[1,2,136,128]{3,2,1,0:T(8,128)S(1)}, f32[1,2,136,128]{3,2,1,0:T(8,128)S(1)}, u32[]{:S(2)}, u32[]{:S(2)}) collective-permute-start(f32[1,2,136,128]{3,2,1,0:T(8,128)S(1)} %get-tuple-element.32), channel_id=1, source_target_pairs={{0,4},{1,5},{2,6},{3,7},{4,0},{5,1},{6,2},{7,3},{8,12},{9,13},{10,... | collective-permute-start | bytes 417800 | tf_op jit(solution)/shard_map/ppermute | solution.py:409
  57.0 20.5 %collective-permute-start.10 = (f32[768,256]{1,0:T(8,128)S(1)}, f32[768,256]{1,0:T(8,128)S(1)}, u32[]{:S(2)}, u32[]{:S(2)}) collective-permute-start(f32[768,256]{1,0:T(8,128)S(1)} %shard_map.140.refs_5_.refs_3_), channel_id=1, source_target_pairs={{0,4},{1,5},{2,6},{3,7},{4,0},{5,1},{6,2},{7,3},{8,12},{9,13},{10,... | collective-permute-start | bytes 2359304 | tf_op jit(solution)/shard_map/ppermute | solution.py:409
  64.2 2.8 %collective-permute-start.13 = (f32[8,2,136,128]{3,2,1,0:T(8,128)S(1)}, f32[8,2,136,128]{3,2,1,0:T(8,128)S(1)}, u32[]{:S(2)}, u32[]{:S(2)}) collective-permute-start(f32[8,2,136,128]{3,2,1,0:T(8,128)S(1)} %shard_map.143.refs_4_), channel_id=1, source_target_pairs={{0,1},{1,0},{2,3},{3,2},{4,5},{5,4},{6,7},{7,6},{8,9},{9,8},{10,11... | collective-permute-start | bytes 3342344 | tf_op jit(solution)/shard_map/ppermute | solution.py:409
  65.9 11.7 %copy-start.5 = (bf16[512,512]{1,0:T(8,128)(2,1)S(1)}, bf16[512,512]{1,0:T(8,128)(2,1)}, u32[]{:S(2)}) copy-start(bf16[512,512]{1,0:T(8,128)(2,1)} %refs_1_.11) | copy-start | bytes 1572868

commit v3 on v2

--- a/solution.py
+++ b/solution.py
@@ -13,7 +13,6 @@
 QUARTER = NU // 4
 HALF = NU // 2
 
-HIGHEST = lax.Precision.HIGHEST
 F32 = jnp.float32
 BF16 = jnp.bfloat16
 AXES = ("cube", "front")
@@ -25,10 +24,6 @@
     return lax.dot_general(a, b, dims, preferred_element_type=F32)
 
 
-def exact(a, b, dims=NN):
-    return lax.dot_general(a, b, dims, preferred_element_type=F32, precision=HIGHEST)
-
-
 def split(x):
     high = x.astype(BF16)
     return high, (x - high.astype(F32)).astype(BF16)
@@ -44,7 +39,22 @@
 def mm3(a, b, dims=NN):
     ah, al = split(a)
     bh, bl = split(b)
-    return mm(ah, bh, dims) + (mm(ah, bl, dims) + mm(al, bh, dims))
+    rows = dims[0][1][0]
+    return mm(
+        jnp.concatenate([ah, ah, al], axis=1), jnp.concatenate([bh, bl, bh], axis=rows), dims
+    )
+
+
+def pick_rows(places, values):
+    high, low = split(values)
+    return mm(jnp.concatenate([places, places], axis=1), jnp.concatenate([high, low], axis=0))
+
+
+def pick_cols(values, places):
+    high, low = split(values)
+    return mm(
+        jnp.concatenate([high, low], axis=1), jnp.concatenate([places, places], axis=1), NT
+    )
 
 
 def iota(shape, axis):
@@ -62,7 +72,7 @@
     row = 1.0 / jnp.sum(diagonal, axis=0, keepdims=True)
     col = 1.0 / jnp.sum(diagonal, axis=1, keepdims=True)
     current = jnp.where(eye, 2.0 * row, 0.0) - col * (block * row)
-    return 2.0 * current - exact(current, exact(block, current))
+    return 2.0 * current - mm3(current, mm3(block, current))
 
 
 def pack_kernel(capacity, slots, cube_count, blocks, owner, target, out):
@@ -157,7 +167,7 @@
         added = lax.fori_loop(0, cube_count, step, jnp.zeros((leaves * rows, width), F32))
     for leaf in range(leaves):
         rhs = coupling[leaf] + added[leaf * rows : (leaf + 1) * rows, :]
-        part = exact(rhs, inverse[leaf])
+        part = mm3(rhs, inverse[leaf])
         factor[leaf] = part
         sent[leaf, 0:rows, :] = -mm3(part, rhs, NT)
         sent[leaf, rows : rows + 8, :] = jnp.where(
@@ -165,12 +175,9 @@
         )
 
 
-def panel_parts(pivots):
-    upper = newton_inverse(pivots[0:PIV, 0:PIV])
-    below = pivots[PIV:KU, 0:PIV]
-    lower = newton_inverse(
-        pivots[PIV:KU, PIV:KU] - exact(exact(below, upper), below, NT)
-    )
+def panel_parts(first, below, last):
+    upper = newton_inverse(first)
+    lower = newton_inverse(last - mm3(mm3(below, upper), below, NT))
     return upper, below, lower
 
 
@@ -186,14 +193,13 @@
 
 
 def mid_kernel(
-    where, front, from_x, from_y, from_core, pair, far, factor, left, cols, send, rows
+    where, front, both, from_x, from_y, from_core, cross, left, cols, parts, send, rows
 ):
     low, high, pos = where[0], where[1], where[2]
-    is_low = low == 0
 
     @pl.when(pos == 0)
     def _():
-        rows[...] = front[:, 0:KU].astype(F32)
+        rows[...] = both[0:HALF, :]
 
     @pl.when(pos == 2)
     def _():
@@ -204,42 +210,49 @@
         rows[...] = from_core[0:HALF, :]
 
     own_cols = pl.multiple_of((pos % 2) * QUARTER, QUARTER)
-    held = (pos // 2) == low
     other_cols = jnp.where(
         pos == 0,
         from_y[0:QUARTER, :],
-        jnp.where(
-            pos == 1, from_core[HALF + QUARTER : NU, :], jnp.where(pos == 2, pair[...], far[...])
-        ),
-    )
-    col_rows = jnp.where(held, rows[pl.ds(own_cols, QUARTER), :], other_cols)
-    other_pivots = jnp.where(pos == 1, from_core[NU:, :], other_cols[0:KU, :])
-    pivots = jnp.where(is_low, rows[0:KU, :], other_pivots)
-    upper, below, lower = panel_parts(pivots)
-    row_left, _ = panel_rows(rows[...], low * HALF, upper, below, lower)
+        jnp.where(pos == 1, from_core[HALF : HALF + QUARTER, :], cross[...]),
+    )
+    col_rows = jnp.where(pos // 2 == low, rows[pl.ds(own_cols, QUARTER), :], other_cols)
+    other_pivots = jnp.where(pos == 1, from_core[HALF + QUARTER :, :], other_cols[0:KU, :])
+    pivots = jnp.where(low == 0, rows[0:KU, :], other_pivots)
+    upper, below, lower = panel_parts(
+        pivots[0:PIV, 0:PIV], pivots[PIV:KU, 0:PIV], pivots[PIV:KU, PIV:KU]
+    )
+    parts[0], parts[1], parts[2] = upper, below, lower
     _, col_keep = panel_rows(col_rows, pos * QUARTER, upper, below, lower)
+    cols[...] = col_keep
+    start = pl.multiple_of((1 - high) * QUARTER, QUARTER)
+    row_left, _ = panel_rows(
+        rows[pl.ds(start, QUARTER), :], low * HALF + start, upper, below, lower
+    )
     left[...] = row_left
-    cols[...] = col_keep
-    slab = HALF // 4
-    factor[...] = left[pl.ds(pl.multiple_of(pos * slab, slab), slab), :]
-    start = pl.multiple_of((1 - high) * QUARTER, QUARTER)
-    send[...] = front[pl.ds(start, QUARTER), :].astype(F32) - mm3(
-        left[pl.ds(start, QUARTER), :], col_keep, NT
-    )
+    send[...] = front[pl.ds(start, QUARTER), :].astype(F32) - mm3(row_left, col_keep, NT)
 
 
 def spread(values, places, other):
-    high, low = split(values)
     row_place, col_place = places[2 * other], places[2 * other + 1]
-    high, low = split(mm(row_place, high) + mm(row_place, low))
-    return mm(high, col_place, NT) + mm(low, col_place, NT)
-
-
-def own_kernel(where, front, left, cols, places, out):
-    start = pl.multiple_of(where[1] * QUARTER, QUARTER)
-    block = front[pl.ds(start, QUARTER), :].astype(F32) - mm3(
-        left[pl.ds(start, QUARTER), :], cols[...], NT
-    )
+    return pick_cols(pick_rows(row_place, values), col_place)
+
+
+def own_kernel(
+    where, front, both, from_x, from_core, left, cols, parts, places, factor, out, own
+):
+    low, high, pos = where[0], where[1], where[2]
+    start = pl.multiple_of(high * QUARTER, QUARTER)
+    here = pl.ds(start, QUARTER)
+    rows = jnp.where(
+        pos == 0, both[here, :], jnp.where(pos == 2, from_x[here, :], from_core[here, :])
+    )
+    row_left, _ = panel_rows(rows, low * HALF + start, parts[0], parts[1], parts[2])
+    own[...] = row_left
+    slab = factor.shape[0]
+    first = pos * slab
+    inner = pl.ds(pl.multiple_of(first % QUARTER, slab), slab)
+    factor[...] = jnp.where(first // QUARTER == high, own[inner, :], left[inner, :])
+    block = front[here, :].astype(F32) - mm3(row_left, cols[...], NT)
     out[...] = spread(block, places, 0)
 
 
@@ -251,34 +264,31 @@
     low, pos, quarter = where[0], where[2], where[3]
     col_rows = jnp.where(low == pos // 2, here[0:QUARTER, :], from_y[0:QUARTER, :])
     pivots = jnp.where(low == 0, here[QUARTER:, :], from_y[QUARTER:, :])
-    upper, below, lower = panel_parts(pivots)
+    last = jnp.concatenate([pivots[PIV:, 0:PIV], pivots[PIV:, PIV:KU]], axis=0)
+    upper, below, lower = panel_parts(pivots[0:PIV, 0:PIV], pivots[0:PIV, PIV:KU], last)
     row_left, _ = panel_rows(rows[...], quarter * QUARTER, upper, below, lower)
     _, col_keep = panel_rows(col_rows, pos * QUARTER, upper, below, lower)
     out[...] = base[...] + front[...].astype(F32) - mm3(row_left, col_keep, NT)
 
 
 def gather_kernel(count, where, *refs):
-    sources, base, out = refs[0:count], refs[count], refs[count + 1]
+    sources, out = refs[0:count], refs[-1]
     row_first = where[3] * QUARTER
     col_first = where[2] * QUARTER
     units = [source.at[unit] for source in sources for unit in range(source.shape[0])]
     leaves, _, width = units[0].shape
-    total = base[...]
+    total = refs[count][...] if len(refs) > count + 1 else jnp.zeros(out.shape, F32)
     spots = iota((QUARTER, width), 0)
     for first in range(0, len(units), 2):
-        places, highs, lows = [], [], []
+        row_places, blocks = [], []
         for unit in units[first : first + 2]:
             for leaf in range(leaves):
                 link = unit[leaf, width : width + 1, :].astype(jnp.int32)
-                places.append(onehot(spots == link - row_first))
-                cols = onehot(spots == link - col_first)
-                high, low = split(unit[leaf, 0:width, :])
-                high, low = split(mm(high, cols, NT) + mm(low, cols, NT))
-                highs.append(high)
-                lows.append(low)
-        place = jnp.concatenate(places, axis=1)
-        total = total + (
-            mm(place, jnp.concatenate(highs, axis=0)) + mm(place, jnp.concatenate(lows, axis=0))
+                row_places.append(onehot(spots == link - row_first))
+                col_places = onehot(spots == link - col_first)
+                blocks.append(pick_cols(unit[leaf, 0:width, :], col_places))
+        total = total + pick_rows(
+            jnp.concatenate(row_places, axis=1), jnp.concatenate(blocks, axis=0)
         )
     out[...] = total
 
@@ -314,35 +324,40 @@
     both[HALF:, :] = top_part[...].astype(F32)
 
 
-def relay_kernel(where, both, from_x, from_y, core, far, pair):
-    core[0 : HALF + QUARTER, :] = jnp.where(where[2] == 0, both[...], from_x[...])
-    core[HALF + QUARTER : NU, :] = from_y[QUARTER:HALF, :]
-    core[NU:, :] = from_y[0:KU, :]
-    far[...] = jnp.where(where[0] == 0, from_y[QUARTER:HALF, :], from_y[0:QUARTER, :])
-    pair[...] = from_x[0:QUARTER, :]
-
-
-def choose_kernel(where, both, from_x, from_core, out):
-    pos = where[2]
-    held = jnp.where(pos == 0, both[HALF:, :], from_x[HALF:, :])
-    out[...] = jnp.where(pos % 2 == 0, held, from_core[HALF : HALF + QUARTER, :])
-
-
-def pair_kernel(where, top_rows, top_z, out):
+def relay_kernel(where, both, from_x, from_y, core, cross):
+    here = where[2] == 0
+    core[0:HALF, :] = jnp.where(here, both[0:HALF, :], from_x[0:HALF, :])
+    core[HALF : HALF + QUARTER, :] = from_y[QUARTER:HALF, :]
+    core[HALF + QUARTER :, :] = from_y[0:KU, :]
+    far = jnp.where(where[0] == 0, from_y[QUARTER:HALF, :], from_y[0:QUARTER, :])
+    cross[...] = jnp.where(here, far, from_x[0:QUARTER, :])
+
+
+def choose_kernel(where, both, from_x, out):
+    out[...] = jnp.where(where[2] == 0, both[HALF:, :], from_x[HALF:, :])
+
+
+def pair_kernel(where, top_rows, top_z, pair):
     first = where[1] == 0
-    even = jnp.where(first, top_rows[...], top_z[...])
-    odd = jnp.where(first, top_z[...], top_rows[...])
-    out[0:QUARTER, :] = jnp.where(where[2] % 2 == 0, even, odd)
-    out[QUARTER:, :] = even[0:KU, :]
-
-
-def slices_kernel(from_y, from_x, out_x, out_y):
-    out_x[...] = from_y[0:1]
-    out_y[...] = from_x[1:2]
+    pair[0:QUARTER, :] = jnp.where(first, top_rows[...], top_z[...])
+    pair[QUARTER:, :] = jnp.where(first, top_z[...], top_rows[...])
+
+
+def here_kernel(where, pair, from_core, rows, out):
+    even = where[2] % 2 == 0
+    own = pl.multiple_of(where[1] * QUARTER, QUARTER)
+    rows[...] = jnp.where(even, pair[pl.ds(own, QUARTER), :], from_core[pl.ds(own, QUARTER), :])
+    out[0:QUARTER, :] = jnp.where(even, pair[0:QUARTER, :], from_core[QUARTER:, :])
+    half = PIV // 2
+    first = jnp.where(even, pair[0:KU, :], from_core[0:KU, :])
+    out[QUARTER : QUARTER + PIV, 0:PIV] = first[0:PIV, 0:PIV]
+    out[QUARTER : QUARTER + PIV, PIV:KU] = first[PIV:KU, 0:PIV]
+    out[QUARTER + PIV :, 0:PIV] = first[PIV : PIV + half, PIV:KU]
+    out[QUARTER + PIV :, PIV:KU] = first[PIV + half : KU, PIV:KU]
 
 
 COST = pl.CostEstimate(flops=10**9, bytes_accessed=1000, transcendentals=0)
-FENCE = pl.CostEstimate(flops=10**11, bytes_accessed=1000, transcendentals=0)
+FENCE = pl.CostEstimate(flops=3 * 10**10, bytes_accessed=1000, transcendentals=0)
 
 
 def call(body, outs, args, after=(), scalars=True, scratch=(), fence=False, far=(), kind=F32):
@@ -453,54 +468,67 @@
         far=(1, 2),
     )
 
+    top_rows = call(choose_kernel, [(QUARTER, KU)], [where, both, both_x], [inverse])
+    top_z = move(top_rows, lambda y, z, f: (y, 1 - z, f) if f % 2 == 0 else None)
+
+    to_core, to_cross = call(
+        relay_kernel,
+        [(HALF + QUARTER + KU, KU), (QUARTER, KU)],
+        [where, both, both_x, mid_y],
+        [top_rows, got],
+    )
+    mid_cross = move(to_cross, lambda y, z, f: {0: (y, z, 3), 2: (1 - y, z, 2)}.get(f))
+    mid_core = move(to_core, lambda y, z, f: (y, z, f + 1) if f % 2 == 0 else None)
+
     factor, sent = call(
         functools.partial(leaf_kernel, capacity, slots, cube_count),
         [leaf_coupling.shape, (leaves, size + 8, size)],
         [got, inverse, links, coupling],
+        [to_core],
         scalars=False,
     )
     sent = sent[None]
     k_z = move(sent, lambda y, z, f: (y, 1 - z, f))
-
-    to_core, to_far, to_pair = call(
-        relay_kernel,
-        [(NU + KU, KU), (QUARTER, KU), (QUARTER, KU)],
-        [where, both, both_x, mid_y],
+    mid_left, mid_keep, mid_parts, mid_send = call(
+        mid_kernel,
+        [(QUARTER, KU), (QUARTER, KU), (3, PIV, PIV), (QUARTER, QUARTER)],
+        [where, mid_front, both, both_x, mid_y, mid_core, mid_cross],
         [sent],
-    )
-    mid_pair = move(to_pair, lambda y, z, f: (1 - y, z, 2) if f == 2 else None)
-    mid_far = move(to_far, lambda y, z, f: (y, z, 3) if f == 0 else None)
-    mid_core = move(to_core, lambda y, z, f: (y, z, f + 1) if f % 2 == 0 else None)
-    k_own = stack([sent, k_z], [to_core])
+        scratch=[pltpu.VMEM((HALF, KU), F32)],
+        fence=True,
+    )
+    mid_other = move(mid_send, lambda y, z, f: (y, 1 - z, f))
+
+    square = [(QUARTER, QUARTER)]
+    k_own = stack([sent, k_z], [mid_send])
     k_x = move(k_own, lambda y, z, f: (y, z, f ^ 2))
     k_y = move(k_own, lambda y, z, f: (1 - y, z, f))
-    top_rows = call(choose_kernel, [(QUARTER, KU)], [where, both, both_x, mid_core], [k_own])
-    top_z = move(top_rows, lambda y, z, f: (y, 1 - z, f))
-
-    mid_factor, mid_left, mid_keep, mid_send = call(
-        mid_kernel,
-        [(HALF // front_count, KU), (HALF, KU), (QUARTER, KU), (QUARTER, QUARTER)],
-        [where, mid_front, both_x, mid_y, mid_core, mid_pair, mid_far],
-        [top_rows],
-        scratch=[pltpu.VMEM((HALF, KU), F32)],
-    )
-    mid_other = move(mid_send, lambda y, z, f: (y, 1 - z, f))
-
-    square = [(QUARTER, QUARTER)]
-    to_x, to_y = call(
-        slices_kernel, [sent.shape, sent.shape], [k_y, k_x], [mid_send], scalars=False
-    )
+    pair = call(pair_kernel, [(HALF, KU)], [where, top_rows, top_z], [k_own])
+    pair_core = move(pair, lambda y, z, f: (y, z, f ^ 1))
+    top_own, here = call(
+        here_kernel,
+        [(QUARTER, KU), (QUARTER + PIV + PIV // 2, KU)],
+        [where, pair, pair_core],
+    )
+    top_y = move(here, lambda y, z, f: (1 - y, z, f))
+    mid_factor, upper = call(
+        own_kernel,
+        [(HALF // front_count, KU), (QUARTER, QUARTER)],
+        [where, mid_front, both, both_x, mid_core, mid_left, mid_keep, mid_parts, places],
+        [here],
+        scratch=[pltpu.VMEM((QUARTER, KU), F32)],
+    )
+    to_x = stack([k_y], [upper])
     k_xy = move(to_x, lambda y, z, f: (y, z, f ^ 2))
-    k_yx = move(to_y, lambda y, z, f: (1 - y, z, f))
-    here = call(pair_kernel, [(QUARTER + KU, KU)], [where, top_rows, top_z], [to_x])
-    top_y = move(here, lambda y, z, f: (1 - y, z, f))
-    upper = call(own_kernel, square, [where, mid_front, mid_left, mid_keep, places], [here])
-    upper = call(gather_kernel_of(3), square, [where, k_own, k_x, k_y, upper])
-    units = stack([k_own, k_x, k_y, k_xy, k_yx], [upper])
+    units = stack([k_own, k_x, k_y], [to_x])
     swapped = move(units, lambda y, z, f: (y, z, f ^ 1))
-    upper = call(gather_kernel_of(2), square, [where, k_xy, k_yx, upper], [units], fence=True)
+    upper = call(gather_kernel_of(3), square, [where, k_own, k_x, k_y, upper], [units], fence=True)
     upper = call(gather_kernel_of(1), square, [where, swapped, upper])
-    upper = call(top_kernel, square, [where, top_front, top_rows, here, top_y, upper])
+    units = stack([k_xy], [upper])
+    swapped = move(units, lambda y, z, f: (y, z, f ^ 1))
+    upper = call(gather_kernel_of(1), square, [where, k_xy, upper], [units], fence=True)
+    upper = call(gather_kernel_of(1), square, [where, swapped, upper])
+    upper = call(top_kernel, square, [where, top_front, top_own, here, top_y, upper])
     upper = call(other_kernel, square, [mid_other, places, upper], scalars=False)
     return factor, mid_factor, upper
 

time: 83.9 us -> 79.1 us (0.943)
  the two profiles are of different devices: /device:TPU:0 before, /device:TPU:26 now
where the time goes in v3:
time: 79.1 us; the launch traced here: 78.5 us
  Pallas kernels  32.2 us (41%)
  waiting for transfers between devices  20.3 us (26%)
  starting transfers between devices  19.7 us (25%)
  local copies, waits for them, and re-layouts  5.38 us (7%)
  between operations  1.01 us (1%)
    pallas_call x21, Pallas kernels, call(): pl.pallas_call(kernel, out_shape=shapes[0] if single else shapes, in_spec...  32.2 us
    ppermute x14, waiting for transfers between devices, move(): return lax.ppermute(array, AXES, pairs)  20.3 us
    ppermute x14, starting transfers between devices, move(): return lax.ppermute(array, AXES, pairs)  13.6 us
    all_to_all x1, starting transfers between devices, local(): lax.all_to_all(packed.reshape(cube_count, slots, width), 'cube', split_ax...  6.05 us
    unnamed x42, local copies, waits for them, and re-layouts  5.3 us
  transfers between devices with their start and end apart: 15, of which 7 were waited for; matrix products, arithmetic and copies ran while one was open for 0% of the time, Pallas kernels for 33%

profile of v3, /device:TPU:26, one launch (start us, length us, event | category | flops | bytes accessed | tf_op | source)
XLA Modules:
  0.0 78.5 jit_solution(8948721300055634294)
XLA Ops:
  0.6 1.2 %copy-done.2 = bf16[1024,512]{1,0:T(8,128)(2,1)S(1)} copy-done((bf16[1024,512]{1,0:T(8,128)(2,1)S(1)}, bf16[1024,512]{1,0:T(8,128)(2,1)}, u32[]{:S(2)}) %copy-start.2) | copy-done | bytes 1048600
  1.9 1.0 %copy-done.4 = bf16[512,512]{1,0:T(8,128)(2,1)S(1)} copy-done((bf16[512,512]{1,0:T(8,128)(2,1)S(1)}, bf16[512,512]{1,0:T(8,128)(2,1)}, u32[]{:S(2)}) %copy-start.4) | copy-done | bytes 524312
  2.9 1.2 %shard_map.130 = (f32[1536,256]{1,0:T(8,128)S(1)}, f32[1024,256]{1,0:T(8,128)}) custom-call(bf16[1024,512]{1,0:T(8,128)(2,1)S(1)} %copy-done.2, bf16[512,512]{1,0:T(8,128)(2,1)S(1)} %copy-done.4), custom_call_target="tpu_custom_call" | custom-call | flops 1000000000 | bytes 1000 | tf_op jit(solution)/shard_map/pallas_call | solution.py:377
  4.1 1.3 %collective-permute-start = (f32[1536,256]{1,0:T(8,128)S(1)}, f32[1536,256]{1,0:T(8,128)S(1)}, u32[]{:S(2)}, u32[]{:S(2)}) collective-permute-start(f32[1536,256]{1,0:T(8,128)S(1)} %get-tuple-element.20.refs_3_.refs_1_.refs_2_), channel_id=1, source_target_pairs={{0,2},{4,6},{8,10},{12,14},{16,18},{20,22},{24,26},{28,30}} | collective-permute-start | bytes 4718600 | tf_op jit(solution)/shard_map/ppermute | solution.py:424
  5.4 1.7 %collective-permute-start.1 = (f32[1024,256]{1,0:T(8,128)}, f32[1024,256]{1,0:T(8,128)}, u32[]{:S(2)}, u32[]{:S(2)}) collective-permute-start(f32[1024,256]{1,0:T(8,128)} %get-tuple-element.24), channel_id=1, source_target_pairs={{0,4},{4,0},{8,12},{12,8},{16,20},{20,16},{24,28},{28,24}} | collective-permute-start | bytes 3145736 | tf_op jit(solution)/shard_map/ppermute | solution.py:424
  7.1 0.6 shard_map.131.refs_2_
  7.7 0.7 copy-done.6
  8.4 6.1 %all-to-all-start = ((f32[8,72,128]{2,1,0:T(8,128)}), f32[8,72,128]{2,1,0:T(8,128)S(1)}, u32[]{:S(2)}, u32[]{:S(2)}) async-start(f32[8,72,128]{2,1,0:T(8,128)} %bitcast.9), calls=%async_computation | async-start | bytes 589824 | tf_op jit(solution)/shard_map/all_to_all | solution.py:453
  14.5 0.1 stack.23.refs_0_
  14.6 1.0 %copy-done.7 = f32[576,128]{1,0:T(8,128)S(1)} copy-done((f32[576,128]{1,0:T(8,128)S(1)}, f32[576,128]{1,0:T(8,128)}, u32[]{:S(2)}) %copy-start.7) | copy-done | bytes 294936
  15.5 0.9 %shard_map.132.refs_7_.refs_8_.refs_1_ = bf16[4,512,512]{2,1,0:T(8,128)(2,1)S(1)} custom-call(s32[5]{0:T(128)S(1)} %stack.23.refs_0_, s32[4,2048]{1,0:T(4,128)S(1)} %copy-done.13, f32[576,128]{1,0:T(8,128)S(1)} %copy-done.7), custom_call_target="tpu_custom_call" | custom-call | flops 1000000000 | bytes 1000 | tf_op jit(solution)/shard_map/pallas_call | solution.py:377
  16.6 1.8 %shard_map.133 = (f32[2,128,128]{2,1,0:T(8,128)S(1)}, f32[8,128]{1,0:T(8,128)S(1)}, f32[2,128,128]{2,1,0:T(8,128)S(1)}) custom-call(s32[5]{0:T(128)S(1)} %stack.23.refs_0_, f32[2,128,128]{2,1,0:T(8,128)S(1)} %copy-done.11, f32[2,128,128]{2,1,0:T(8,128)S(1)} %copy-done.12, s32[2,128]{1,0:T(2,128)S(1)} %copy-done.16, f32[2,128]{1,0:T(2,128)S(1)} %copy-done.17, ...), custom_call_target="tpu_custom_call" | custom-call | flops 1000000000 | bytes 1000 | tf_op jit(solution)/shard_map/pallas_call | solution.py:377
  18.4 0.0 copy-start.19
  18.4 0.6 copy-done.19
  19.1 7.4 %collective-permute-done.refs_2_.refs_3_ = f32[1536,256]{1,0:T(8,128)S(1)} collective-permute-done((f32[1536,256]{1,0:T(8,128)S(1)}, f32[1536,256]{1,0:T(8,128)S(1)}, u32[]{:S(2)}, u32[]{:S(2)}) %collective-permute-start) | collective-permute-done | bytes 1572896 | tf_op jit(solution)/shard_map/ppermute | solution.py:424
  26.4 1.4 %shard_map.134.refs_4_.refs_1_ = f32[512,256]{1,0:T(8,128)} custom-call(s32[5]{0:T(128)S(1)} %stack.23.refs_0_, f32[1536,256]{1,0:T(8,128)S(1)} %get-tuple-element.20.refs_3_.refs_1_.refs_2_, f32[1536,256]{1,0:T(8,128)S(1)} %collective-permute-done.refs_2_.refs_3_, f32[2,128,128]{2,1,0:T(8,128)S(1)} %get-tuple-element.21.refs_3_.refs_1_), custom_call_target="tpu_custom_call" | custom-call | flops 1000000000 | bytes 1000 | tf_op jit(solution)/shard_map/pallas_call | solution.py:377
  27.8 0.7 copy-done.8
  28.5 1.5 %shard_map.135 = (f32[1792,256]{1,0:T(8,128)S(1)}, f32[512,256]{1,0:T(8,128)S(1)}) custom-call(s32[5]{0:T(128)S(1)} %stack.23.refs_0_, f32[1536,256]{1,0:T(8,128)S(1)} %get-tuple-element.20.refs_3_.refs_1_.refs_2_, f32[1536,256]{1,0:T(8,128)S(1)} %collective-permute-done.refs_2_.refs_3_, f32[1024,256]{1,0:T(8,128)} %collective-permute-done.1.refs_3_.refs_4_, ...), custom_call_target="tpu_custom_call" | custom-call | flops 1000000000 | bytes 1000 | tf_op jit(solution)/shard_map/pallas_call | solution.py:377
  30.0 1.4 %collective-permute-start.2 = (f32[1792,256]{1,0:T(8,128)S(1)}, f32[1792,256]{1,0:T(8,128)S(1)}, u32[]{:S(2)}, u32[]{:S(2)}) collective-permute-start(f32[1792,256]{1,0:T(8,128)S(1)} %get-tuple-element.25.refs_4_), channel_id=1, source_target_pairs={{0,1},{2,3},{4,5},{6,7},{8,9},{10,11},{12,13},{14,15},{16,17},{18,... | collective-permute-start | bytes 5505032 | tf_op jit(solution)/shard_map/ppermute | solution.py:424
  31.4 3.4 %collective-permute-start.3 = (f32[512,256]{1,0:T(8,128)S(1)}, f32[512,256]{1,0:T(8,128)S(1)}, u32[]{:S(2)}, u32[]{:S(2)}) collective-permute-start(f32[512,256]{1,0:T(8,128)S(1)} %get-tuple-element.27), channel_id=1, source_target_pairs={{0,3},{2,6},{4,7},{6,2},{8,11},{10,14},{12,15},{14,10},{16,19},{18... | collective-permute-start | bytes 1572872 | tf_op jit(solution)/shard_map/ppermute | solution.py:424
  34.8 2.4 %collective-permute-start.4 = (f32[512,256]{1,0:T(8,128)}, f32[512,256]{1,0:T(8,128)S(1)}, u32[]{:S(2)}, u32[]{:S(2)}) collective-permute-start(f32[512,256]{1,0:T(8,128)} %shard_map.134.refs_4_.refs_1_), channel_id=1, source_target_pairs={{0,8},{2,10},{4,12},{6,14},{8,0},{10,2},{12,4},{14,6},{16,24},{18,... | collective-permute-start | bytes 1572872 | tf_op jit(solution)/shard_map/ppermute | solution.py:424
  37.2 1.6 %shard_map.136 = (f32[2,128,128]{2,1,0:T(8,128)}, f32[2,136,128]{2,1,0:T(8,128)S(1)}) custom-call(f32[8,72,128]{2,1,0:T(8,128)S(1)} %all-to-all-done.refs_5_.refs_0_, f32[2,128,128]{2,1,0:T(8,128)S(1)} %copy-done.9, f32[8,128]{1,0:T(8,128)S(1)} %get-tuple-element.22.refs_2_, f32[2,128,128]{2,1,0:T(8,128)S(1)} %copy-done.20, ...), custom_call_target="tpu_custom_call" | custom-call | flops 1000000000 | bytes 1000 | tf_op jit(solution)/shard_map/pallas_call | solution.py:377
  38.8 1.6 %collective-permute-start.5 = (f32[1,2,136,128]{3,2,1,0:T(8,128)S(1)}, f32[1,2,136,128]{3,2,1,0:T(8,128)S(1)}, u32[]{:S(2)}, u32[]{:S(2)}) collective-permute-start(f32[1,2,136,128]{3,2,1,0:T(8,128)S(1)} %bitcast.10), channel_id=1, source_target_pairs={{0,8},{1,9},{2,10},{3,11},{4,12},{5,13},{6,14},{7,15},{8,0},{9,1},... | collective-permute-start | bytes 417800 | tf_op jit(solution)/shard_map/ppermute | solution.py:424
  40.4 2.1 %collective-permute-done.3.refs_6_ = f32[512,256]{1,0:T(8,128)S(1)} collective-permute-done((f32[512,256]{1,0:T(8,128)S(1)}, f32[512,256]{1,0:T(8,128)S(1)}, u32[]{:S(2)}, u32[]{:S(2)}) %collective-permute-start.3) | collective-permute-done | bytes 524320 | tf_op jit(solution)/shard_map/ppermute | solution.py:424
  42.5 3.7 %shard_map.137 = (f32[512,256]{1,0:T(8,128)S(1)}, f32[512,256]{1,0:T(8,128)S(1)}, f32[3,128,128]{2,1,0:T(8,128)S(1)}, f32[512,512]{1,0:T(8,128)S(1)}) custom-call(s32[5]{0:T(128)S(1)} %stack.23.refs_0_, bf16[1024,512]{1,0:T(8,128)(2,1)S(1)} %copy-done.3, f32[1536,256]{1,0:T(8,128)S(1)} %get-tuple-element.20.refs_3_.refs_1_.refs_2_, ...), custom_call_target="tpu_custom_call" | custom-call | flops 30000001024 | bytes 1000 | tf_op jit(solution)/shard_map/pallas_call | solution.py:377
  46.2 1.4 %collective-permute-done.5.refs_1_ = f32[1,2,136,128]{3,2,1,0:T(8,128)S(1)} collective-permute-done((f32[1,2,136,128]{3,2,1,0:T(8,128)S(1)}, f32[1,2,136,128]{3,2,1,0:T(8,128)S(1)}, u32[]{:S(2)}, u32[]{:S(2)}) %collective-permute-start.5) | collective-permute-done | bytes 139296 | tf_op jit(solution)/shard_map/ppermute | solution.py:424
  47.6 1.2 %shard_map.139.refs_1_ = f32[1024,256]{1,0:T(8,128)S(1)} custom-call(s32[5]{0:T(128)S(1)} %stack.23.refs_0_, f32[512,256]{1,0:T(8,128)} %shard_map.134.refs_4_.refs_1_, f32[512,256]{1,0:T(8,128)S(1)} %collective-permute-done.4.refs_2_, f32[2,2,136,128]{3,2,1,0:T(8,128)S(1)} %shard_map.138.refs_3_.refs_0_.refs_1_), custom_call_target="tpu_custom_call" | custom-call | flops 1000000000 | bytes 1000 | tf_op jit(solution)/shard_map/pallas_call | solution.py:377
  48.8 0.1 collective-permute-start.6
  48.9 0.6 collective-permute-start.9
  49.5 0.4 collective-permute-start.7
  49.9 1.6 %collective-permute-done.6.refs_2_ = f32[1024,256]{1,0:T(8,128)S(1)} collective-permute-done((f32[1024,256]{1,0:T(8,128)S(1)}, f32[1024,256]{1,0:T(8,128)S(1)}, u32[]{:S(2)}, u32[]{:S(2)}) %collective-permute-start.6) | collective-permute-done | bytes 1048608 | tf_op jit(solution)/shard_map/ppermute | solution.py:424
  51.5 0.7 shard_map.140
  52.2 0.6 collective-permute-start.8
  52.8 2.7 %shard_map.141 = (f32[256,256]{1,0:T(8,128)}, f32[512,512]{1,0:T(8,128)S(1)}) custom-call(s32[5]{0:T(128)S(1)} %stack.23.refs_0_, bf16[1024,512]{1,0:T(8,128)(2,1)S(1)} %copy-done.3, f32[1536,256]{1,0:T(8,128)S(1)} %get-tuple-element.20.refs_3_.refs_1_.refs_2_, f32[1536,256]{1,0:T(8,128)S(1)} %collective-permute-done.refs_2_.refs_3_, ...), custom_call_target="tpu_custom_call" | custom-call | flops 1000000000 | bytes 1000 | tf_op jit(solution)/shard_map/pallas_call | solution.py:377
  55.5 2.9 %collective-permute-done.9.refs_0_.refs_2_.refs_3_ = f32[2,2,136,128]{3,2,1,0:T(8,128)S(1)} collective-permute-done((f32[2,2,136,128]{3,2,1,0:T(8,128)S(1)}, f32[2,2,136,128]{3,2,1,0:T(8,128)S(1)}, u32[]{:S(2)}, u32[]{:S(2)}) %collective-permute-start.9) | collective-permute-done | bytes 278560 | tf_op jit(solution)/shard_map/ppermute | solution.py:424
  58.4 0.1 collective-permute-start.10
  58.5 0.1 shard_map.143.refs_5_
  58.6 0.1 collective-permute-start.12
  58.7 3.3 %shard_map.144.refs_2_ = f32[512,512]{1,0:T(8,128)S(1)} custom-call(s32[5]{0:T(128)S(1)} %stack.23.refs_0_, f32[2,2,136,128]{3,2,1,0:T(8,128)S(1)} %shard_map.138.refs_3_.refs_0_.refs_1_, f32[2,2,136,128]{3,2,1,0:T(8,128)S(1)} %collective-permute-done.11.refs_1_.refs_2_, f32[2,2,136,128]{3,2,1,0:T(8,128)S(1)} %collective-permute-done.9.refs_0_.refs_2_.refs_3_, ...), custom_call_target="tpu_custom_call" | custom-call | flops 30000001024 | bytes 1000 | tf_op jit(solution)/shard_map/pallas_call | solution.py:377
  62.0 3.3 %shard_map.145.refs_1_.refs_2_ = f32[512,512]{1,0:T(8,128)S(1)} custom-call(s32[5]{0:T(128)S(1)} %stack.23.refs_0_, f32[6,2,136,128]{3,2,1,0:T(8,128)S(1)} %collective-permute-done.12.refs_1_, f32[512,512]{1,0:T(8,128)S(1)} %shard_map.144.refs_2_), custom_call_target="tpu_custom_call" | custom-call | flops 1000000000 | bytes 1000 | tf_op jit(solution)/shard_map/pallas_call | solution.py:377
  65.2 1.0 %collective-permute-done.10.refs_0_.refs_1_ = f32[2,2,136,128]{3,2,1,0:T(8,128)S(1)} collective-permute-done((f32[2,2,136,128]{3,2,1,0:T(8,128)S(1)}, f32[2,2,136,128]{3,2,1,0:T(8,128)S(1)}, u32[]{:S(2)}, u32[]{:S(2)}) %collective-permute-start.10) | collective-permute-done | bytes 278560 | tf_op jit(solution)/shard_map/ppermute | solution.py:424
  66.3 0.1 collective-permute-start.13
  66.4 1.6 %shard_map.147.refs_2_ = f32[512,512]{1,0:T(8,128)S(1)} custom-call(s32[5]{0:T(128)S(1)} %stack.23.refs_0_, f32[2,2,136,128]{3,2,1,0:T(8,128)S(1)} %collective-permute-done.10.refs_0_.refs_1_, f32[512,512]{1,0:T(8,128)S(1)} %shard_map.145.refs_1_.refs_2_, f32[2,2,136,128]{3,2,1,0:T(8,128)S(1)} %shard_map.146.refs_3_), custom_call_target="tpu_custom_call" | custom-call | flops 30000001024 | bytes 1000 | tf_op jit(solution)/shard_map/pallas_call | solution.py:377
  68.0 0.0 copy-start.5
  68.0 1.6 %shard_map.148.refs_5_ = f32[512,512]{1,0:T(8,128)S(1)} custom-call(s32[5]{0:T(128)S(1)} %stack.23.refs_0_, f32[2,2,136,128]{3,2,1,0:T(8,128)S(1)} %collective-permute-done.13.refs_1_, f32[512,512]{1,0:T(8,128)S(1)} %shard_map.147.refs_2_), custom_call_target="tpu_custom_call" | custom-call | flops 1000000000 | bytes 1000 | tf_op jit(solution)/shard_map/pallas_call | solution.py:377
  69.6 3.8 %collective-permute-done.8.refs_4_ = f32[704,256]{1,0:T(8,128)S(1)} collective-permute-done((f32[704,256]{1,0:T(8,128)S(1)}, f32[704,256]{1,0:T(8,128)S(1)}, u32[]{:S(2)}, u32[]{:S(2)}) %collective-permute-start.8) | collective-permute-done | bytes 720928 | tf_op jit(solution)/shard_map/ppermute | solution.py:424
  73.4 2.9 %shard_map.149.refs_2_ = f32[512,512]{1,0:T(8,128)S(1)} custom-call(s32[5]{0:T(128)S(1)} %stack.23.refs_0_, bf16[512,512]{1,0:T(8,128)(2,1)S(1)} %copy-done.5, f32[512,256]{1,0:T(8,128)S(1)} %get-tuple-element.35.refs_2_, f32[704,256]{1,0:T(8,128)S(1)} %get-tuple-element.33.refs_9_.refs_3_, f32[704,256]{1,0:T(8,128)S(1)} %collective-permute-done.8.refs_4_, ...), custom_call_target="tpu_custom_call" | custom-call | flops 1000000000 | bytes 1000 | tf_op jit(solution)/shard_map/pallas_call | solution.py:377
  76.3 2.2 %shard_map.150 = f32[512,512]{1,0:T(8,128)} custom-call(f32[512,512]{1,0:T(8,128)S(1)} %collective-permute-done.7.refs_0_, bf16[4,512,512]{2,1,0:T(8,128)(2,1)S(1)} %copy-done.1, f32[512,512]{1,0:T(8,128)S(1)} %shard_map.149.refs_2_), custom_call_target="tpu_custom_call" | custom-call | flops 1000000000 | bytes 1000 | tf_op jit(solution)/shard_map/pallas_call | solution.py:377
  (46 shorter events, 0.2 us)
Async XLA Ops:
  0.6 1.2 %copy-start.2 = (bf16[1024,512]{1,0:T(8,128)(2,1)S(1)}, bf16[1024,512]{1,0:T(8,128)(2,1)}, u32[]{:S(2)}) copy-start(bf16[1024,512]{1,0:T(8,128)(2,1)} %refs_1_.10) | copy-start | bytes 3145732
  1.9 1.0 %copy-start.4 = (bf16[512,512]{1,0:T(8,128)(2,1)S(1)}, bf16[512,512]{1,0:T(8,128)(2,1)}, u32[]{:S(2)}) copy-start(bf16[512,512]{1,0:T(8,128)(2,1)} %refs_1_.11) | copy-start | bytes 1572868
  2.9 4.2 %copy-start.10 = (f32[1,256,128]{2,1,0:T(8,128)S(1)}, f32[1,256,128]{2,1,0:T(8,128)}, u32[]{:S(2)}) copy-start(f32[1,256,128]{2,1,0:T(8,128)} %param.11) | copy-start | bytes 393220
  2.9 4.2 %copy-start.14 = (s32[1,256,1]{1,2,0:T(1,128)S(1)}, s32[1,256,1]{1,2,0:T(1,128)}, u32[]{:S(2)}) copy-start(s32[1,256,1]{1,2,0:T(1,128)} %param.12) | copy-start | bytes 3076
  2.9 4.2 %copy-start.15 = (s32[1,256]{1,0:T(1,128)S(1)}, s32[1,256]{1,0:T(1,128)}, u32[]{:S(2)}) copy-start(s32[1,256]{1,0:T(1,128)} %refs_2_.2) | copy-start | bytes 3076
  4.1 22.3 %collective-permute-start = (f32[1536,256]{1,0:T(8,128)S(1)}, f32[1536,256]{1,0:T(8,128)S(1)}, u32[]{:S(2)}, u32[]{:S(2)}) collective-permute-start(f32[1536,256]{1,0:T(8,128)S(1)} %get-tuple-element.20.refs_3_.refs_1_.refs_2_), channel_id=1, source_target_pairs={{0,2},{4,6},{8,10},{12,14},{16,18},{20,22},{24,26},{28,30}} | collective-permute-start | bytes 4718600 | tf_op jit(solution)/shard_map/ppermute | solution.py:424
  5.4 23.1 %collective-permute-start.1 = (f32[1024,256]{1,0:T(8,128)}, f32[1024,256]{1,0:T(8,128)}, u32[]{:S(2)}, u32[]{:S(2)}) collective-permute-start(f32[1024,256]{1,0:T(8,128)} %get-tuple-element.24), channel_id=1, source_target_pairs={{0,4},{4,0},{8,12},{12,8},{16,20},{20,16},{24,28},{28,24}} | collective-permute-start | bytes 3145736 | tf_op jit(solution)/shard_map/ppermute | solution.py:424
  7.1 7.5 %copy-start.13 = (s32[4,2048]{1,0:T(4,128)S(1)}, s32[4,2048]{1,0:T(4,128)}, u32[]{:S(2)}) copy-start(s32[4,2048]{1,0:T(4,128)} %refs_6_.1) | copy-start | bytes 98308
  7.7 0.7 copy-start.6
  8.4 20.0 %all-to-all-start = ((f32[8,72,128]{2,1,0:T(8,128)}), f32[8,72,128]{2,1,0:T(8,128)S(1)}, u32[]{:S(2)}, u32[]{:S(2)}) async-start(f32[8,72,128]{2,1,0:T(8,128)} %bitcast.9), calls=%async_computation | async-start | bytes 589824 | tf_op jit(solution)/shard_map/all_to_all | solution.py:453
  14.6 1.0 %copy-start.7 = (f32[576,128]{1,0:T(8,128)S(1)}, f32[576,128]{1,0:T(8,128)}, u32[]{:S(2)}) copy-start(f32[576,128]{1,0:T(8,128)} %copy-done.6) | copy-start | bytes 884740
  15.5 1.0 %copy-start.11 = (f32[2,128,128]{2,1,0:T(8,128)S(1)}, f32[2,128,128]{2,1,0:T(8,128)}, u32[]{:S(2)}) copy-start(f32[2,128,128]{2,1,0:T(8,128)} %refs_1_.8) | copy-start | bytes 393220
  15.5 1.0 %copy-start.12 = (f32[2,128,128]{2,1,0:T(8,128)S(1)}, f32[2,128,128]{2,1,0:T(8,128)}, u32[]{:S(2)}) copy-start(f32[2,128,128]{2,1,0:T(8,128)} %refs_2_.3) | copy-start | bytes 393220
  15.5 1.0 %copy-start.16 = (s32[2,128]{1,0:T(2,128)S(1)}, s32[2,128]{1,0:T(2,128)}, u32[]{:S(2)}) copy-start(s32[2,128]{1,0:T(2,128)} %refs_3_.1) | copy-start | bytes 3076
  15.5 1.0 %copy-start.17 = (f32[2,128]{1,0:T(2,128)S(1)}, f32[2,128]{1,0:T(2,128)}, u32[]{:S(2)}) copy-start(f32[2,128]{1,0:T(2,128)} %refs_4_.1) | copy-start | bytes 3076
  15.5 1.0 %copy-start.18 = (s32[2,128]{1,0:T(2,128)S(1)}, s32[2,128]{1,0:T(2,128)}, u32[]{:S(2)}) copy-start(s32[2,128]{1,0:T(2,128)} %refs_5_.1) | copy-start | bytes 3076
  16.5 1.8 %copy-start = (bf16[4,512,512]{2,1,0:T(8,128)(2,1)}, bf16[4,512,512]{2,1,0:T(8,128)(2,1)S(1)}, u32[]{:S(2)}) copy-start(bf16[4,512,512]{2,1,0:T(8,128)(2,1)S(1)} %shard_map.132.refs_7_.refs_8_.refs_1_) | copy-start | bytes 6291460
  18.4 0.7 copy-start.19
  27.8 0.7 copy-start.8
  28.5 8.7 %copy-start.9 = (f32[2,128,128]{2,1,0:T(8,128)S(1)}, f32[2,128,128]{2,1,0:T(8,128)}, u32[]{:S(2)}) copy-start(f32[2,128,128]{2,1,0:T(8,128)} %copy-done.8) | copy-start | bytes 393220
  28.5 8.8 %copy-start.20 = (f32[2,128,128]{2,1,0:T(8,128)S(1)}, f32[2,128,128]{2,1,0:T(8,128)}, u32[]{:S(2)}) copy-start(f32[2,128,128]{2,1,0:T(8,128)} %copy-done.19) | copy-start | bytes 393220
  30.0 12.5 %collective-permute-start.2 = (f32[1792,256]{1,0:T(8,128)S(1)}, f32[1792,256]{1,0:T(8,128)S(1)}, u32[]{:S(2)}, u32[]{:S(2)}) collective-permute-start(f32[1792,256]{1,0:T(8,128)S(1)} %get-tuple-element.25.refs_4_), channel_id=1, source_target_pairs={{0,1},{2,3},{4,5},{6,7},{8,9},{10,11},{12,13},{14,15},{16,17},{18,... | collective-permute-start | bytes 5505032 | tf_op jit(solution)/shard_map/ppermute | solution.py:424
  31.4 11.1 %collective-permute-start.3 = (f32[512,256]{1,0:T(8,128)S(1)}, f32[512,256]{1,0:T(8,128)S(1)}, u32[]{:S(2)}, u32[]{:S(2)}) collective-permute-start(f32[512,256]{1,0:T(8,128)S(1)} %get-tuple-element.27), channel_id=1, source_target_pairs={{0,3},{2,6},{4,7},{6,2},{8,11},{10,14},{12,15},{14,10},{16,19},{18... | collective-permute-start | bytes 1572872 | tf_op jit(solution)/shard_map/ppermute | solution.py:424
  34.8 12.8 %collective-permute-start.4 = (f32[512,256]{1,0:T(8,128)}, f32[512,256]{1,0:T(8,128)S(1)}, u32[]{:S(2)}, u32[]{:S(2)}) collective-permute-start(f32[512,256]{1,0:T(8,128)} %shard_map.134.refs_4_.refs_1_), channel_id=1, source_target_pairs={{0,8},{2,10},{4,12},{6,14},{8,0},{10,2},{12,4},{14,6},{16,24},{18,... | collective-permute-start | bytes 1572872 | tf_op jit(solution)/shard_map/ppermute | solution.py:424
  37.2 5.3 %copy-start.3 = (bf16[1024,512]{1,0:T(8,128)(2,1)S(1)}, bf16[1024,512]{1,0:T(8,128)(2,1)}, u32[]{:S(2)}) copy-start(bf16[1024,512]{1,0:T(8,128)(2,1)} %refs_1_.10) | copy-start | bytes 3145732
  38.8 8.8 %collective-permute-start.5 = (f32[1,2,136,128]{3,2,1,0:T(8,128)S(1)}, f32[1,2,136,128]{3,2,1,0:T(8,128)S(1)}, u32[]{:S(2)}, u32[]{:S(2)}) collective-permute-start(f32[1,2,136,128]{3,2,1,0:T(8,128)S(1)} %bitcast.10), channel_id=1, source_target_pairs={{0,8},{1,9},{2,10},{3,11},{4,12},{5,13},{6,14},{7,15},{8,0},{9,1},... | collective-permute-start | bytes 417800 | tf_op jit(solution)/shard_map/ppermute | solution.py:424
  48.8 4.0 %copy-start.1 = (bf16[4,512,512]{2,1,0:T(8,128)(2,1)S(1)}, bf16[4,512,512]{2,1,0:T(8,128)(2,1)}, u32[]{:S(2)}) copy-start(bf16[4,512,512]{2,1,0:T(8,128)(2,1)} %copy-done) | copy-start | bytes 6291460
  48.8 2.7 %collective-permute-start.6 = (f32[1024,256]{1,0:T(8,128)S(1)}, f32[1024,256]{1,0:T(8,128)S(1)}, u32[]{:S(2)}, u32[]{:S(2)}) collective-permute-start(f32[1024,256]{1,0:T(8,128)S(1)} %shard_map.139.refs_1_), channel_id=1, source_target_pairs={{0,1},{1,0},{2,3},{3,2},{4,5},{5,4},{6,7},{7,6},{8,9},{9,8},{10,11... | collective-permute-start | bytes 3145736 | tf_op jit(solution)/shard_map/ppermute | solution.py:424
  48.9 9.5 %collective-permute-start.9 = (f32[2,2,136,128]{3,2,1,0:T(8,128)S(1)}, f32[2,2,136,128]{3,2,1,0:T(8,128)S(1)}, u32[]{:S(2)}, u32[]{:S(2)}) collective-permute-start(f32[2,2,136,128]{3,2,1,0:T(8,128)S(1)} %shard_map.138.refs_3_.refs_0_.refs_1_), channel_id=1, source_target_pairs={{0,4},{1,5},{2,6},{3,7},{4,0},{5,1},{6,2},{7,3},{8,12},{9,13},{10,... | collective-permute-start | bytes 835592 | tf_op jit(solution)/shard_map/ppermute | solution.py:424
  49.5 26.8 %collective-permute-start.7 = (f32[512,512]{1,0:T(8,128)S(1)}, f32[512,512]{1,0:T(8,128)S(1)}, u32[]{:S(2)}, u32[]{:S(2)}) collective-permute-start(f32[512,512]{1,0:T(8,128)S(1)} %get-tuple-element.32.refs_2_), channel_id=1, source_target_pairs={{0,8},{1,9},{2,10},{3,11},{4,12},{5,13},{6,14},{7,15},{8,0},{9,1},... | collective-permute-start | bytes 3145736 | tf_op jit(solution)/shard_map/ppermute | solution.py:424
  49.9 8.6 %collective-permute-start.11 = (f32[2,2,136,128]{3,2,1,0:T(8,128)S(1)}, f32[2,2,136,128]{3,2,1,0:T(8,128)S(1)}, u32[]{:S(2)}, u32[]{:S(2)}) collective-permute-start(f32[2,2,136,128]{3,2,1,0:T(8,128)S(1)} %shard_map.138.refs_3_.refs_0_.refs_1_), channel_id=1, source_target_pairs={{0,2},{1,3},{2,0},{3,1},{4,6},{5,7},{6,4},{7,5},{8,10},{9,11},{10,... | collective-permute-start | bytes 835592 | tf_op jit(solution)/shard_map/ppermute | solution.py:424
  52.2 21.2 %collective-permute-start.8 = (f32[704,256]{1,0:T(8,128)S(1)}, f32[704,256]{1,0:T(8,128)S(1)}, u32[]{:S(2)}, u32[]{:S(2)}) collective-permute-start(f32[704,256]{1,0:T(8,128)S(1)} %get-tuple-element.33.refs_9_.refs_3_), channel_id=1, source_target_pairs={{0,4},{1,5},{2,6},{3,7},{4,0},{5,1},{6,2},{7,3},{8,12},{9,13},{10,... | collective-permute-start | bytes 2162696 | tf_op jit(solution)/shard_map/ppermute | solution.py:424
  58.4 7.8 %collective-permute-start.10 = (f32[2,2,136,128]{3,2,1,0:T(8,128)S(1)}, f32[2,2,136,128]{3,2,1,0:T(8,128)S(1)}, u32[]{:S(2)}, u32[]{:S(2)}) collective-permute-start(f32[2,2,136,128]{3,2,1,0:T(8,128)S(1)} %shard_map.142.refs_3_), channel_id=1, source_target_pairs={{0,2},{1,3},{2,0},{3,1},{4,6},{5,7},{6,4},{7,5},{8,10},{9,11},{10,... | collective-permute-start | bytes 835592 | tf_op jit(solution)/shard_map/ppermute | solution.py:424
  58.6 3.4 %collective-permute-start.12 = (f32[6,2,136,128]{3,2,1,0:T(8,128)S(1)}, f32[6,2,136,128]{3,2,1,0:T(8,128)S(1)}, u32[]{:S(2)}, u32[]{:S(2)}) collective-permute-start(f32[6,2,136,128]{3,2,1,0:T(8,128)S(1)} %shard_map.143.refs_5_), channel_id=1, source_target_pairs={{0,1},{1,0},{2,3},{3,2},{4,5},{5,4},{6,7},{7,6},{8,9},{9,8},{10,11... | collective-permute-start | bytes 2506760 | tf_op jit(solution)/shard_map/ppermute | solution.py:424
  66.3 1.7 %collective-permute-start.13 = (f32[2,2,136,128]{3,2,1,0:T(8,128)S(1)}, f32[2,2,136,128]{3,2,1,0:T(8,128)S(1)}, u32[]{:S(2)}, u32[]{:S(2)}) collective-permute-start(f32[2,2,136,128]{3,2,1,0:T(8,128)S(1)} %shard_map.146.refs_3_), channel_id=1, source_target_pairs={{0,1},{1,0},{2,3},{3,2},{4,5},{5,4},{6,7},{7,6},{8,9},{9,8},{10,11... | collective-permute-start | bytes 835592 | tf_op jit(solution)/shard_map/ppermute | solution.py:424
  68.0 5.4 %copy-start.5 = (bf16[512,512]{1,0:T(8,128)(2,1)S(1)}, bf16[512,512]{1,0:T(8,128)(2,1)}, u32[]{:S(2)}) copy-start(bf16[512,512]{1,0:T(8,128)(2,1)} %refs_1_.11) | copy-start | bytes 1572868

commit v4 on v3

--- a/solution.py
+++ b/solution.py
@@ -260,12 +260,15 @@
     out[...] = base[...] + spread(block[...], places, 1)
 
 
-def top_kernel(where, front, rows, here, from_y, base, out):
+def top_kernel(where, front, rows, here, first, from_y, from_core, base, out):
     low, pos, quarter = where[0], where[2], where[3]
-    col_rows = jnp.where(low == pos // 2, here[0:QUARTER, :], from_y[0:QUARTER, :])
-    pivots = jnp.where(low == 0, here[QUARTER:, :], from_y[QUARTER:, :])
-    last = jnp.concatenate([pivots[PIV:, 0:PIV], pivots[PIV:, PIV:KU]], axis=0)
-    upper, below, lower = panel_parts(pivots[0:PIV, 0:PIV], pivots[0:PIV, PIV:KU], last)
+    col_rows = jnp.where(low == pos // 2, here[...], from_y[...])
+    pivots = jnp.where(
+        low == 0, first[...], jnp.where(pos == 1, from_core[...], from_y[0:KU, :])
+    )
+    upper, below, lower = panel_parts(
+        pivots[0:PIV, 0:PIV], pivots[PIV:KU, 0:PIV], pivots[PIV:KU, PIV:KU]
+    )
     row_left, _ = panel_rows(rows[...], quarter * QUARTER, upper, below, lower)
     _, col_keep = panel_rows(col_rows, pos * QUARTER, upper, below, lower)
     out[...] = base[...] + front[...].astype(F32) - mm3(row_left, col_keep, NT)
@@ -343,17 +346,18 @@
     pair[QUARTER:, :] = jnp.where(first, top_z[...], top_rows[...])
 
 
-def here_kernel(where, pair, from_core, rows, out):
+def here_kernel(where, pair, from_core, rows, out, first):
     even = where[2] % 2 == 0
-    own = pl.multiple_of(where[1] * QUARTER, QUARTER)
-    rows[...] = jnp.where(even, pair[pl.ds(own, QUARTER), :], from_core[pl.ds(own, QUARTER), :])
-    out[0:QUARTER, :] = jnp.where(even, pair[0:QUARTER, :], from_core[QUARTER:, :])
-    half = PIV // 2
-    first = jnp.where(even, pair[0:KU, :], from_core[0:KU, :])
-    out[QUARTER : QUARTER + PIV, 0:PIV] = first[0:PIV, 0:PIV]
-    out[QUARTER : QUARTER + PIV, PIV:KU] = first[PIV:KU, 0:PIV]
-    out[QUARTER + PIV :, 0:PIV] = first[PIV : PIV + half, PIV:KU]
-    out[QUARTER + PIV :, PIV:KU] = first[PIV + half : KU, PIV:KU]
+    own = pl.ds(pl.multiple_of(where[1] * QUARTER, QUARTER), QUARTER)
+    rows[...] = jnp.where(even, pair[own, :], from_core[own, :])
+    low_half = jnp.where(even, pair[0:QUARTER, :], from_core[0:QUARTER, :])
+    first[...] = low_half[0:KU, :]
+    second = jnp.logical_and(jnp.logical_not(even), where[2] // 2 == where[0])
+    out[...] = jnp.where(second, from_core[QUARTER:, :], low_half)
+
+
+def first_kernel(from_y, out):
+    out[...] = from_y[0:KU, :]
 
 
 COST = pl.CostEstimate(flops=10**9, bytes_accessed=1000, transcendentals=0)
@@ -468,17 +472,17 @@
         far=(1, 2),
     )
 
-    top_rows = call(choose_kernel, [(QUARTER, KU)], [where, both, both_x], [inverse])
-    top_z = move(top_rows, lambda y, z, f: (y, 1 - z, f) if f % 2 == 0 else None)
-
     to_core, to_cross = call(
         relay_kernel,
         [(HALF + QUARTER + KU, KU), (QUARTER, KU)],
         [where, both, both_x, mid_y],
-        [top_rows, got],
+        [inverse, got],
     )
     mid_cross = move(to_cross, lambda y, z, f: {0: (y, z, 3), 2: (1 - y, z, 2)}.get(f))
     mid_core = move(to_core, lambda y, z, f: (y, z, f + 1) if f % 2 == 0 else None)
+
+    top_rows = call(choose_kernel, [(QUARTER, KU)], [where, both, both_x], [to_core])
+    top_z = move(top_rows, lambda y, z, f: (y, 1 - z, f))
 
     factor, sent = call(
         functools.partial(leaf_kernel, capacity, slots, cube_count),
@@ -505,9 +509,9 @@
     k_y = move(k_own, lambda y, z, f: (1 - y, z, f))
     pair = call(pair_kernel, [(HALF, KU)], [where, top_rows, top_z], [k_own])
     pair_core = move(pair, lambda y, z, f: (y, z, f ^ 1))
-    top_own, here = call(
+    top_own, here, top_first = call(
         here_kernel,
-        [(QUARTER, KU), (QUARTER + PIV + PIV // 2, KU)],
+        [(QUARTER, KU), (QUARTER, KU), (KU, KU)],
         [where, pair, pair_core],
     )
     top_y = move(here, lambda y, z, f: (1 - y, z, f))
@@ -527,8 +531,14 @@
     units = stack([k_xy], [upper])
     swapped = move(units, lambda y, z, f: (y, z, f ^ 1))
     upper = call(gather_kernel_of(1), square, [where, k_xy, upper], [units], fence=True)
-    upper = call(gather_kernel_of(1), square, [where, swapped, upper])
-    upper = call(top_kernel, square, [where, top_front, top_own, here, top_y, upper])
+    from_y = call(first_kernel, [(KU, KU)], [top_y], [upper], scalars=False)
+    top_core = move(from_y, lambda y, z, f: (y, z, f ^ 1))
+    upper = call(gather_kernel_of(1), square, [where, swapped, upper], [from_y])
+    upper = call(
+        top_kernel,
+        square,
+        [where, top_front, top_own, here, top_first, top_y, top_core, upper],
+    )
     upper = call(other_kernel, square, [mid_other, places, upper], scalars=False)
     return factor, mid_factor, upper
 

time: 79.1 us -> 76.1 us (0.962)
  the two profiles are of different devices: /device:TPU:26 before, /device:TPU:0 now
where the time goes in v4:
time: 76.1 us; the launch traced here: 75.6 us
  Pallas kernels  31 us (41%)
  starting transfers between devices  27.5 us (36%)
  waiting for transfers between devices  8.4 us (11%)
  local copies, waits for them, and re-layouts  7.66 us (10%)
  between operations  1.04 us (1%)
    pallas_call x22, Pallas kernels, call(): pl.pallas_call(kernel, out_shape=shapes[0] if single else shapes, in_spec...  31 us
    ppermute x15, starting transfers between devices, move(): return lax.ppermute(array, AXES, pairs)  22.6 us
    unnamed x44, local copies, waits for them, and re-layouts  7.58 us
    all_to_all x1, starting transfers between devices, local(): lax.all_to_all(packed.reshape(cube_count, slots, width), 'cube', split_ax...  4.89 us
    ppermute x15, waiting for transfers between devices, move(): return lax.ppermute(array, AXES, pairs)  4.64 us
    all_to_all x1, waiting for transfers between devices, local(): lax.all_to_all(packed.reshape(cube_count, slots, width), 'cube', split_ax...  3.76 us
  transfers between devices with their start and end apart: 16, of which 5 were waited for; matrix products, arithmetic and copies ran while one was open for 0% of the time, Pallas kernels for 34%

profile of v4, /device:TPU:0, one launch (start us, length us, event | category | flops | bytes accessed | tf_op | source)
XLA Modules:
  0.0 75.6 jit_solution(7433123733979385296)
XLA Ops:
  0.6 1.2 %copy-done.2 = bf16[1024,512]{1,0:T(8,128)(2,1)S(1)} copy-done((bf16[1024,512]{1,0:T(8,128)(2,1)S(1)}, bf16[1024,512]{1,0:T(8,128)(2,1)}, u32[]{:S(2)}) %copy-start.2) | copy-done | bytes 1048600
  1.9 1.0 %copy-done.4 = bf16[512,512]{1,0:T(8,128)(2,1)S(1)} copy-done((bf16[512,512]{1,0:T(8,128)(2,1)S(1)}, bf16[512,512]{1,0:T(8,128)(2,1)}, u32[]{:S(2)}) %copy-start.4) | copy-done | bytes 524312
  2.9 1.2 %shard_map.130 = (f32[1536,256]{1,0:T(8,128)S(1)}, f32[1024,256]{1,0:T(8,128)}) custom-call(bf16[1024,512]{1,0:T(8,128)(2,1)S(1)} %copy-done.2, bf16[512,512]{1,0:T(8,128)(2,1)S(1)} %copy-done.4), custom_call_target="tpu_custom_call" | custom-call | flops 1000000000 | bytes 1000 | tf_op jit(solution)/shard_map/pallas_call | solution.py:381
  4.1 4.9 %collective-permute-start = (f32[1536,256]{1,0:T(8,128)S(1)}, f32[1536,256]{1,0:T(8,128)S(1)}, u32[]{:S(2)}, u32[]{:S(2)}) collective-permute-start(f32[1536,256]{1,0:T(8,128)S(1)} %get-tuple-element.21.refs_3_.refs_1_.refs_2_), channel_id=1, source_target_pairs={{0,2},{4,6},{8,10},{12,14},{16,18},{20,22},{24,26},{28,30}} | collective-permute-start | bytes 4718600 | tf_op jit(solution)/shard_map/ppermute | solution.py:428
  9.0 3.4 %collective-permute-start.1 = (f32[1024,256]{1,0:T(8,128)}, f32[1024,256]{1,0:T(8,128)}, u32[]{:S(2)}, u32[]{:S(2)}) collective-permute-start(f32[1024,256]{1,0:T(8,128)} %get-tuple-element.25), channel_id=1, source_target_pairs={{0,4},{4,0},{8,12},{12,8},{16,20},{20,16},{24,28},{28,24}} | collective-permute-start | bytes 3145736 | tf_op jit(solution)/shard_map/ppermute | solution.py:428
  12.5 0.6 shard_map.131.refs_2_
  13.2 0.7 copy-done.6
  13.9 4.9 %all-to-all-start = ((f32[8,72,128]{2,1,0:T(8,128)}), f32[8,72,128]{2,1,0:T(8,128)S(1)}, u32[]{:S(2)}, u32[]{:S(2)}) async-start(f32[8,72,128]{2,1,0:T(8,128)} %bitcast.9), calls=%async_computation | async-start | bytes 589824 | tf_op jit(solution)/shard_map/all_to_all | solution.py:457
  18.8 0.1 stack.23.refs_0_
  18.9 1.0 %copy-done.7 = f32[576,128]{1,0:T(8,128)S(1)} copy-done((f32[576,128]{1,0:T(8,128)S(1)}, f32[576,128]{1,0:T(8,128)}, u32[]{:S(2)}) %copy-start.7) | copy-done | bytes 294936
  19.9 0.9 %shard_map.132.refs_7_.refs_8_.refs_1_ = bf16[4,512,512]{2,1,0:T(8,128)(2,1)S(1)} custom-call(s32[5]{0:T(128)S(1)} %stack.23.refs_0_, s32[4,2048]{1,0:T(4,128)S(1)} %copy-done.14, f32[576,128]{1,0:T(8,128)S(1)} %copy-done.7), custom_call_target="tpu_custom_call" | custom-call | flops 1000000000 | bytes 1000 | tf_op jit(solution)/shard_map/pallas_call | solution.py:381
  20.9 1.8 %shard_map.133 = (f32[2,128,128]{2,1,0:T(8,128)S(1)}, f32[8,128]{1,0:T(8,128)S(1)}, f32[2,128,128]{2,1,0:T(8,128)S(1)}) custom-call(s32[5]{0:T(128)S(1)} %stack.23.refs_0_, f32[2,128,128]{2,1,0:T(8,128)S(1)} %copy-done.12, f32[2,128,128]{2,1,0:T(8,128)S(1)} %copy-done.13, s32[2,128]{1,0:T(2,128)S(1)} %copy-done.17, f32[2,128]{1,0:T(2,128)S(1)} %copy-done.18, ...), custom_call_target="tpu_custom_call" | custom-call | flops 1000000000 | bytes 1000 | tf_op jit(solution)/shard_map/pallas_call | solution.py:381
  22.7 1.3 %copy-done = bf16[4,512,512]{2,1,0:T(8,128)(2,1)} copy-done((bf16[4,512,512]{2,1,0:T(8,128)(2,1)}, bf16[4,512,512]{2,1,0:T(8,128)(2,1)S(1)}, u32[]{:S(2)}) %copy-start) | copy-done | bytes 2097176
  24.0 0.7 copy-done.8
  24.7 0.7 copy-done.20
  25.3 3.8 %all-to-all-done.refs_5_.refs_0_ = f32[8,72,128]{2,1,0:T(8,128)S(1)} async-done(((f32[8,72,128]{2,1,0:T(8,128)}), f32[8,72,128]{2,1,0:T(8,128)S(1)}, u32[]{:S(2)}, u32[]{:S(2)}) %all-to-all-start) | async-done | bytes 294944 | tf_op jit(solution)/shard_map/all_to_all | solution.py:457
  29.1 0.9 %copy-done.9 = f32[2,128,128]{2,1,0:T(8,128)S(1)} copy-done((f32[2,128,128]{2,1,0:T(8,128)S(1)}, f32[2,128,128]{2,1,0:T(8,128)}, u32[]{:S(2)}) %copy-start.9) | copy-done | bytes 131096
  30.0 1.5 %shard_map.134 = (f32[1792,256]{1,0:T(8,128)S(1)}, f32[512,256]{1,0:T(8,128)S(1)}) custom-call(s32[5]{0:T(128)S(1)} %stack.23.refs_0_, f32[1536,256]{1,0:T(8,128)S(1)} %get-tuple-element.21.refs_3_.refs_1_.refs_2_, f32[1536,256]{1,0:T(8,128)S(1)} %collective-permute-done.refs_2_.refs_3_, f32[1024,256]{1,0:T(8,128)} %collective-permute-done.1.refs_3_.refs_4_, ...), custom_call_target="tpu_custom_call" | custom-call | flops 1000000000 | bytes 1000 | tf_op jit(solution)/shard_map/pallas_call | solution.py:381
  31.5 1.4 %collective-permute-start.2 = (f32[1792,256]{1,0:T(8,128)S(1)}, f32[1792,256]{1,0:T(8,128)S(1)}, u32[]{:S(2)}, u32[]{:S(2)}) collective-permute-start(f32[1792,256]{1,0:T(8,128)S(1)} %get-tuple-element.26.refs_4_.refs_3_), channel_id=1, source_target_pairs={{0,1},{2,3},{4,5},{6,7},{8,9},{10,11},{12,13},{14,15},{16,17},{18,... | collective-permute-start | bytes 5505032 | tf_op jit(solution)/shard_map/ppermute | solution.py:428
  32.9 1.5 %collective-permute-start.3 = (f32[512,256]{1,0:T(8,128)S(1)}, f32[512,256]{1,0:T(8,128)S(1)}, u32[]{:S(2)}, u32[]{:S(2)}) collective-permute-start(f32[512,256]{1,0:T(8,128)S(1)} %get-tuple-element.28), channel_id=1, source_target_pairs={{0,3},{2,6},{4,7},{6,2},{8,11},{10,14},{12,15},{14,10},{16,19},{18... | collective-permute-start | bytes 1572872 | tf_op jit(solution)/shard_map/ppermute | solution.py:428
  34.4 0.6 shard_map.137.refs_1_
  35.0 1.6 %collective-permute-start.4 = (f32[512,256]{1,0:T(8,128)S(1)}, f32[512,256]{1,0:T(8,128)S(1)}, u32[]{:S(2)}, u32[]{:S(2)}) collective-permute-start(f32[512,256]{1,0:T(8,128)S(1)} %shard_map.137.refs_1_), channel_id=1, source_target_pairs={{0,8},{1,9},{2,10},{3,11},{4,12},{5,13},{6,14},{7,15},{8,0},{9,1},... | collective-permute-start | bytes 1572872 | tf_op jit(solution)/shard_map/ppermute | solution.py:428
  36.6 1.6 %shard_map.135 = (f32[2,128,128]{2,1,0:T(8,128)}, f32[2,136,128]{2,1,0:T(8,128)S(1)}) custom-call(f32[8,72,128]{2,1,0:T(8,128)S(1)} %all-to-all-done.refs_5_.refs_0_, f32[2,128,128]{2,1,0:T(8,128)S(1)} %copy-done.10, f32[8,128]{1,0:T(8,128)S(1)} %get-tuple-element.23.refs_2_, f32[2,128,128]{2,1,0:T(8,128)S(1)} %copy-done.21, ...), custom_call_target="tpu_custom_call" | custom-call | flops 1000000000 | bytes 1000 | tf_op jit(solution)/shard_map/pallas_call | solution.py:381
  38.2 0.5 collective-permute-start.5
  38.7 2.4 %collective-permute-done.3.refs_6_ = f32[512,256]{1,0:T(8,128)S(1)} collective-permute-done((f32[512,256]{1,0:T(8,128)S(1)}, f32[512,256]{1,0:T(8,128)S(1)}, u32[]{:S(2)}, u32[]{:S(2)}) %collective-permute-start.3) | collective-permute-done | bytes 524320 | tf_op jit(solution)/shard_map/ppermute | solution.py:428
  41.0 3.7 %shard_map.136 = (f32[512,256]{1,0:T(8,128)S(1)}, f32[512,256]{1,0:T(8,128)S(1)}, f32[3,128,128]{2,1,0:T(8,128)S(1)}, f32[512,512]{1,0:T(8,128)S(1)}) custom-call(s32[5]{0:T(128)S(1)} %stack.23.refs_0_, bf16[1024,512]{1,0:T(8,128)(2,1)S(1)} %copy-done.3, f32[1536,256]{1,0:T(8,128)S(1)} %get-tuple-element.21.refs_3_.refs_1_.refs_2_, ...), custom_call_target="tpu_custom_call" | custom-call | flops 30000001024 | bytes 1000 | tf_op jit(solution)/shard_map/pallas_call | solution.py:381
  44.8 1.0 %collective-permute-done.5.refs_1_ = f32[1,2,136,128]{3,2,1,0:T(8,128)S(1)} collective-permute-done((f32[1,2,136,128]{3,2,1,0:T(8,128)S(1)}, f32[1,2,136,128]{3,2,1,0:T(8,128)S(1)}, u32[]{:S(2)}, u32[]{:S(2)}) %collective-permute-start.5) | collective-permute-done | bytes 139296 | tf_op jit(solution)/shard_map/ppermute | solution.py:428
  45.8 0.7 shard_map.139.refs_1_
  46.4 0.1 collective-permute-start.6
  46.5 1.6 %collective-permute-start.9 = (f32[2,2,136,128]{3,2,1,0:T(8,128)S(1)}, f32[2,2,136,128]{3,2,1,0:T(8,128)S(1)}, u32[]{:S(2)}, u32[]{:S(2)}) collective-permute-start(f32[2,2,136,128]{3,2,1,0:T(8,128)S(1)} %shard_map.138.refs_3_.refs_0_.refs_1_), channel_id=1, source_target_pairs={{0,4},{1,5},{2,6},{3,7},{4,0},{5,1},{6,2},{7,3},{8,12},{9,13},{10,... | collective-permute-start | bytes 835592 | tf_op jit(solution)/shard_map/ppermute | solution.py:428
  48.1 1.6 %collective-permute-start.7 = (f32[512,512]{1,0:T(8,128)S(1)}, f32[512,512]{1,0:T(8,128)S(1)}, u32[]{:S(2)}, u32[]{:S(2)}) collective-permute-start(f32[512,512]{1,0:T(8,128)S(1)} %get-tuple-element.33.refs_2_), channel_id=1, source_target_pairs={{0,8},{1,9},{2,10},{3,11},{4,12},{5,13},{6,14},{7,15},{8,0},{9,1},... | collective-permute-start | bytes 3145736 | tf_op jit(solution)/shard_map/ppermute | solution.py:428
  49.7 2.4 %collective-permute-start.11 = (f32[2,2,136,128]{3,2,1,0:T(8,128)S(1)}, f32[2,2,136,128]{3,2,1,0:T(8,128)S(1)}, u32[]{:S(2)}, u32[]{:S(2)}) collective-permute-start(f32[2,2,136,128]{3,2,1,0:T(8,128)S(1)} %shard_map.138.refs_3_.refs_0_.refs_1_), channel_id=1, source_target_pairs={{0,2},{1,3},{2,0},{3,1},{4,6},{5,7},{6,4},{7,5},{8,10},{9,11},{10,... | collective-permute-start | bytes 835592 | tf_op jit(solution)/shard_map/ppermute | solution.py:428
  52.1 0.7 shard_map.140
  52.8 0.6 collective-permute-start.8
  53.3 2.7 %shard_map.141 = (f32[256,256]{1,0:T(8,128)}, f32[512,512]{1,0:T(8,128)S(1)}) custom-call(s32[5]{0:T(128)S(1)} %stack.23.refs_0_, bf16[1024,512]{1,0:T(8,128)(2,1)S(1)} %copy-done.3, f32[1536,256]{1,0:T(8,128)S(1)} %get-tuple-element.21.refs_3_.refs_1_.refs_2_, f32[1536,256]{1,0:T(8,128)S(1)} %collective-permute-done.refs_2_.refs_3_, ...), custom_call_target="tpu_custom_call" | custom-call | flops 1000000000 | bytes 1000 | tf_op jit(solution)/shard_map/pallas_call | solution.py:381
  56.1 2.4 %collective-permute-start.10 = (f32[2,2,136,128]{3,2,1,0:T(8,128)S(1)}, f32[2,2,136,128]{3,2,1,0:T(8,128)S(1)}, u32[]{:S(2)}, u32[]{:S(2)}) collective-permute-start(f32[2,2,136,128]{3,2,1,0:T(8,128)S(1)} %shard_map.142.refs_3_), channel_id=1, source_target_pairs={{0,2},{1,3},{2,0},{3,1},{4,6},{5,7},{6,4},{7,5},{8,10},{9,11},{10,... | collective-permute-start | bytes 835592 | tf_op jit(solution)/shard_map/ppermute | solution.py:428
  58.5 0.4 collective-permute-done.11.refs_1_.refs_2_
  58.9 0.1 shard_map.143.refs_5_
  59.0 0.1 collective-permute-start.12
  59.0 3.3 %shard_map.144.refs_2_ = f32[512,512]{1,0:T(8,128)S(1)} custom-call(s32[5]{0:T(128)S(1)} %stack.23.refs_0_, f32[2,2,136,128]{3,2,1,0:T(8,128)S(1)} %shard_map.138.refs_3_.refs_0_.refs_1_, f32[2,2,136,128]{3,2,1,0:T(8,128)S(1)} %collective-permute-done.11.refs_1_.refs_2_, f32[2,2,136,128]{3,2,1,0:T(8,128)S(1)} %collective-permute-done.9.refs_0_.refs_2_.refs_3_, ...), custom_call_target="tpu_custom_call" | custom-call | flops 30000001024 | bytes 1000 | tf_op jit(solution)/shard_map/pallas_call | solution.py:381
  62.3 3.3 %shard_map.145.refs_1_.refs_2_ = f32[512,512]{1,0:T(8,128)S(1)} custom-call(s32[5]{0:T(128)S(1)} %stack.23.refs_0_, f32[6,2,136,128]{3,2,1,0:T(8,128)S(1)} %collective-permute-done.12.refs_1_, f32[512,512]{1,0:T(8,128)S(1)} %shard_map.144.refs_2_), custom_call_target="tpu_custom_call" | custom-call | flops 1000000000 | bytes 1000 | tf_op jit(solution)/shard_map/pallas_call | solution.py:381
  65.6 0.6 collective-permute-start.14
  66.2 1.6 %shard_map.147.refs_1_.refs_2_ = f32[512,512]{1,0:T(8,128)S(1)} custom-call(s32[5]{0:T(128)S(1)} %stack.23.refs_0_, f32[2,2,136,128]{3,2,1,0:T(8,128)S(1)} %collective-permute-done.10.refs_0_.refs_1_, f32[512,512]{1,0:T(8,128)S(1)} %shard_map.145.refs_1_.refs_2_, f32[2,2,136,128]{3,2,1,0:T(8,128)S(1)} %shard_map.146.refs_3_), custom_call_target="tpu_custom_call" | custom-call | flops 30000001024 | bytes 1000 | tf_op jit(solution)/shard_map/pallas_call | solution.py:381
  67.8 0.1 collective-permute-start.13
  67.9 1.6 %shard_map.149.refs_7_ = f32[512,512]{1,0:T(8,128)S(1)} custom-call(s32[5]{0:T(128)S(1)} %stack.23.refs_0_, f32[2,2,136,128]{3,2,1,0:T(8,128)S(1)} %collective-permute-done.14.refs_1_, f32[512,512]{1,0:T(8,128)S(1)} %shard_map.147.refs_1_.refs_2_, f32[256,256]{1,0:T(8,128)S(1)} %shard_map.148.refs_3_), custom_call_target="tpu_custom_call" | custom-call | flops 1000000000 | bytes 1000 | tf_op jit(solution)/shard_map/pallas_call | solution.py:381
  69.5 2.9 %shard_map.150.refs_2_ = f32[512,512]{1,0:T(8,128)S(1)} custom-call(s32[5]{0:T(128)S(1)} %stack.23.refs_0_, bf16[512,512]{1,0:T(8,128)(2,1)S(1)} %copy-done.5, f32[512,256]{1,0:T(8,128)S(1)} %get-tuple-element.36.refs_2_, f32[512,256]{1,0:T(8,128)S(1)} %get-tuple-element.34.refs_9_.refs_3_, f32[256,256]{1,0:T(8,128)S(1)} %get-tuple-element.37.refs_4_, ...), custom_call_target="tpu_custom_call" | custom-call | flops 1000000000 | bytes 1000 | tf_op jit(solution)/shard_map/pallas_call | solution.py:381
  72.4 0.9 %collective-permute-done.7.refs_0_ = f32[512,512]{1,0:T(8,128)S(1)} collective-permute-done((f32[512,512]{1,0:T(8,128)S(1)}, f32[512,512]{1,0:T(8,128)S(1)}, u32[]{:S(2)}, u32[]{:S(2)}) %collective-permute-start.7) | collective-permute-done | bytes 1048608 | tf_op jit(solution)/shard_map/ppermute | solution.py:428
  73.3 2.2 %shard_map.151 = f32[512,512]{1,0:T(8,128)} custom-call(f32[512,512]{1,0:T(8,128)S(1)} %collective-permute-done.7.refs_0_, bf16[4,512,512]{2,1,0:T(8,128)(2,1)S(1)} %copy-done.1, f32[512,512]{1,0:T(8,128)S(1)} %shard_map.150.refs_2_), custom_call_target="tpu_custom_call" | custom-call | flops 1000000000 | bytes 1000 | tf_op jit(solution)/shard_map/pallas_call | solution.py:381
  (51 shorter events, 0.2 us)
Async XLA Ops:
  0.6 1.2 %copy-start.2 = (bf16[1024,512]{1,0:T(8,128)(2,1)S(1)}, bf16[1024,512]{1,0:T(8,128)(2,1)}, u32[]{:S(2)}) copy-start(bf16[1024,512]{1,0:T(8,128)(2,1)} %refs_1_.10) | copy-start | bytes 3145732
  1.9 1.0 %copy-start.4 = (bf16[512,512]{1,0:T(8,128)(2,1)S(1)}, bf16[512,512]{1,0:T(8,128)(2,1)}, u32[]{:S(2)}) copy-start(bf16[512,512]{1,0:T(8,128)(2,1)} %refs_1_.11) | copy-start | bytes 1572868
  2.9 9.6 %copy-start.11 = (f32[1,256,128]{2,1,0:T(8,128)S(1)}, f32[1,256,128]{2,1,0:T(8,128)}, u32[]{:S(2)}) copy-start(f32[1,256,128]{2,1,0:T(8,128)} %param.11) | copy-start | bytes 393220
  2.9 9.6 %copy-start.15 = (s32[1,256,1]{1,2,0:T(1,128)S(1)}, s32[1,256,1]{1,2,0:T(1,128)}, u32[]{:S(2)}) copy-start(s32[1,256,1]{1,2,0:T(1,128)} %param.12) | copy-start | bytes 3076
  2.9 9.6 %copy-start.16 = (s32[1,256]{1,0:T(1,128)S(1)}, s32[1,256]{1,0:T(1,128)}, u32[]{:S(2)}) copy-start(s32[1,256]{1,0:T(1,128)} %refs_2_.2) | copy-start | bytes 3076
  4.1 25.0 %collective-permute-start = (f32[1536,256]{1,0:T(8,128)S(1)}, f32[1536,256]{1,0:T(8,128)S(1)}, u32[]{:S(2)}, u32[]{:S(2)}) collective-permute-start(f32[1536,256]{1,0:T(8,128)S(1)} %get-tuple-element.21.refs_3_.refs_1_.refs_2_), channel_id=1, source_target_pairs={{0,2},{4,6},{8,10},{12,14},{16,18},{20,22},{24,26},{28,30}} | collective-permute-start | bytes 4718600 | tf_op jit(solution)/shard_map/ppermute | solution.py:428
  9.0 20.1 %collective-permute-start.1 = (f32[1024,256]{1,0:T(8,128)}, f32[1024,256]{1,0:T(8,128)}, u32[]{:S(2)}, u32[]{:S(2)}) collective-permute-start(f32[1024,256]{1,0:T(8,128)} %get-tuple-element.25), channel_id=1, source_target_pairs={{0,4},{4,0},{8,12},{12,8},{16,20},{20,16},{24,28},{28,24}} | collective-permute-start | bytes 3145736 | tf_op jit(solution)/shard_map/ppermute | solution.py:428
  12.5 6.4 %copy-start.14 = (s32[4,2048]{1,0:T(4,128)S(1)}, s32[4,2048]{1,0:T(4,128)}, u32[]{:S(2)}) copy-start(s32[4,2048]{1,0:T(4,128)} %refs_6_.1) | copy-start | bytes 98308
  13.2 0.7 copy-start.6
  13.9 15.2 %all-to-all-start = ((f32[8,72,128]{2,1,0:T(8,128)}), f32[8,72,128]{2,1,0:T(8,128)S(1)}, u32[]{:S(2)}, u32[]{:S(2)}) async-start(f32[8,72,128]{2,1,0:T(8,128)} %bitcast.9), calls=%async_computation | async-start | bytes 589824 | tf_op jit(solution)/shard_map/all_to_all | solution.py:457
  18.9 1.0 %copy-start.7 = (f32[576,128]{1,0:T(8,128)S(1)}, f32[576,128]{1,0:T(8,128)}, u32[]{:S(2)}) copy-start(f32[576,128]{1,0:T(8,128)} %copy-done.6) | copy-start | bytes 884740
  19.8 1.0 %copy-start.12 = (f32[2,128,128]{2,1,0:T(8,128)S(1)}, f32[2,128,128]{2,1,0:T(8,128)}, u32[]{:S(2)}) copy-start(f32[2,128,128]{2,1,0:T(8,128)} %refs_1_.8) | copy-start | bytes 393220
  19.8 1.0 %copy-start.13 = (f32[2,128,128]{2,1,0:T(8,128)S(1)}, f32[2,128,128]{2,1,0:T(8,128)}, u32[]{:S(2)}) copy-start(f32[2,128,128]{2,1,0:T(8,128)} %refs_2_.3) | copy-start | bytes 393220
  19.8 1.0 %copy-start.17 = (s32[2,128]{1,0:T(2,128)S(1)}, s32[2,128]{1,0:T(2,128)}, u32[]{:S(2)}) copy-start(s32[2,128]{1,0:T(2,128)} %refs_3_.1) | copy-start | bytes 3076
  19.8 1.0 %copy-start.18 = (f32[2,128]{1,0:T(2,128)S(1)}, f32[2,128]{1,0:T(2,128)}, u32[]{:S(2)}) copy-start(f32[2,128]{1,0:T(2,128)} %refs_4_.1) | copy-start | bytes 3076
  19.8 1.0 %copy-start.19 = (s32[2,128]{1,0:T(2,128)S(1)}, s32[2,128]{1,0:T(2,128)}, u32[]{:S(2)}) copy-start(s32[2,128]{1,0:T(2,128)} %refs_5_.1) | copy-start | bytes 3076
  22.7 1.4 %copy-start = (bf16[4,512,512]{2,1,0:T(8,128)(2,1)}, bf16[4,512,512]{2,1,0:T(8,128)(2,1)S(1)}, u32[]{:S(2)}) copy-start(bf16[4,512,512]{2,1,0:T(8,128)(2,1)S(1)} %shard_map.132.refs_7_.refs_8_.refs_1_) | copy-start | bytes 6291460
  24.0 0.7 copy-start.8
  24.7 0.7 copy-start.20
  29.1 0.9 %copy-start.9 = (f32[2,128,128]{2,1,0:T(8,128)S(1)}, f32[2,128,128]{2,1,0:T(8,128)}, u32[]{:S(2)}) copy-start(f32[2,128,128]{2,1,0:T(8,128)} %copy-done.8) | copy-start | bytes 393220
  31.5 9.6 %collective-permute-start.2 = (f32[1792,256]{1,0:T(8,128)S(1)}, f32[1792,256]{1,0:T(8,128)S(1)}, u32[]{:S(2)}, u32[]{:S(2)}) collective-permute-start(f32[1792,256]{1,0:T(8,128)S(1)} %get-tuple-element.26.refs_4_.refs_3_), channel_id=1, source_target_pairs={{0,1},{2,3},{4,5},{6,7},{8,9},{10,11},{12,13},{14,15},{16,17},{18,... | collective-permute-start | bytes 5505032 | tf_op jit(solution)/shard_map/ppermute | solution.py:428
  32.9 3.7 %copy-start.10 = (f32[2,128,128]{2,1,0:T(8,128)S(1)}, f32[2,128,128]{2,1,0:T(8,128)}, u32[]{:S(2)}) copy-start(f32[2,128,128]{2,1,0:T(8,128)} %copy-done.8) | copy-start | bytes 393220
  32.9 3.7 %copy-start.21 = (f32[2,128,128]{2,1,0:T(8,128)S(1)}, f32[2,128,128]{2,1,0:T(8,128)}, u32[]{:S(2)}) copy-start(f32[2,128,128]{2,1,0:T(8,128)} %copy-done.20) | copy-start | bytes 393220
  32.9 8.1 %collective-permute-start.3 = (f32[512,256]{1,0:T(8,128)S(1)}, f32[512,256]{1,0:T(8,128)S(1)}, u32[]{:S(2)}, u32[]{:S(2)}) collective-permute-start(f32[512,256]{1,0:T(8,128)S(1)} %get-tuple-element.28), channel_id=1, source_target_pairs={{0,3},{2,6},{4,7},{6,2},{8,11},{10,14},{12,15},{14,10},{16,19},{18... | collective-permute-start | bytes 1572872 | tf_op jit(solution)/shard_map/ppermute | solution.py:428
  35.0 10.8 %collective-permute-start.4 = (f32[512,256]{1,0:T(8,128)S(1)}, f32[512,256]{1,0:T(8,128)S(1)}, u32[]{:S(2)}, u32[]{:S(2)}) collective-permute-start(f32[512,256]{1,0:T(8,128)S(1)} %shard_map.137.refs_1_), channel_id=1, source_target_pairs={{0,8},{1,9},{2,10},{3,11},{4,12},{5,13},{6,14},{7,15},{8,0},{9,1},... | collective-permute-start | bytes 1572872 | tf_op jit(solution)/shard_map/ppermute | solution.py:428
  36.6 4.4 %copy-start.3 = (bf16[1024,512]{1,0:T(8,128)(2,1)S(1)}, bf16[1024,512]{1,0:T(8,128)(2,1)}, u32[]{:S(2)}) copy-start(bf16[1024,512]{1,0:T(8,128)(2,1)} %refs_1_.10) | copy-start | bytes 3145732
  38.2 7.5 %collective-permute-start.5 = (f32[1,2,136,128]{3,2,1,0:T(8,128)S(1)}, f32[1,2,136,128]{3,2,1,0:T(8,128)S(1)}, u32[]{:S(2)}, u32[]{:S(2)}) collective-permute-start(f32[1,2,136,128]{3,2,1,0:T(8,128)S(1)} %bitcast.10), channel_id=1, source_target_pairs={{0,8},{1,9},{2,10},{3,11},{4,12},{5,13},{6,14},{7,15},{8,0},{9,1},... | collective-permute-start | bytes 417800 | tf_op jit(solution)/shard_map/ppermute | solution.py:428
  46.4 6.9 %copy-start.1 = (bf16[4,512,512]{2,1,0:T(8,128)(2,1)S(1)}, bf16[4,512,512]{2,1,0:T(8,128)(2,1)}, u32[]{:S(2)}) copy-start(bf16[4,512,512]{2,1,0:T(8,128)(2,1)} %copy-done) | copy-start | bytes 6291460
  46.4 5.6 %collective-permute-start.6 = (f32[1024,256]{1,0:T(8,128)S(1)}, f32[1024,256]{1,0:T(8,128)S(1)}, u32[]{:S(2)}, u32[]{:S(2)}) collective-permute-start(f32[1024,256]{1,0:T(8,128)S(1)} %shard_map.139.refs_1_), channel_id=1, source_target_pairs={{0,1},{1,0},{2,3},{3,2},{4,5},{5,4},{6,7},{7,6},{8,9},{9,8},{10,11... | collective-permute-start | bytes 3145736 | tf_op jit(solution)/shard_map/ppermute | solution.py:428
  46.5 9.6 %collective-permute-start.9 = (f32[2,2,136,128]{3,2,1,0:T(8,128)S(1)}, f32[2,2,136,128]{3,2,1,0:T(8,128)S(1)}, u32[]{:S(2)}, u32[]{:S(2)}) collective-permute-start(f32[2,2,136,128]{3,2,1,0:T(8,128)S(1)} %shard_map.138.refs_3_.refs_0_.refs_1_), channel_id=1, source_target_pairs={{0,4},{1,5},{2,6},{3,7},{4,0},{5,1},{6,2},{7,3},{8,12},{9,13},{10,... | collective-permute-start | bytes 835592 | tf_op jit(solution)/shard_map/ppermute | solution.py:428
  48.1 25.2 %collective-permute-start.7 = (f32[512,512]{1,0:T(8,128)S(1)}, f32[512,512]{1,0:T(8,128)S(1)}, u32[]{:S(2)}, u32[]{:S(2)}) collective-permute-start(f32[512,512]{1,0:T(8,128)S(1)} %get-tuple-element.33.refs_2_), channel_id=1, source_target_pairs={{0,8},{1,9},{2,10},{3,11},{4,12},{5,13},{6,14},{7,15},{8,0},{9,1},... | collective-permute-start | bytes 3145736 | tf_op jit(solution)/shard_map/ppermute | solution.py:428
  49.7 9.2 %collective-permute-start.11 = (f32[2,2,136,128]{3,2,1,0:T(8,128)S(1)}, f32[2,2,136,128]{3,2,1,0:T(8,128)S(1)}, u32[]{:S(2)}, u32[]{:S(2)}) collective-permute-start(f32[2,2,136,128]{3,2,1,0:T(8,128)S(1)} %shard_map.138.refs_3_.refs_0_.refs_1_), channel_id=1, source_target_pairs={{0,2},{1,3},{2,0},{3,1},{4,6},{5,7},{6,4},{7,5},{8,10},{9,11},{10,... | collective-permute-start | bytes 835592 | tf_op jit(solution)/shard_map/ppermute | solution.py:428
  52.8 15.0 %collective-permute-start.8 = (f32[512,256]{1,0:T(8,128)S(1)}, f32[512,256]{1,0:T(8,128)S(1)}, u32[]{:S(2)}, u32[]{:S(2)}) collective-permute-start(f32[512,256]{1,0:T(8,128)S(1)} %get-tuple-element.34.refs_9_.refs_3_), channel_id=1, source_target_pairs={{0,4},{1,5},{2,6},{3,7},{4,0},{5,1},{6,2},{7,3},{8,12},{9,13},{10,... | collective-permute-start | bytes 1572872 | tf_op jit(solution)/shard_map/ppermute | solution.py:428
  56.1 9.5 %collective-permute-start.10 = (f32[2,2,136,128]{3,2,1,0:T(8,128)S(1)}, f32[2,2,136,128]{3,2,1,0:T(8,128)S(1)}, u32[]{:S(2)}, u32[]{:S(2)}) collective-permute-start(f32[2,2,136,128]{3,2,1,0:T(8,128)S(1)} %shard_map.142.refs_3_), channel_id=1, source_target_pairs={{0,2},{1,3},{2,0},{3,1},{4,6},{5,7},{6,4},{7,5},{8,10},{9,11},{10,... | collective-permute-start | bytes 835592 | tf_op jit(solution)/shard_map/ppermute | solution.py:428
  59.0 3.4 %collective-permute-start.12 = (f32[6,2,136,128]{3,2,1,0:T(8,128)S(1)}, f32[6,2,136,128]{3,2,1,0:T(8,128)S(1)}, u32[]{:S(2)}, u32[]{:S(2)}) collective-permute-start(f32[6,2,136,128]{3,2,1,0:T(8,128)S(1)} %shard_map.143.refs_5_), channel_id=1, source_target_pairs={{0,1},{1,0},{2,3},{3,2},{4,5},{5,4},{6,7},{7,6},{8,9},{9,8},{10,11... | collective-permute-start | bytes 2506760 | tf_op jit(solution)/shard_map/ppermute | solution.py:428
  65.6 2.3 %collective-permute-start.14 = (f32[2,2,136,128]{3,2,1,0:T(8,128)S(1)}, f32[2,2,136,128]{3,2,1,0:T(8,128)S(1)}, u32[]{:S(2)}, u32[]{:S(2)}) collective-permute-start(f32[2,2,136,128]{3,2,1,0:T(8,128)S(1)} %shard_map.146.refs_3_), channel_id=1, source_target_pairs={{0,1},{1,0},{2,3},{3,2},{4,5},{5,4},{6,7},{7,6},{8,9},{9,8},{10,11... | collective-permute-start | bytes 835592 | tf_op jit(solution)/shard_map/ppermute | solution.py:428
  67.8 1.7 %copy-start.5 = (bf16[512,512]{1,0:T(8,128)(2,1)S(1)}, bf16[512,512]{1,0:T(8,128)(2,1)}, u32[]{:S(2)}) copy-start(bf16[512,512]{1,0:T(8,128)(2,1)} %refs_1_.11) | copy-start | bytes 1572868
  67.8 1.7 %collective-permute-start.13 = (f32[256,256]{1,0:T(8,128)S(1)}, f32[256,256]{1,0:T(8,128)S(1)}, u32[]{:S(2)}, u32[]{:S(2)}) collective-permute-start(f32[256,256]{1,0:T(8,128)S(1)} %shard_map.148.refs_3_), channel_id=1, source_target_pairs={{0,1},{1,0},{2,3},{3,2},{4,5},{5,4},{6,7},{7,6},{8,9},{9,8},{10,11... | collective-permute-start | bytes 786440 | tf_op jit(solution)/shard_map/ppermute | solution.py:428

commit v5 on v4

--- a/solution.py
+++ b/solution.py
@@ -75,7 +75,7 @@
     return 2.0 * current - mm3(current, mm3(block, current))
 
 
-def pack_kernel(capacity, slots, cube_count, blocks, owner, target, out):
+def pack_kernel(capacity, slots, cube_count, blocks, owner, target, out, token):
     count = blocks.shape[0]
     owners = owner[...]
     named = iota((max(cube_count, 16), count), 0) == owners
@@ -90,6 +90,7 @@
     tags = jnp.where(spots == first + capacity, target[...].astype(F32), 0.0).astype(BF16)
     lanes = onehot(iota((blocks.shape[1], count), 0) == rank)
     out[...] = values + mm(tags, lanes, NT)
+    token[...] = jnp.zeros(token.shape, F32)
 
 
 def prepare_kernel(
@@ -129,7 +130,7 @@
     copies[1].wait()
 
 
-def places_kernel(where, level_map, out):
+def places_kernel(where, level_map, out, token):
     for index, quarter in enumerate((where[3], where[2])):
         start = pl.multiple_of(quarter * QUARTER, QUARTER)
         kept = start + iota((1, QUARTER), 1) >= KU
@@ -138,6 +139,7 @@
             target = level_map[pl.ds(group, 1), pl.ds(start, QUARTER)] - start
             target = jnp.where(kept, target, -1)
             out[2 * other + index] = onehot(iota((QUARTER, QUARTER), 0) == target)
+    token[...] = jnp.zeros(token.shape, BF16)
 
 
 def leaf_kernel(capacity, slots, cube_count, got, inverse, links, coupling, factor, sent):
@@ -312,18 +314,10 @@
     return call(functools.partial(stack_kernel, len(parts)), [shape], parts, after, scalars=False)
 
 
-def cast_kernel(mid_front, top_front, both, mid_cols, mid_part, top_part, done):
-    copies = [
-        pltpu.make_async_copy(front.at[:, pl.ds(0, KU)], part, done.at[index])
-        for index, (front, part) in enumerate(((mid_front, mid_part), (top_front, top_part)))
-    ]
-    for copy in copies:
-        copy.start()
-    copies[0].wait()
+def cast_kernel(mid_part, top_part, both, mid_cols):
     values = mid_part[...].astype(F32)
     mid_cols[...] = values
     both[0:HALF, :] = values
-    copies[1].wait()
     both[HALF:, :] = top_part[...].astype(F32)
 
 
@@ -435,21 +429,15 @@
     both, mid_cols = call(
         cast_kernel,
         [(HALF + QUARTER, KU), (HALF, KU)],
-        [mid_front, top_front],
+        [mid_front[:, 0:KU], top_front[:, 0:KU]],
         scalars=False,
-        scratch=[
-            pltpu.VMEM((HALF, KU), BF16),
-            pltpu.VMEM((QUARTER, KU), BF16),
-            pltpu.SemaphoreType.DMA((2,)),
-        ],
-        far=(0, 1),
     )
     both_x = move(both, lambda y, z, f: (y, z, 2) if f == 0 else None)
     mid_y = move(mid_cols, lambda y, z, f: (1 - y, z, 0) if f == 0 else None)
 
-    packed = call(
+    packed, packed_token = call(
         functools.partial(pack_kernel, capacity, slots, cube_count),
-        [(cube_count * slots, width)],
+        [(cube_count * slots, width), (8, width)],
         [blocks, kkt_owner.reshape(1, block_count), kkt_target.reshape(1, block_count)],
         [both],
         scalars=False,
@@ -458,25 +446,29 @@
         packed.reshape(cube_count, slots, width), "cube", split_axis=0, concat_axis=0, tiled=True
     )
 
-    places = call(
-        places_kernel, [(4, QUARTER, QUARTER)], [where, level_map], [packed], kind=BF16
-    )
     leaves = leaf_pivot.shape[0]
     size = leaf_pivot.shape[2]
     inverse, links, coupling = call(
         prepare_kernel,
         [(leaves, size, size), (8, size), leaf_coupling.shape],
         [where, leaf_pivot, leaf_coupling, pivot_signs, perturb, leaf_map, level_map],
-        [places],
+        [packed_token],
         scratch=[pltpu.VMEM(leaf_pivot.shape, F32), pltpu.SemaphoreType.DMA((2,))],
         far=(1, 2),
+    )
+    places, places_token = call(
+        places_kernel,
+        [(4, QUARTER, QUARTER), (16, PIV)],
+        [where, level_map],
+        [links],
+        kind=BF16,
     )
 
     to_core, to_cross = call(
         relay_kernel,
         [(HALF + QUARTER + KU, KU), (QUARTER, KU)],
         [where, both, both_x, mid_y],
-        [inverse, got],
+        [places_token, got],
     )
     mid_cross = move(to_cross, lambda y, z, f: {0: (y, z, 3), 2: (1 - y, z, 2)}.get(f))
     mid_core = move(to_core, lambda y, z, f: (y, z, f + 1) if f % 2 == 0 else None)

time: 76.1 us -> 74.9 us (0.984)
  waiting for transfers between devices: 8.4 us -> 7.59 us
    unnamed x44 -> x36, local copies, waits for them, and re-layouts: 7.58 us -> 5.26 us
    slice x0 -> x2, local copies, waits for them, and re-layouts: none -> 2.05 us  [the longest x1 1.08 us: local(): mid_front[:, 0:KU]]
    all_to_all x1, waiting for transfers between devices: 3.76 us -> 2.95 us  [local(): lax.all_to_all(packed.reshape(cube_count, slots, width), 'cube', split_ax...]
where the time goes in v5:
time: 74.9 us; the launch traced here: 74.4 us
  Pallas kernels  30.9 us (41%)
  starting transfers between devices  27.5 us (37%)
  waiting for transfers between devices  7.59 us (10%)
  local copies, waits for them, and re-layouts  7.39 us (10%)
  between operations  1.04 us (1%)
    pallas_call x22, Pallas kernels, call(): pl.pallas_call(kernel, out_shape=shapes[0] if single else shapes, in_spec...  30.9 us
    ppermute x15, starting transfers between devices, move(): return lax.ppermute(array, AXES, pairs)  22.6 us
    unnamed x36, local copies, waits for them, and re-layouts  5.26 us
    all_to_all x1, starting transfers between devices, local(): lax.all_to_all(packed.reshape(cube_count, slots, width), 'cube', split_ax...  4.87 us
    ppermute x15, waiting for transfers between devices, move(): return lax.ppermute(array, AXES, pairs)  4.64 us
    all_to_all x1, waiting for transfers between devices, local(): lax.all_to_all(packed.reshape(cube_count, slots, width), 'cube', split_ax...  2.95 us
  transfers between devices with their start and end apart: 16, of which 5 were waited for; matrix products, arithmetic and copies ran while one was open for 0% of the time, Pallas kernels for 34%

profile of v5, /device:TPU:0, one launch (start us, length us, event | category | flops | bytes accessed | tf_op | source)
XLA Modules:
  0.0 74.4 jit_solution(1245889274603783688)
XLA Ops:
  0.6 1.1 %slice.6.refs_0_ = bf16[1024,256]{1,0:T(8,128)(2,1)S(1)} slice(bf16[1024,512]{1,0:T(8,128)(2,1)} %refs_1_.8), slice={[0:1024], [0:256]} | slice | bytes 1048576 | tf_op jit(solution)/shard_map/slice | solution.py:432
  1.7 1.0 %slice.7.refs_1_ = bf16[512,256]{1,0:T(8,128)(2,1)S(1)} slice(bf16[512,512]{1,0:T(8,128)(2,1)} %refs_1_.9), slice={[0:512], [0:256]} | slice | bytes 524288 | tf_op jit(solution)/shard_map/slice | solution.py:432
  2.7 1.1 %shard_map.130 = (f32[1536,256]{1,0:T(8,128)S(1)}, f32[1024,256]{1,0:T(8,128)}) custom-call(bf16[1024,256]{1,0:T(8,128)(2,1)S(1)} %slice.6.refs_0_, bf16[512,256]{1,0:T(8,128)(2,1)S(1)} %slice.7.refs_1_), custom_call_target="tpu_custom_call" | custom-call | flops 1000000000 | bytes 1000 | tf_op jit(solution)/shard_map/pallas_call | solution.py:375
  3.8 4.9 %collective-permute-start = (f32[1536,256]{1,0:T(8,128)S(1)}, f32[1536,256]{1,0:T(8,128)S(1)}, u32[]{:S(2)}, u32[]{:S(2)}) collective-permute-start(f32[1536,256]{1,0:T(8,128)S(1)} %get-tuple-element.25.refs_3_.refs_1_.refs_2_), channel_id=1, source_target_pairs={{0,2},{4,6},{8,10},{12,14},{16,18},{20,22},{24,26},{28,30}} | collective-permute-start | bytes 4718600 | tf_op jit(solution)/shard_map/ppermute | solution.py:422
  8.8 3.4 %collective-permute-start.1 = (f32[1024,256]{1,0:T(8,128)}, f32[1024,256]{1,0:T(8,128)}, u32[]{:S(2)}, u32[]{:S(2)}) collective-permute-start(f32[1024,256]{1,0:T(8,128)} %get-tuple-element.31), channel_id=1, source_target_pairs={{0,4},{4,0},{8,12},{12,8},{16,20},{20,16},{24,28},{28,24}} | collective-permute-start | bytes 3145736 | tf_op jit(solution)/shard_map/ppermute | solution.py:422
  12.3 0.6 shard_map.131
  12.9 0.7 copy-done.4
  13.6 4.9 %all-to-all-start = ((f32[8,72,128]{2,1,0:T(8,128)}), f32[8,72,128]{2,1,0:T(8,128)S(1)}, u32[]{:S(2)}, u32[]{:S(2)}) async-start(f32[8,72,128]{2,1,0:T(8,128)} %bitcast.9), calls=%async_computation | async-start | bytes 589824 | tf_op jit(solution)/shard_map/all_to_all | solution.py:445
  18.5 0.1 stack.23.refs_0_
  18.6 0.9 %copy-done.6 = f32[2,128,128]{2,1,0:T(8,128)S(1)} copy-done((f32[2,128,128]{2,1,0:T(8,128)S(1)}, f32[2,128,128]{2,1,0:T(8,128)}, u32[]{:S(2)}) %copy-start.6) | copy-done | bytes 131096
  19.5 0.9 %copy-done.7 = f32[2,128,128]{2,1,0:T(8,128)S(1)} copy-done((f32[2,128,128]{2,1,0:T(8,128)S(1)}, f32[2,128,128]{2,1,0:T(8,128)}, u32[]{:S(2)}) %copy-start.7) | copy-done | bytes 131096
  20.4 1.8 %shard_map.132 = (f32[2,128,128]{2,1,0:T(8,128)S(1)}, f32[8,128]{1,0:T(8,128)S(1)}, f32[2,128,128]{2,1,0:T(8,128)S(1)}) custom-call(s32[5]{0:T(128)S(1)} %stack.23.refs_0_, f32[2,128,128]{2,1,0:T(8,128)S(1)} %copy-done.6, f32[2,128,128]{2,1,0:T(8,128)S(1)} %copy-done.7, s32[2,128]{1,0:T(2,128)S(1)} %copy-done.11, f32[2,128]{1,0:T(2,128)S(1)} %copy-done.12, ...), custom_call_target="tpu_custom_call" | custom-call | flops 1000000000 | bytes 1000 | tf_op jit(solution)/shard_map/pallas_call | solution.py:375
  22.3 0.6 copy-done.14
  22.9 0.7 copy-done.16
  23.6 0.9 %shard_map.133 = (bf16[4,512,512]{2,1,0:T(8,128)(2,1)S(1)}, bf16[16,128]{1,0:T(8,128)(2,1)S(1)}) custom-call(s32[5]{0:T(128)S(1)} %stack.23.refs_0_, s32[4,2048]{1,0:T(4,128)S(1)} %copy-done.8, f32[8,128]{1,0:T(8,128)S(1)} %get-tuple-element.29.refs_2_), custom_call_target="tpu_custom_call" | custom-call | flops 1000000000 | bytes 1000 | tf_op jit(solution)/shard_map/pallas_call | solution.py:375
  24.5 1.4 %copy-done = bf16[4,512,512]{2,1,0:T(8,128)(2,1)} copy-done((bf16[4,512,512]{2,1,0:T(8,128)(2,1)}, bf16[4,512,512]{2,1,0:T(8,128)(2,1)S(1)}, u32[]{:S(2)}) %copy-start) | copy-done | bytes 2097176
  25.9 2.9 %all-to-all-done.refs_5_.refs_0_ = f32[8,72,128]{2,1,0:T(8,128)S(1)} async-done(((f32[8,72,128]{2,1,0:T(8,128)}), f32[8,72,128]{2,1,0:T(8,128)S(1)}, u32[]{:S(2)}, u32[]{:S(2)}) %all-to-all-start) | async-done | bytes 294944 | tf_op jit(solution)/shard_map/all_to_all | solution.py:445
  28.8 1.5 %shard_map.134 = (f32[1792,256]{1,0:T(8,128)S(1)}, f32[512,256]{1,0:T(8,128)S(1)}) custom-call(s32[5]{0:T(128)S(1)} %stack.23.refs_0_, f32[1536,256]{1,0:T(8,128)S(1)} %get-tuple-element.25.refs_3_.refs_1_.refs_2_, f32[1536,256]{1,0:T(8,128)S(1)} %collective-permute-done.refs_2_.refs_3_, f32[1024,256]{1,0:T(8,128)} %collective-permute-done.1.refs_3_.refs_4_, ...), custom_call_target="tpu_custom_call" | custom-call | flops 1000000000 | bytes 1000 | tf_op jit(solution)/shard_map/pallas_call | solution.py:375
  30.3 1.4 %collective-permute-start.2 = (f32[1792,256]{1,0:T(8,128)S(1)}, f32[1792,256]{1,0:T(8,128)S(1)}, u32[]{:S(2)}, u32[]{:S(2)}) collective-permute-start(f32[1792,256]{1,0:T(8,128)S(1)} %get-tuple-element.33.refs_4_.refs_3_), channel_id=1, source_target_pairs={{0,1},{2,3},{4,5},{6,7},{8,9},{10,11},{12,13},{14,15},{16,17},{18,... | collective-permute-start | bytes 5505032 | tf_op jit(solution)/shard_map/ppermute | solution.py:422
  31.8 1.5 %collective-permute-start.3 = (f32[512,256]{1,0:T(8,128)S(1)}, f32[512,256]{1,0:T(8,128)S(1)}, u32[]{:S(2)}, u32[]{:S(2)}) collective-permute-start(f32[512,256]{1,0:T(8,128)S(1)} %get-tuple-element.35), channel_id=1, source_target_pairs={{0,3},{2,6},{4,7},{6,2},{8,11},{10,14},{12,15},{14,10},{16,19},{18... | collective-permute-start | bytes 1572872 | tf_op jit(solution)/shard_map/ppermute | solution.py:422
  33.2 0.6 shard_map.137.refs_1_
  33.8 1.6 %collective-permute-start.4 = (f32[512,256]{1,0:T(8,128)S(1)}, f32[512,256]{1,0:T(8,128)S(1)}, u32[]{:S(2)}, u32[]{:S(2)}) collective-permute-start(f32[512,256]{1,0:T(8,128)S(1)} %shard_map.137.refs_1_), channel_id=1, source_target_pairs={{0,8},{1,9},{2,10},{3,11},{4,12},{5,13},{6,14},{7,15},{8,0},{9,1},... | collective-permute-start | bytes 1572872 | tf_op jit(solution)/shard_map/ppermute | solution.py:422
  35.5 1.6 %shard_map.135 = (f32[2,128,128]{2,1,0:T(8,128)}, f32[2,136,128]{2,1,0:T(8,128)S(1)}) custom-call(f32[8,72,128]{2,1,0:T(8,128)S(1)} %all-to-all-done.refs_5_.refs_0_, f32[2,128,128]{2,1,0:T(8,128)S(1)} %copy-done.15, f32[8,128]{1,0:T(8,128)S(1)} %get-tuple-element.29.refs_2_, f32[2,128,128]{2,1,0:T(8,128)S(1)} %copy-done.17, ...), custom_call_target="tpu_custom_call" | custom-call | flops 1000000000 | bytes 1000 | tf_op jit(solution)/shard_map/pallas_call | solution.py:375
  37.0 0.5 collective-permute-start.5
  37.5 2.4 %collective-permute-done.3.refs_6_ = f32[512,256]{1,0:T(8,128)S(1)} collective-permute-done((f32[512,256]{1,0:T(8,128)S(1)}, f32[512,256]{1,0:T(8,128)S(1)}, u32[]{:S(2)}, u32[]{:S(2)}) %collective-permute-start.3) | collective-permute-done | bytes 524320 | tf_op jit(solution)/shard_map/ppermute | solution.py:422
  39.9 3.7 %shard_map.136 = (f32[512,256]{1,0:T(8,128)S(1)}, f32[512,256]{1,0:T(8,128)S(1)}, f32[3,128,128]{2,1,0:T(8,128)S(1)}, f32[512,512]{1,0:T(8,128)S(1)}) custom-call(s32[5]{0:T(128)S(1)} %stack.23.refs_0_, bf16[1024,512]{1,0:T(8,128)(2,1)S(1)} %copy-done.2, f32[1536,256]{1,0:T(8,128)S(1)} %get-tuple-element.25.refs_3_.refs_1_.refs_2_, ...), custom_call_target="tpu_custom_call" | custom-call | flops 30000001024 | bytes 1000 | tf_op jit(solution)/shard_map/pallas_call | solution.py:375
  43.6 1.0 %collective-permute-done.5.refs_1_ = f32[1,2,136,128]{3,2,1,0:T(8,128)S(1)} collective-permute-done((f32[1,2,136,128]{3,2,1,0:T(8,128)S(1)}, f32[1,2,136,128]{3,2,1,0:T(8,128)S(1)}, u32[]{:S(2)}, u32[]{:S(2)}) %collective-permute-start.5) | collective-permute-done | bytes 139296 | tf_op jit(solution)/shard_map/ppermute | solution.py:422
  44.6 0.7 shard_map.139.refs_1_
  45.3 0.1 collective-permute-start.6
  45.3 1.6 %collective-permute-start.9 = (f32[2,2,136,128]{3,2,1,0:T(8,128)S(1)}, f32[2,2,136,128]{3,2,1,0:T(8,128)S(1)}, u32[]{:S(2)}, u32[]{:S(2)}) collective-permute-start(f32[2,2,136,128]{3,2,1,0:T(8,128)S(1)} %shard_map.138.refs_3_.refs_0_.refs_1_), channel_id=1, source_target_pairs={{0,4},{1,5},{2,6},{3,7},{4,0},{5,1},{6,2},{7,3},{8,12},{9,13},{10,... | collective-permute-start | bytes 835592 | tf_op jit(solution)/shard_map/ppermute | solution.py:422
  46.9 1.6 %collective-permute-start.7 = (f32[512,512]{1,0:T(8,128)S(1)}, f32[512,512]{1,0:T(8,128)S(1)}, u32[]{:S(2)}, u32[]{:S(2)}) collective-permute-start(f32[512,512]{1,0:T(8,128)S(1)} %get-tuple-element.41.refs_2_), channel_id=1, source_target_pairs={{0,8},{1,9},{2,10},{3,11},{4,12},{5,13},{6,14},{7,15},{8,0},{9,1},... | collective-permute-start | bytes 3145736 | tf_op jit(solution)/shard_map/ppermute | solution.py:422
  48.5 2.4 %collective-permute-start.11 = (f32[2,2,136,128]{3,2,1,0:T(8,128)S(1)}, f32[2,2,136,128]{3,2,1,0:T(8,128)S(1)}, u32[]{:S(2)}, u32[]{:S(2)}) collective-permute-start(f32[2,2,136,128]{3,2,1,0:T(8,128)S(1)} %shard_map.138.refs_3_.refs_0_.refs_1_), channel_id=1, source_target_pairs={{0,2},{1,3},{2,0},{3,1},{4,6},{5,7},{6,4},{7,5},{8,10},{9,11},{10,... | collective-permute-start | bytes 835592 | tf_op jit(solution)/shard_map/ppermute | solution.py:422
  50.9 0.7 shard_map.140
  51.6 0.6 collective-permute-start.8
  52.2 2.7 %shard_map.141 = (f32[256,256]{1,0:T(8,128)}, f32[512,512]{1,0:T(8,128)S(1)}) custom-call(s32[5]{0:T(128)S(1)} %stack.23.refs_0_, bf16[1024,512]{1,0:T(8,128)(2,1)S(1)} %copy-done.2, f32[1536,256]{1,0:T(8,128)S(1)} %get-tuple-element.25.refs_3_.refs_1_.refs_2_, f32[1536,256]{1,0:T(8,128)S(1)} %collective-permute-done.refs_2_.refs_3_, ...), custom_call_target="tpu_custom_call" | custom-call | flops 1000000000 | bytes 1000 | tf_op jit(solution)/shard_map/pallas_call | solution.py:375
  54.9 2.4 %collective-permute-start.10 = (f32[2,2,136,128]{3,2,1,0:T(8,128)S(1)}, f32[2,2,136,128]{3,2,1,0:T(8,128)S(1)}, u32[]{:S(2)}, u32[]{:S(2)}) collective-permute-start(f32[2,2,136,128]{3,2,1,0:T(8,128)S(1)} %shard_map.142.refs_3_), channel_id=1, source_target_pairs={{0,2},{1,3},{2,0},{3,1},{4,6},{5,7},{6,4},{7,5},{8,10},{9,11},{10,... | collective-permute-start | bytes 835592 | tf_op jit(solution)/shard_map/ppermute | solution.py:422
  57.3 0.4 collective-permute-done.11.refs_1_.refs_2_
  57.7 0.1 shard_map.143.refs_5_
  57.8 0.1 collective-permute-start.12
  57.8 3.3 %shard_map.144.refs_2_ = f32[512,512]{1,0:T(8,128)S(1)} custom-call(s32[5]{0:T(128)S(1)} %stack.23.refs_0_, f32[2,2,136,128]{3,2,1,0:T(8,128)S(1)} %shard_map.138.refs_3_.refs_0_.refs_1_, f32[2,2,136,128]{3,2,1,0:T(8,128)S(1)} %collective-permute-done.11.refs_1_.refs_2_, f32[2,2,136,128]{3,2,1,0:T(8,128)S(1)} %collective-permute-done.9.refs_0_.refs_2_.refs_3_, ...), custom_call_target="tpu_custom_call" | custom-call | flops 30000001024 | bytes 1000 | tf_op jit(solution)/shard_map/pallas_call | solution.py:375
  61.1 3.3 %shard_map.145.refs_1_.refs_2_ = f32[512,512]{1,0:T(8,128)S(1)} custom-call(s32[5]{0:T(128)S(1)} %stack.23.refs_0_, f32[6,2,136,128]{3,2,1,0:T(8,128)S(1)} %collective-permute-done.12.refs_1_, f32[512,512]{1,0:T(8,128)S(1)} %shard_map.144.refs_2_), custom_call_target="tpu_custom_call" | custom-call | flops 1000000000 | bytes 1000 | tf_op jit(solution)/shard_map/pallas_call | solution.py:375
  64.4 0.6 collective-permute-start.14
  65.0 1.6 %shard_map.147.refs_1_.refs_2_ = f32[512,512]{1,0:T(8,128)S(1)} custom-call(s32[5]{0:T(128)S(1)} %stack.23.refs_0_, f32[2,2,136,128]{3,2,1,0:T(8,128)S(1)} %collective-permute-done.10.refs_0_.refs_1_, f32[512,512]{1,0:T(8,128)S(1)} %shard_map.145.refs_1_.refs_2_, f32[2,2,136,128]{3,2,1,0:T(8,128)S(1)} %shard_map.146.refs_3_), custom_call_target="tpu_custom_call" | custom-call | flops 30000001024 | bytes 1000 | tf_op jit(solution)/shard_map/pallas_call | solution.py:375
  66.6 0.1 collective-permute-start.13
  66.7 1.6 %shard_map.149.refs_7_ = f32[512,512]{1,0:T(8,128)S(1)} custom-call(s32[5]{0:T(128)S(1)} %stack.23.refs_0_, f32[2,2,136,128]{3,2,1,0:T(8,128)S(1)} %collective-permute-done.14.refs_1_, f32[512,512]{1,0:T(8,128)S(1)} %shard_map.147.refs_1_.refs_2_, f32[256,256]{1,0:T(8,128)S(1)} %shard_map.148.refs_3_), custom_call_target="tpu_custom_call" | custom-call | flops 1000000000 | bytes 1000 | tf_op jit(solution)/shard_map/pallas_call | solution.py:375
  68.4 2.9 %shard_map.150.refs_2_ = f32[512,512]{1,0:T(8,128)S(1)} custom-call(s32[5]{0:T(128)S(1)} %stack.23.refs_0_, bf16[512,512]{1,0:T(8,128)(2,1)S(1)} %copy-done.3, f32[512,256]{1,0:T(8,128)S(1)} %get-tuple-element.44.refs_2_, f32[512,256]{1,0:T(8,128)S(1)} %get-tuple-element.42.refs_9_.refs_3_, f32[256,256]{1,0:T(8,128)S(1)} %get-tuple-element.45.refs_4_, ...), custom_call_target="tpu_custom_call" | custom-call | flops 1000000000 | bytes 1000 | tf_op jit(solution)/shard_map/pallas_call | solution.py:375
  71.3 0.9 %collective-permute-done.7.refs_0_ = f32[512,512]{1,0:T(8,128)S(1)} collective-permute-done((f32[512,512]{1,0:T(8,128)S(1)}, f32[512,512]{1,0:T(8,128)S(1)}, u32[]{:S(2)}, u32[]{:S(2)}) %collective-permute-start.7) | collective-permute-done | bytes 1048608 | tf_op jit(solution)/shard_map/ppermute | solution.py:422
  72.2 2.2 %shard_map.151 = f32[512,512]{1,0:T(8,128)} custom-call(f32[512,512]{1,0:T(8,128)S(1)} %collective-permute-done.7.refs_0_, bf16[4,512,512]{2,1,0:T(8,128)(2,1)S(1)} %copy-done.1, f32[512,512]{1,0:T(8,128)S(1)} %shard_map.150.refs_2_), custom_call_target="tpu_custom_call" | custom-call | flops 1000000000 | bytes 1000 | tf_op jit(solution)/shard_map/pallas_call | solution.py:375
  (45 shorter events, 0.2 us)
Async XLA Ops:
  2.7 9.5 %copy-start.5 = (f32[1,256,128]{2,1,0:T(8,128)S(1)}, f32[1,256,128]{2,1,0:T(8,128)}, u32[]{:S(2)}) copy-start(f32[1,256,128]{2,1,0:T(8,128)} %param.11) | copy-start | bytes 393220
  2.7 9.5 %copy-start.9 = (s32[1,256,1]{1,2,0:T(1,128)S(1)}, s32[1,256,1]{1,2,0:T(1,128)}, u32[]{:S(2)}) copy-start(s32[1,256,1]{1,2,0:T(1,128)} %param.12) | copy-start | bytes 3076
  2.7 9.5 %copy-start.10 = (s32[1,256]{1,0:T(1,128)S(1)}, s32[1,256]{1,0:T(1,128)}, u32[]{:S(2)}) copy-start(s32[1,256]{1,0:T(1,128)} %refs_2_.2) | copy-start | bytes 3076
  3.8 25.0 %collective-permute-start = (f32[1536,256]{1,0:T(8,128)S(1)}, f32[1536,256]{1,0:T(8,128)S(1)}, u32[]{:S(2)}, u32[]{:S(2)}) collective-permute-start(f32[1536,256]{1,0:T(8,128)S(1)} %get-tuple-element.25.refs_3_.refs_1_.refs_2_), channel_id=1, source_target_pairs={{0,2},{4,6},{8,10},{12,14},{16,18},{20,22},{24,26},{28,30}} | collective-permute-start | bytes 4718600 | tf_op jit(solution)/shard_map/ppermute | solution.py:422
  8.8 20.1 %collective-permute-start.1 = (f32[1024,256]{1,0:T(8,128)}, f32[1024,256]{1,0:T(8,128)}, u32[]{:S(2)}, u32[]{:S(2)}) collective-permute-start(f32[1024,256]{1,0:T(8,128)} %get-tuple-element.31), channel_id=1, source_target_pairs={{0,4},{4,0},{8,12},{12,8},{16,20},{20,16},{24,28},{28,24}} | collective-permute-start | bytes 3145736 | tf_op jit(solution)/shard_map/ppermute | solution.py:422
  12.2 6.4 %copy-start.8 = (s32[4,2048]{1,0:T(4,128)S(1)}, s32[4,2048]{1,0:T(4,128)}, u32[]{:S(2)}) copy-start(s32[4,2048]{1,0:T(4,128)} %refs_1_.6) | copy-start | bytes 98308
  12.2 6.4 %copy-start.11 = (s32[2,128]{1,0:T(2,128)S(1)}, s32[2,128]{1,0:T(2,128)}, u32[]{:S(2)}) copy-start(s32[2,128]{1,0:T(2,128)} %refs_3_.1) | copy-start | bytes 3076
  12.3 6.4 %copy-start.12 = (f32[2,128]{1,0:T(2,128)S(1)}, f32[2,128]{1,0:T(2,128)}, u32[]{:S(2)}) copy-start(f32[2,128]{1,0:T(2,128)} %refs_4_.1) | copy-start | bytes 3076
  12.3 6.3 %copy-start.13 = (s32[2,128]{1,0:T(2,128)S(1)}, s32[2,128]{1,0:T(2,128)}, u32[]{:S(2)}) copy-start(s32[2,128]{1,0:T(2,128)} %refs_5_.1) | copy-start | bytes 3076
  12.9 0.7 copy-start.4
  13.6 15.2 %all-to-all-start = ((f32[8,72,128]{2,1,0:T(8,128)}), f32[8,72,128]{2,1,0:T(8,128)S(1)}, u32[]{:S(2)}, u32[]{:S(2)}) async-start(f32[8,72,128]{2,1,0:T(8,128)} %bitcast.9), calls=%async_computation | async-start | bytes 589824 | tf_op jit(solution)/shard_map/all_to_all | solution.py:445
  18.6 0.9 %copy-start.6 = (f32[2,128,128]{2,1,0:T(8,128)S(1)}, f32[2,128,128]{2,1,0:T(8,128)}, u32[]{:S(2)}) copy-start(f32[2,128,128]{2,1,0:T(8,128)} %refs_1_.5) | copy-start | bytes 393220
  19.5 0.9 %copy-start.7 = (f32[2,128,128]{2,1,0:T(8,128)S(1)}, f32[2,128,128]{2,1,0:T(8,128)}, u32[]{:S(2)}) copy-start(f32[2,128,128]{2,1,0:T(8,128)} %refs_2_.3) | copy-start | bytes 393220
  22.3 0.7 copy-start.14
  22.9 0.7 copy-start.16
  24.5 1.4 %copy-start = (bf16[4,512,512]{2,1,0:T(8,128)(2,1)}, bf16[4,512,512]{2,1,0:T(8,128)(2,1)S(1)}, u32[]{:S(2)}) copy-start(bf16[4,512,512]{2,1,0:T(8,128)(2,1)S(1)} %get-tuple-element.40.refs_8_.refs_1_) | copy-start | bytes 6291460
  30.3 9.6 %collective-permute-start.2 = (f32[1792,256]{1,0:T(8,128)S(1)}, f32[1792,256]{1,0:T(8,128)S(1)}, u32[]{:S(2)}, u32[]{:S(2)}) collective-permute-start(f32[1792,256]{1,0:T(8,128)S(1)} %get-tuple-element.33.refs_4_.refs_3_), channel_id=1, source_target_pairs={{0,1},{2,3},{4,5},{6,7},{8,9},{10,11},{12,13},{14,15},{16,17},{18,... | collective-permute-start | bytes 5505032 | tf_op jit(solution)/shard_map/ppermute | solution.py:422
  31.7 3.7 %copy-start.15 = (f32[2,128,128]{2,1,0:T(8,128)S(1)}, f32[2,128,128]{2,1,0:T(8,128)}, u32[]{:S(2)}) copy-start(f32[2,128,128]{2,1,0:T(8,128)} %copy-done.14) | copy-start | bytes 393220
  31.7 3.7 %copy-start.17 = (f32[2,128,128]{2,1,0:T(8,128)S(1)}, f32[2,128,128]{2,1,0:T(8,128)}, u32[]{:S(2)}) copy-start(f32[2,128,128]{2,1,0:T(8,128)} %copy-done.16) | copy-start | bytes 393220
  31.8 8.1 %collective-permute-start.3 = (f32[512,256]{1,0:T(8,128)S(1)}, f32[512,256]{1,0:T(8,128)S(1)}, u32[]{:S(2)}, u32[]{:S(2)}) collective-permute-start(f32[512,256]{1,0:T(8,128)S(1)} %get-tuple-element.35), channel_id=1, source_target_pairs={{0,3},{2,6},{4,7},{6,2},{8,11},{10,14},{12,15},{14,10},{16,19},{18... | collective-permute-start | bytes 1572872 | tf_op jit(solution)/shard_map/ppermute | solution.py:422
  33.8 10.8 %collective-permute-start.4 = (f32[512,256]{1,0:T(8,128)S(1)}, f32[512,256]{1,0:T(8,128)S(1)}, u32[]{:S(2)}, u32[]{:S(2)}) collective-permute-start(f32[512,256]{1,0:T(8,128)S(1)} %shard_map.137.refs_1_), channel_id=1, source_target_pairs={{0,8},{1,9},{2,10},{3,11},{4,12},{5,13},{6,14},{7,15},{8,0},{9,1},... | collective-permute-start | bytes 1572872 | tf_op jit(solution)/shard_map/ppermute | solution.py:422
  35.5 4.4 %copy-start.2 = (bf16[1024,512]{1,0:T(8,128)(2,1)S(1)}, bf16[1024,512]{1,0:T(8,128)(2,1)}, u32[]{:S(2)}) copy-start(bf16[1024,512]{1,0:T(8,128)(2,1)} %refs_1_.8) | copy-start | bytes 3145732
  37.0 7.5 %collective-permute-start.5 = (f32[1,2,136,128]{3,2,1,0:T(8,128)S(1)}, f32[1,2,136,128]{3,2,1,0:T(8,128)S(1)}, u32[]{:S(2)}, u32[]{:S(2)}) collective-permute-start(f32[1,2,136,128]{3,2,1,0:T(8,128)S(1)} %bitcast.10), channel_id=1, source_target_pairs={{0,8},{1,9},{2,10},{3,11},{4,12},{5,13},{6,14},{7,15},{8,0},{9,1},... | collective-permute-start | bytes 417800 | tf_op jit(solution)/shard_map/ppermute | solution.py:422
  45.3 6.9 %copy-start.1 = (bf16[4,512,512]{2,1,0:T(8,128)(2,1)S(1)}, bf16[4,512,512]{2,1,0:T(8,128)(2,1)}, u32[]{:S(2)}) copy-start(bf16[4,512,512]{2,1,0:T(8,128)(2,1)} %copy-done) | copy-start | bytes 6291460
  45.3 5.6 %collective-permute-start.6 = (f32[1024,256]{1,0:T(8,128)S(1)}, f32[1024,256]{1,0:T(8,128)S(1)}, u32[]{:S(2)}, u32[]{:S(2)}) collective-permute-start(f32[1024,256]{1,0:T(8,128)S(1)} %shard_map.139.refs_1_), channel_id=1, source_target_pairs={{0,1},{1,0},{2,3},{3,2},{4,5},{5,4},{6,7},{7,6},{8,9},{9,8},{10,11... | collective-permute-start | bytes 3145736 | tf_op jit(solution)/shard_map/ppermute | solution.py:422
  45.3 9.6 %collective-permute-start.9 = (f32[2,2,136,128]{3,2,1,0:T(8,128)S(1)}, f32[2,2,136,128]{3,2,1,0:T(8,128)S(1)}, u32[]{:S(2)}, u32[]{:S(2)}) collective-permute-start(f32[2,2,136,128]{3,2,1,0:T(8,128)S(1)} %shard_map.138.refs_3_.refs_0_.refs_1_), channel_id=1, source_target_pairs={{0,4},{1,5},{2,6},{3,7},{4,0},{5,1},{6,2},{7,3},{8,12},{9,13},{10,... | collective-permute-start | bytes 835592 | tf_op jit(solution)/shard_map/ppermute | solution.py:422
  46.9 25.2 %collective-permute-start.7 = (f32[512,512]{1,0:T(8,128)S(1)}, f32[512,512]{1,0:T(8,128)S(1)}, u32[]{:S(2)}, u32[]{:S(2)}) collective-permute-start(f32[512,512]{1,0:T(8,128)S(1)} %get-tuple-element.41.refs_2_), channel_id=1, source_target_pairs={{0,8},{1,9},{2,10},{3,11},{4,12},{5,13},{6,14},{7,15},{8,0},{9,1},... | collective-permute-start | bytes 3145736 | tf_op jit(solution)/shard_map/ppermute | solution.py:422
  48.5 9.2 %collective-permute-start.11 = (f32[2,2,136,128]{3,2,1,0:T(8,128)S(1)}, f32[2,2,136,128]{3,2,1,0:T(8,128)S(1)}, u32[]{:S(2)}, u32[]{:S(2)}) collective-permute-start(f32[2,2,136,128]{3,2,1,0:T(8,128)S(1)} %shard_map.138.refs_3_.refs_0_.refs_1_), channel_id=1, source_target_pairs={{0,2},{1,3},{2,0},{3,1},{4,6},{5,7},{6,4},{7,5},{8,10},{9,11},{10,... | collective-permute-start | bytes 835592 | tf_op jit(solution)/shard_map/ppermute | solution.py:422
  51.6 15.0 %collective-permute-start.8 = (f32[512,256]{1,0:T(8,128)S(1)}, f32[512,256]{1,0:T(8,128)S(1)}, u32[]{:S(2)}, u32[]{:S(2)}) collective-permute-start(f32[512,256]{1,0:T(8,128)S(1)} %get-tuple-element.42.refs_9_.refs_3_), channel_id=1, source_target_pairs={{0,4},{1,5},{2,6},{3,7},{4,0},{5,1},{6,2},{7,3},{8,12},{9,13},{10,... | collective-permute-start | bytes 1572872 | tf_op jit(solution)/shard_map/ppermute | solution.py:422
  54.9 9.5 %collective-permute-start.10 = (f32[2,2,136,128]{3,2,1,0:T(8,128)S(1)}, f32[2,2,136,128]{3,2,1,0:T(8,128)S(1)}, u32[]{:S(2)}, u32[]{:S(2)}) collective-permute-start(f32[2,2,136,128]{3,2,1,0:T(8,128)S(1)} %shard_map.142.refs_3_), channel_id=1, source_target_pairs={{0,2},{1,3},{2,0},{3,1},{4,6},{5,7},{6,4},{7,5},{8,10},{9,11},{10,... | collective-permute-start | bytes 835592 | tf_op jit(solution)/shard_map/ppermute | solution.py:422
  57.8 3.4 %collective-permute-start.12 = (f32[6,2,136,128]{3,2,1,0:T(8,128)S(1)}, f32[6,2,136,128]{3,2,1,0:T(8,128)S(1)}, u32[]{:S(2)}, u32[]{:S(2)}) collective-permute-start(f32[6,2,136,128]{3,2,1,0:T(8,128)S(1)} %shard_map.143.refs_5_), channel_id=1, source_target_pairs={{0,1},{1,0},{2,3},{3,2},{4,5},{5,4},{6,7},{7,6},{8,9},{9,8},{10,11... | collective-permute-start | bytes 2506760 | tf_op jit(solution)/shard_map/ppermute | solution.py:422
  64.4 2.3 %collective-permute-start.14 = (f32[2,2,136,128]{3,2,1,0:T(8,128)S(1)}, f32[2,2,136,128]{3,2,1,0:T(8,128)S(1)}, u32[]{:S(2)}, u32[]{:S(2)}) collective-permute-start(f32[2,2,136,128]{3,2,1,0:T(8,128)S(1)} %shard_map.146.refs_3_), channel_id=1, source_target_pairs={{0,1},{1,0},{2,3},{3,2},{4,5},{5,4},{6,7},{7,6},{8,9},{9,8},{10,11... | collective-permute-start | bytes 835592 | tf_op jit(solution)/shard_map/ppermute | solution.py:422
  66.6 1.7 %copy-start.3 = (bf16[512,512]{1,0:T(8,128)(2,1)S(1)}, bf16[512,512]{1,0:T(8,128)(2,1)}, u32[]{:S(2)}) copy-start(bf16[512,512]{1,0:T(8,128)(2,1)} %refs_1_.9) | copy-start | bytes 1572868
  66.6 1.7 %collective-permute-start.13 = (f32[256,256]{1,0:T(8,128)S(1)}, f32[256,256]{1,0:T(8,128)S(1)}, u32[]{:S(2)}, u32[]{:S(2)}) collective-permute-start(f32[256,256]{1,0:T(8,128)S(1)} %shard_map.148.refs_3_), channel_id=1, source_target_pairs={{0,1},{1,0},{2,3},{3,2},{4,5},{5,4},{6,7},{7,6},{8,9},{9,8},{10,11... | collective-permute-start | bytes 786440 | tf_op jit(solution)/shard_map/ppermute | solution.py:422
